TPU v7x, 256 devices: a whole 4x4x8 slice. The times are simulated.
256 devices in a mesh: gx: 4 (over y), gy: 8 (over z_lo, core), gz: 8 (over z_hi, x).
Axes of the slice: x: 4, y: 4, z: 8 (z_hi: 2, z_lo: 4; z = z_hi * 4 + z_lo), core: 2. Of those that a mesh axis runs over, the one named last changes fastest.
Arguments:
- density: float32 [3, 3, 3, 8, 16, 1024], P(None, None, None, 'gx', 'gy', 'gz'), may hold values from 0.5 to 2
- energy: float32 [3, 3, 3, 8, 16, 1024], P(None, None, None, 'gx', 'gy', 'gz'), may hold values from 0.2 to 10
- velocity: float32 [3, 16, 32, 2048], P(None, 'gx', 'gy', 'gz'), may hold values from -3 to 3
Outputs:
- new_velocity: float32 [3, 16, 32, 2048], P(None, 'gx', 'gy', 'gz')
- remapped: float32 [5, 3, 3, 3, 8, 16, 1024], P(None, None, None, None, 'gx', 'gy', 'gz')
All inputs are finite; a program needn't handle non-finite values.
Results may differ from a plain program's by a relative error of at most 0.00002.
Values sent between devices are 32-bit elements; how exact they have to be, the bound alone decides.
No kernel may reach another device: no remote copies, remote signals or barrier semaphores. Data moves between devices by JAX's collectives and lax.ppermute only.
A program may use at most 128 MiB of HBM per device.

v0:
```python
import functools
import math

import jax
import jax.numpy as jnp
from jax import lax
from jax.experimental import pallas as pl
from jax.experimental.pallas import tpu as pltpu
from jax.sharding import PartitionSpec as P

GAMMA = 1.4
CFL = 0.1
F32 = jnp.float32
TILE = (8, 128)
GROUP = 14


def tables():
    root = math.sqrt(0.6)
    points = [0.5 - 0.5 * root, 0.5, 0.5 + 0.5 * root]
    weights = [5.0 / 18.0, 8.0 / 18.0, 5.0 / 18.0]

    def bernstein(t):
        return [(1.0 - t) * (1.0 - t), 2.0 * t * (1.0 - t), t * t]

    def bern_slope(t):
        return [-2.0 * (1.0 - t), 2.0 - 4.0 * t, 2.0 * t]

    def lagrange(a, t):
        result = 1.0
        for m in range(3):
            if m != a:
                result = result * (t - points[m]) / (points[a] - points[m])
        return result

    def lagrange_slope(a, t):
        result = 0.0
        for k in range(3):
            if k != a:
                factor = 1.0 / (points[a] - points[k])
                for m in range(3):
                    if m != a and m != k:
                        factor = factor * (t - points[m]) / (points[a] - points[m])
                result = result + factor
        return result

    return {
        "eval_b": [[bernstein(points[q])[a] for q in range(3)] for a in range(3)],
        "force_b": [[weights[q] * bernstein(points[q])[a] for a in range(3)] for q in range(3)],
        "force_d": [[weights[q] * bern_slope(points[q])[a] for a in range(3)] for q in range(3)],
        "volume": [
            [weights[q] * lagrange_slope(a, points[q]) / weights[a] for a in range(3)]
            for q in range(3)
        ],
        "low_trace": [lagrange(a, 0.0) for a in range(3)],
        "high_trace": [lagrange(a, 1.0) for a in range(3)],
        "low_lift": [lagrange(a, 0.0) / weights[a] for a in range(3)],
        "high_lift": [lagrange(a, 1.0) / weights[a] for a in range(3)],
    }


TAB = tables()


def row_index():
    return lax.broadcasted_iota(jnp.int32, TILE, 0)


def lane_index():
    return lax.broadcasted_iota(jnp.int32, TILE, 1)


def roll_rows(x, by):
    return pltpu.roll(x, by % 8, 0)


def roll_lanes(x, by):
    by = by % 128
    return x if by == 0 else pltpu.roll(x, by, 1)


class Shifts:
    def __init__(self):
        row = row_index()
        lane = lane_index()
        self.first = {2: (row & 2) == 0, 1: (row & 1) == 0}
        self.top = lane == 127
        self.bottom = lane == 0

    def pack_low(self, a, b, step):
        return a if b is None else jnp.where(self.first[step], a, roll_rows(b, step))

    def pack_high(self, a, b, step):
        return a if b is None else jnp.where(self.first[step], roll_rows(b, -step), a)

    def prev(self, own, packed, second, step):
        outside = packed if second else roll_rows(packed, -step)
        return jnp.where(self.first[step], outside, roll_rows(own, step))

    def next(self, own, packed, second, step):
        outside = packed if second else roll_rows(packed, step)
        return jnp.where(self.first[step], roll_rows(own, -step), outside)

    def z_prev(self, x):
        t = roll_lanes(x, 1)
        return jnp.where(self.bottom, roll_rows(t, 4), t)

    def z_next(self, x):
        t = roll_lanes(x, -1)
        return jnp.where(self.top, roll_rows(t, 4), t)


def combine(values, coefs):
    total = None
    for value, coef in zip(values, coefs):
        if coef == 0.0:
            continue
        term = coef * value
        total = term if total is None else total + term
    return total


def column(matrix, j):
    return [matrix[i][j] for i in range(3)]


def contract(source, matrix, position):
    result = {}
    for key in source:
        if key[position] == 0:
            keys = [key[:position] + (m,) + key[position + 1 :] for m in range(3)]
            for j in range(3):
                result[keys[j]] = combine([source[k] for k in keys], column(matrix, j))
    return result


POINTS = [(a, b, c) for a in range(3) for b in range(3) for c in range(3)]


def point(a, b, c):
    return 9 * a + 3 * b + c


def pack_kernel(dens, ener, vel, to_up, to_down, both, nodes, top, wide, split):
    lane = lane_index()
    low = ener[0, 0]
    for q in range(27):
        for i in range(2):
            both[q, 2 * i : 2 * i + 2, :] = dens[q, i]
            both[q, 4 + 2 * i : 6 + 2 * i, :] = ener[q, i]
            low = jnp.maximum(low, ener[q, i])
    top[...] = jnp.broadcast_to(jnp.max(low, keepdims=True), TILE)
    half = (2 * lane) % 128
    for d in range(3):
        for px in range(2):
            slot = 2 * d + px
            wide[slot, 0:4, :] = vel[d, px]
            wide[slot, 4:8, :] = vel[d, 2 + px]
            left = wide[slot, :, 0:128]
            right = wide[slot, :, 128:256]
            for pz in range(2):
                picked = jnp.where(
                    lane < 64,
                    jnp.take_along_axis(left, half + pz, axis=1),
                    jnp.take_along_axis(right, half + pz, axis=1),
                )
                split[slot, 8 * pz : 8 * pz + 8, :] = picked
            for py in range(2):
                nodes[2 * slot + py] = split[slot, pl.ds(py, 8, stride=2), :]
    sources = [[both[q] for q in range(GROUP)], [both[q] for q in range(GROUP, 27)]]
    sources.append([nodes[n] for n in range(12)])
    for t in range(3):
        up = jnp.ones(TILE, F32)
        down = jnp.ones(TILE, F32)
        for g, tile in enumerate(sources[t]):
            group = lane // 4
            up = jnp.where(group == 2 * g, roll_lanes(tile, 8 * g - 124), up)
            down = jnp.where(group == 2 * g + 1, roll_lanes(tile, 8 * g + 4), down)
        to_up[t] = up
        to_down[t] = down


def force_kernel(both, nodes, from_below, from_above, rho, vz, parts, to_right, to_left):
    sh = Shifts()
    row = row_index()
    own = row < 4
    lane = lane_index()
    merged = [jnp.where((lane & 7) < 4, from_below[t], from_above[t]) for t in range(3)]

    def extend(tile, t, g):
        halo = roll_lanes(merged[t], 124 - 8 * g)
        return (
            jnp.where(own, tile, roll_rows(halo, 4)),
            jnp.where(own, roll_rows(tile, 4), halo),
        )

    density = {}
    pressure = {}
    for key in POINTS:
        q = point(*key)
        dens, ener = extend(both[q], q // GROUP, q % GROUP)
        rho[0, q] = dens
        heat = dens * ener
        rho[1, q] = heat
        density[key] = dens
        pressure[key] = (GAMMA - 1.0) * heat
    for n in range(12):
        even, odd = extend(nodes[n], 2, n)
        vz[2 * n] = even
        vz[2 * n + 1] = odd
    fb = TAB["force_b"]
    fd = TAB["force_d"]
    along_b = contract(pressure, fb, 0)
    along_d = contract(pressure, fd, 0)
    bb = contract(along_b, fb, 1)
    fields = [
        contract(contract(along_d, fb, 1), fb, 2),
        contract(contract(along_b, fd, 1), fb, 2),
        contract(bb, fd, 2),
        contract(contract(contract(density, fb, 0), fb, 1), fb, 2),
    ]
    for f in range(4):
        for a in range(3):
            for b in range(3):
                even = fields[f][a, b, 0] + sh.z_prev(fields[f][a, b, 2])
                odd = fields[f][a, b, 1]
                parts[f, 3 * a + b, 0] = even
                parts[f, 3 * a + b, 1] = odd
                if a == 2:
                    to_right[3 * f + b] = sh.pack_high(even, odd, 2)
                if a == 0:
                    to_left[3 * f + b] = sh.pack_low(even, odd, 2)
    for d in range(3):
        for py in range(2):
            n = 4 * d + py
            to_left[12 + 2 * d + py] = sh.pack_low(vz[2 * n], vz[2 * n + 1], 2)


def rim_kernel(parts, vz, from_left, from_right, sums, ev, to_up, to_down):
    sh = Shifts()
    for f in range(4):
        for b in range(3):
            for z in range(2):
                first = parts[f, b, z]
                last = parts[f, 6 + b, z]
                full = [
                    first + sh.prev(last, from_left[3 * f + b], z, 2),
                    parts[f, 3 + b, z],
                    last + sh.next(first, from_right[3 * f + b], z, 2),
                ]
                for a in range(3):
                    sums[f, 3 * a + b, z] = full[a]
        for a in range(3):
            to_up[3 * f + a] = sh.pack_high(sums[f, 3 * a + 2, 0], sums[f, 3 * a + 2, 1], 1)
            to_down[3 * f + a] = sh.pack_low(sums[f, 3 * a, 0], sums[f, 3 * a, 1], 1)
    for d in range(3):
        for py in range(2):
            for z in range(2):
                first = vz[2 * (4 * d + py) + z]
                ev[d, py, z] = first
                ev[d, 2 + py, z] = vz[2 * (4 * d + 2 + py) + z]
                ev[d, 4 + py, z] = sh.next(first, from_right[12 + 2 * d + py], z, 2)
        for a in range(3):
            to_down[12 + 3 * d + a] = sh.pack_low(ev[d, 2 * a, 0], ev[d, 2 * a, 1], 1)


def face_messages(sh, fields, f, right, left, up, down):
    low = TAB["low_trace"]
    high = TAB["high_trace"]
    for step, over, under in ((2, right, left), (1, up, down)):
        lows = []
        highs = []
        for m in range(3):
            for c in range(3):
                if step == 2:
                    line = [fields[a, m, c] for a in range(3)]
                else:
                    line = [fields[m, b, c] for b in range(3)]
                lows.append(combine(line, low))
                highs.append(combine(line, high))
        lows.append(None)
        highs.append(None)
        for n in range(5):
            over[f, n] = sh.pack_high(highs[2 * n], highs[2 * n + 1], step)
            under[f, n] = sh.pack_low(lows[2 * n], lows[2 * n + 1], step)


def velocity_kernel(
    sums, ev, from_down, from_up, tops, rho,
    new_vel, u0, disp, speeds, right, left, up, down, split, wide,
):
    sh = Shifts()
    lane = lane_index()
    top = tops[0:8]
    for n in range(1, tops.shape[0] // 8):
        top = jnp.maximum(top, tops[8 * n : 8 * n + 8])
    for by in (4, 2, 1):
        top = jnp.maximum(top, roll_rows(top, by))
    step = CFL / jnp.sqrt((GAMMA * (GAMMA - 1.0)) * top)
    vel = [{} for _ in range(3)]
    for a in range(3):
        for z in range(2):
            total = []
            for f in range(4):
                first = sums[f, 3 * a, z]
                last = sums[f, 3 * a + 2, z]
                total.append(
                    [
                        first + sh.prev(last, from_down[3 * f + a], z, 1),
                        sums[f, 3 * a + 1, z],
                        last + sh.next(first, from_up[3 * f + a], z, 1),
                    ]
                )
            scale = [step / total[3][b] for b in range(3)]
            for d in range(3):
                first = ev[d, 2 * a, z]
                old = [
                    first,
                    ev[d, 2 * a + 1, z],
                    sh.next(first, from_up[12 + 3 * d + a], z, 1),
                ]
                for b in range(3):
                    vel[d][a, b, z] = old[b] + total[d][b] * scale[b]
    for d in range(3):
        for px in range(2):
            slot = 2 * d + px
            for py in range(2):
                even = vel[d][px, py, 0]
                odd = vel[d][px, py, 1]
                tile = jnp.where(row_index() < 4, even, roll_rows(odd, 4))
                split[slot, pl.ds(py, 8, stride=2), :] = tile
            even = split[slot, 0:8, :]
            odd = split[slot, 8:16, :]
            for part in range(2):
                at = 64 * part + lane // 2
                wide[slot, :, 128 * part : 128 * part + 128] = jnp.where(
                    (lane & 1) == 0,
                    jnp.take_along_axis(even, at, axis=1),
                    jnp.take_along_axis(odd, at, axis=1),
                )
            new_vel[d, px] = wide[slot, 0:4, :]
            new_vel[d, 2 + px] = wide[slot, 4:8, :]
    eb = TAB["eval_b"]
    minus = -step

    def along_z(even, odd):
        line = [even, odd, sh.z_next(even)]
        return [combine(line, column(eb, q)) for q in range(3)]

    for a, at in ((0, 0), (2, 1)):
        for q in range(3):
            pair = [combine([vel[0][a, b, z] for b in range(3)], column(eb, q)) for z in range(2)]
            for c, value in enumerate(along_z(*pair)):
                speeds[at, 3 * q + c] = minus * value
    gauss = [{} for _ in range(3)]
    for d in range(3):
        across = {}
        for b in range(3):
            for z in range(2):
                line = [vel[d][a, b, z] for a in range(3)]
                for q in range(3):
                    across[q, b, z] = combine(line, column(eb, q))
        if d == 1:
            for b, at in ((0, 2), (2, 3)):
                for q in range(3):
                    for c, value in enumerate(along_z(across[q, b, 0], across[q, b, 1])):
                        speeds[at, 3 * q + c] = minus * value
        for qx in range(3):
            for qy in range(3):
                pair = [
                    combine([across[qx, b, z] for b in range(3)], column(eb, qy)) for z in range(2)
                ]
                if d == 2:
                    speeds[4, 3 * qx + qy] = minus * pair[0]
                for c, value in enumerate(along_z(*pair)):
                    gauss[d][qx, qy, c] = value
                    disp[d, point(qx, qy, c)] = minus * value
    for f in range(5):
        fields = {}
        for key in POINTS:
            q = point(*key)
            if f < 2:
                fields[key] = rho[f, q]
            else:
                fields[key] = rho[0, q] * gauss[f - 2][key]
            u0[f, q] = fields[key]
        face_messages(sh, fields, f, right, left, up, down)


def stage_kernel(weight, last, *refs):
    refs = list(refs)
    u0 = refs.pop(0)
    u = u0 if weight is None else refs.pop(0)
    disp, speeds, from_left, from_right, from_down, from_up = refs[:6]
    outs = refs[6:]
    sh = Shifts()
    low = TAB["low_trace"]
    high = TAB["high_trace"]
    low_lift = TAB["low_lift"]
    high_lift = TAB["high_lift"]
    volume = TAB["volume"]

    def one_field(f, carry):
        fields = {key: u[f, point(*key)] for key in POINTS}
        rate = {}
        for d in range(3):
            for m in range(3):
                for n in range(3):
                    if d == 0:
                        keys = [(a, m, n) for a in range(3)]
                    elif d == 1:
                        keys = [(m, a, n) for a in range(3)]
                    else:
                        keys = [(m, n, a) for a in range(3)]
                    at = 3 * m + n
                    line = [fields[k] for k in keys]
                    moved = [disp[d, point(*k)] * fields[k] for k in keys]
                    tm = combine(line, low)
                    tp = combine(line, high)
                    if d < 2:
                        step = 2 - d
                        under, over = ((from_left, from_right), (from_down, from_up))[d]
                        before = sh.prev(tp, under[f, at // 2], at % 2, step)
                        after = sh.next(tm, over[f, at // 2], at % 2, step)
                        s_low = speeds[2 * d, at]
                        s_high = speeds[2 * d + 1, at]
                        f_low = s_low * jnp.where(s_low > 0.0, before, tm)
                        f_high = s_high * jnp.where(s_high > 0.0, tp, after)
                    else:
                        s_low = speeds[4, at]
                        f_low = s_low * jnp.where(s_low > 0.0, sh.z_prev(tp), tm)
                        f_high = sh.z_next(f_low)
                    for a in range(3):
                        piece = combine(
                            moved + [f_low, f_high],
                            column(volume, a) + [low_lift[a], -high_lift[a]],
                        )
                        rate[keys[a]] = rate[keys[a]] + piece if d else piece
        after = {}
        for key in POINTS:
            q = point(*key)
            if weight is None:
                value = fields[key] + rate[key]
            else:
                value = (1.0 - weight) * u0[f, q] + weight * (fields[key] + rate[key])
            if last:
                outs[0][f, q, 0] = value[0:2]
                outs[0][f, q, 1] = value[2:4]
            else:
                outs[0][f, q] = value
                after[key] = value
        if not last:
            face_messages(sh, after, f, *outs[1:])
        return carry

    lax.fori_loop(0, 5, one_field, 0)


def call(kernel, outs, *args, scratch=(), name=None):
    return pl.pallas_call(
        kernel,
        out_shape=[jax.ShapeDtypeStruct(o, F32) for o in outs],
        in_specs=[pl.BlockSpec(memory_space=pltpu.VMEM)] * len(args),
        out_specs=[pl.BlockSpec(memory_space=pltpu.VMEM)] * len(outs),
        scratch_shapes=[pltpu.VMEM(s, F32) for s in scratch],
        compiler_params=pltpu.CompilerParams(vmem_limit_bytes=32 * 1024 * 1024),
        name=name,
    )(*args)


def send(value, axis, by):
    count = lax.axis_size(axis)
    return lax.ppermute(value, axis, [(i, (i + by) % count) for i in range(count)])


def exchange(right, left, up, down):
    return (
        send(right, "gx", 1),
        send(left, "gx", -1),
        send(up, "gy", 1),
        send(down, "gy", -1),
    )


def shards(density, energy, velocity):
    tile = TILE
    dens = density.reshape((27,) + density.shape[3:])
    ener = energy.reshape((27,) + energy.shape[3:])
    to_up, to_down, both, nodes, top = call(
        pack_kernel,
        [(3,) + tile, (3,) + tile, (27,) + tile, (12,) + tile, tile],
        dens, ener, velocity,
        scratch=[(6, 8, 256), (6, 16, 128)],
        name="pack",
    )
    from_below = send(to_up, "gz", 1)
    from_above = send(to_down, "gz", -1)
    tops = [top] + [send(top, "gx", k) for k in range(1, lax.axis_size("gx"))]
    top = functools.reduce(jnp.maximum, tops)
    peers = lax.axis_size("gy") * lax.axis_size("gz")
    spread = jnp.broadcast_to(top[0:1], (peers, 128))
    tops = lax.all_to_all(spread, ("gy", "gz"), 0, 0, tiled=True)
    rho, vz, parts, to_right, to_left = call(
        force_kernel,
        [(2, 27) + tile, (24,) + tile, (4, 9, 2) + tile, (12,) + tile, (18,) + tile],
        both, nodes, from_below, from_above,
        name="force",
    )
    from_left = send(to_right, "gx", 1)
    from_right = send(to_left, "gx", -1)
    sums, ev, to_up, to_down = call(
        rim_kernel,
        [(4, 9, 2) + tile, (3, 6, 2) + tile, (12,) + tile, (21,) + tile],
        parts, vz, from_left, from_right,
        name="rim",
    )
    from_down = send(to_up, "gy", 1)
    from_up = send(to_down, "gy", -1)
    faces = [(5, 5) + tile] * 4
    state = (5, 27) + tile
    new_velocity, u0, disp, speeds, *messages = call(
        velocity_kernel,
        [velocity.shape, state, (3, 27) + tile, (5, 9) + tile] + faces,
        sums, ev, from_down, from_up, tops, rho,
        scratch=[(6, 16, 128), (6, 8, 256)],
        name="velocity",
    )
    one, *messages = call(
        functools.partial(stage_kernel, None, False), [state] + faces,
        u0, disp, speeds, *exchange(*messages),
        name="stage_one",
    )
    two, *messages = call(
        functools.partial(stage_kernel, 0.25, False), [state] + faces,
        u0, one, disp, speeds, *exchange(*messages),
        name="stage_two",
    )
    (remapped,) = call(
        functools.partial(stage_kernel, 2.0 / 3.0, True), [(5, 27) + density.shape[3:]],
        u0, two, disp, speeds, *exchange(*messages),
        name="stage_three",
    )
    return new_velocity, remapped.reshape((5, 3, 3, 3) + density.shape[3:])


def solution(mesh):
    return jax.shard_map(
        shards,
        mesh=mesh,
        in_specs=(
            P(None, None, None, "gx", "gy", "gz"),
            P(None, None, None, "gx", "gy", "gz"),
            P(None, "gx", "gy", "gz"),
        ),
        out_specs=(P(None, "gx", "gy", "gz"), P(None, None, None, None, "gx", "gy", "gz")),
        check_vma=False,
    )
```

profile of v0, /device:TPU:97, one launch (start us, length us, event | category | flops | bytes accessed | tf_op | source)
XLA Modules:
  0.0 76.8 jit_solution(16352913486091989976)
XLA Ops:
  3.3 1.3 %collective-permute-start = (f32[3,8,128]{2,1,0:T(8,128)S(1)}, f32[3,8,128]{2,1,0:T(8,128)S(1)}, u32[]{:S(2)}, u32[]{:S(2)}) collective-permute-start(f32[3,8,128]{2,1,0:T(8,128)S(1)} %get-tuple-element.36), channel_id=1, source_target_pairs={{0,1},{1,2},{2,3},{3,4},{4,5},{5,6},{6,7},{7,0},{8,9},{9,10},{10,1... | collective-permute-start | bytes 36872 | tf_op jit(solution)/shard_map/ppermute | solution.py:473
  4.6 6.3 %collective-permute-start.1 = (f32[3,8,128]{2,1,0:T(8,128)S(1)}, f32[3,8,128]{2,1,0:T(8,128)S(1)}, u32[]{:S(2)}, u32[]{:S(2)}) collective-permute-start(f32[3,8,128]{2,1,0:T(8,128)S(1)} %get-tuple-element.37), channel_id=1, source_target_pairs={{0,7},{1,0},{2,1},{3,2},{4,3},{5,4},{6,5},{7,6},{8,15},{9,8},{10,9... | collective-permute-start | bytes 36872 | tf_op jit(solution)/shard_map/ppermute | solution.py:473
  10.8 2.7 %collective-permute-start.8 = (f32[8,128]{1,0:T(8,128)S(1)}, f32[8,128]{1,0:T(8,128)S(1)}, u32[]{:S(2)}, u32[]{:S(2)}) collective-permute-start(f32[8,128]{1,0:T(8,128)S(1)} %get-tuple-element.46), channel_id=1, source_target_pairs={{0,192},{64,0},{128,64},{192,128},{1,193},{65,1},{129,65},{193,129... | collective-permute-start | bytes 12296 | tf_op jit(solution)/shard_map/ppermute | solution.py:473
  15.0 1.7 %collective-permute-start.2 = (f32[12,8,128]{2,1,0:T(8,128)S(1)}, f32[12,8,128]{2,1,0:T(8,128)S(1)}, u32[]{:S(2)}, u32[]{:S(2)}) collective-permute-start(f32[12,8,128]{2,1,0:T(8,128)S(1)} %get-tuple-element.40), channel_id=1, source_target_pairs={{0,64},{64,128},{128,192},{192,0},{1,65},{65,129},{129,193},{193,1... | collective-permute-start | bytes 147464 | tf_op jit(solution)/shard_map/ppermute | solution.py:473
  17.7 1.7 %collective-permute-done.2.from_left = f32[12,8,128]{2,1,0:T(8,128)S(1)} collective-permute-done((f32[12,8,128]{2,1,0:T(8,128)S(1)}, f32[12,8,128]{2,1,0:T(8,128)S(1)}, u32[]{:S(2)}, u32[]{:S(2)}) %collective-permute-start.2) | collective-permute-done | bytes 49184 | tf_op jit(solution)/shard_map/ppermute | solution.py:473
  20.2 3.3 %collective-permute-start.5 = (f32[21,8,128]{2,1,0:T(8,128)S(1)}, f32[21,8,128]{2,1,0:T(8,128)S(1)}, u32[]{:S(2)}, u32[]{:S(2)}) collective-permute-start(f32[21,8,128]{2,1,0:T(8,128)S(1)} %get-tuple-element.45), channel_id=1, source_target_pairs={{0,56},{8,0},{16,8},{24,16},{32,24},{40,32},{48,40},{56,48},{1,57}... | collective-permute-start | bytes 258056 | tf_op jit(solution)/shard_map/ppermute | solution.py:473
  24.1 9.0 %all-to-all-start = ((f32[64,1,128]{2,1,0:T(1,128)}), f32[64,1,128]{2,1,0:T(1,128)S(1)}, u32[]{:S(2)}, u32[]{:S(2)}) async-start(f32[64,1,128]{2,1,0:T(1,128)} %broadcast_in_dim.2), calls=%async_computation | async-start | bytes 65536 | tf_op jit(solution)/shard_map/all_to_all | solution.py:502
  33.4 6.0 %all-to-all-done = f32[64,1,128]{2,1,0:T(1,128)S(1)} async-done(((f32[64,1,128]{2,1,0:T(1,128)}), f32[64,1,128]{2,1,0:T(1,128)S(1)}, u32[]{:S(2)}, u32[]{:S(2)}) %all-to-all-start) | async-done | bytes 32800 | tf_op jit(solution)/shard_map/all_to_all | solution.py:502
  40.4 1.3 %collective-permute-start.9 = (f32[5,5,8,128]{3,2,1,0:T(8,128)S(1)}, f32[5,5,8,128]{3,2,1,0:T(8,128)S(1)}, u32[]{:S(2)}, u32[]{:S(2)}) collective-permute-start(f32[5,5,8,128]{3,2,1,0:T(8,128)S(1)} %get-tuple-element.52), channel_id=1, source_target_pairs={{0,64},{64,128},{128,192},{192,0},{1,65},{65,129},{129,193},{193,1... | collective-permute-start | bytes 307208 | tf_op jit(solution)/shard_map/ppermute | solution.py:473
  41.7 1.4 %collective-permute-start.10 = (f32[5,5,8,128]{3,2,1,0:T(8,128)S(1)}, f32[5,5,8,128]{3,2,1,0:T(8,128)S(1)}, u32[]{:S(2)}, u32[]{:S(2)}) collective-permute-start(f32[5,5,8,128]{3,2,1,0:T(8,128)S(1)} %get-tuple-element.53), channel_id=1, source_target_pairs={{0,192},{64,0},{128,64},{192,128},{1,193},{65,1},{129,65},{193,129... | collective-permute-start | bytes 307208 | tf_op jit(solution)/shard_map/ppermute | solution.py:473
  43.1 3.8 %collective-permute-start.11 = (f32[5,5,8,128]{3,2,1,0:T(8,128)S(1)}, f32[5,5,8,128]{3,2,1,0:T(8,128)S(1)}, u32[]{:S(2)}, u32[]{:S(2)}) collective-permute-start(f32[5,5,8,128]{3,2,1,0:T(8,128)S(1)} %get-tuple-element.54), channel_id=1, source_target_pairs={{0,8},{8,16},{16,24},{24,32},{32,40},{40,48},{48,56},{56,0},{1,9},... | collective-permute-start | bytes 307208 | tf_op jit(solution)/shard_map/ppermute | solution.py:473
  46.9 1.9 %collective-permute-done.11.refs_5_ = f32[5,5,8,128]{3,2,1,0:T(8,128)S(1)} collective-permute-done((f32[5,5,8,128]{3,2,1,0:T(8,128)S(1)}, f32[5,5,8,128]{3,2,1,0:T(8,128)S(1)}, u32[]{:S(2)}, u32[]{:S(2)}) %collective-permute-start.11) | collective-permute-done | bytes 102432 | tf_op jit(solution)/shard_map/ppermute | solution.py:473
  48.8 3.9 %collective-permute-done.12.refs_6_ = f32[5,5,8,128]{3,2,1,0:T(8,128)S(1)} collective-permute-done((f32[5,5,8,128]{3,2,1,0:T(8,128)S(1)}, f32[5,5,8,128]{3,2,1,0:T(8,128)S(1)}, u32[]{:S(2)}, u32[]{:S(2)}) %collective-permute-start.12) | collective-permute-done | bytes 102432 | tf_op jit(solution)/shard_map/ppermute | solution.py:473
  52.7 1.2 %stage_one.1 = (f32[5,27,8,128]{3,2,1,0:T(8,128)S(1)}, f32[5,5,8,128]{3,2,1,0:T(8,128)S(1)}, f32[5,5,8,128]{3,2,1,0:T(8,128)S(1)}, f32[5,5,8,128]{3,2,1,0:T(8,128)S(1)}, f32[5,5,8,128]{3,2,1,0:T(8,128)S(1)}) custom-call(f32[5,27,8,128]{3,2,1,0:T(8,128)S(1)} %get-tuple-element.49.refs_0_, f32[3,27,8,128]{3,2,1,0:T(8,128)S(1)} %get-tuple-element.50.refs_1_.refs_2_, ...), custom_call_target="tpu_custom_call" | custom-call | tf_op jit(solution)/shard_map/stage_one/pallas_call | solution.py:460
  54.2 2.6 %collective-permute-start.14 = (f32[5,5,8,128]{3,2,1,0:T(8,128)S(1)}, f32[5,5,8,128]{3,2,1,0:T(8,128)S(1)}, u32[]{:S(2)}, u32[]{:S(2)}) collective-permute-start(f32[5,5,8,128]{3,2,1,0:T(8,128)S(1)} %get-tuple-element.58), channel_id=1, source_target_pairs={{0,192},{64,0},{128,64},{192,128},{1,193},{65,1},{129,65},{193,129... | collective-permute-start | bytes 307208 | tf_op jit(solution)/shard_map/ppermute | solution.py:473
  57.7 1.1 %collective-permute-done.13.refs_4_ = f32[5,5,8,128]{3,2,1,0:T(8,128)S(1)} collective-permute-done((f32[5,5,8,128]{3,2,1,0:T(8,128)S(1)}, f32[5,5,8,128]{3,2,1,0:T(8,128)S(1)}, u32[]{:S(2)}, u32[]{:S(2)}) %collective-permute-start.13) | collective-permute-done | bytes 102432 | tf_op jit(solution)/shard_map/ppermute | solution.py:473
  58.9 1.3 %collective-permute-done.15.refs_6_ = f32[5,5,8,128]{3,2,1,0:T(8,128)S(1)} collective-permute-done((f32[5,5,8,128]{3,2,1,0:T(8,128)S(1)}, f32[5,5,8,128]{3,2,1,0:T(8,128)S(1)}, u32[]{:S(2)}, u32[]{:S(2)}) %collective-permute-start.15) | collective-permute-done | bytes 102432 | tf_op jit(solution)/shard_map/ppermute | solution.py:473
  60.2 3.4 %collective-permute-done.16.refs_7_ = f32[5,5,8,128]{3,2,1,0:T(8,128)S(1)} collective-permute-done((f32[5,5,8,128]{3,2,1,0:T(8,128)S(1)}, f32[5,5,8,128]{3,2,1,0:T(8,128)S(1)}, u32[]{:S(2)}, u32[]{:S(2)}) %collective-permute-start.16) | collective-permute-done | bytes 102432 | tf_op jit(solution)/shard_map/ppermute | solution.py:473
  63.6 1.2 %stage_two.1 = (f32[5,27,8,128]{3,2,1,0:T(8,128)S(1)}, f32[5,5,8,128]{3,2,1,0:T(8,128)S(1)}, f32[5,5,8,128]{3,2,1,0:T(8,128)S(1)}, f32[5,5,8,128]{3,2,1,0:T(8,128)S(1)}, f32[5,5,8,128]{3,2,1,0:T(8,128)S(1)}) custom-call(f32[5,27,8,128]{3,2,1,0:T(8,128)S(1)} %get-tuple-element.49.refs_0_, f32[5,27,8,128]{3,2,1,0:T(8,128)S(1)} %get-tuple-element.56.refs_1_, ...), custom_call_target="tpu_custom_call" | custom-call | tf_op jit(solution)/shard_map/stage_two/pallas_call | solution.py:460
  64.9 2.7 %collective-permute-start.18 = (f32[5,5,8,128]{3,2,1,0:T(8,128)S(1)}, f32[5,5,8,128]{3,2,1,0:T(8,128)S(1)}, u32[]{:S(2)}, u32[]{:S(2)}) collective-permute-start(f32[5,5,8,128]{3,2,1,0:T(8,128)S(1)} %get-tuple-element.63), channel_id=1, source_target_pairs={{0,192},{64,0},{128,64},{192,128},{1,193},{65,1},{129,65},{193,129... | collective-permute-start | bytes 307208 | tf_op jit(solution)/shard_map/ppermute | solution.py:473
  67.6 1.4 %collective-permute-start.19 = (f32[5,5,8,128]{3,2,1,0:T(8,128)S(1)}, f32[5,5,8,128]{3,2,1,0:T(8,128)S(1)}, u32[]{:S(2)}, u32[]{:S(2)}) collective-permute-start(f32[5,5,8,128]{3,2,1,0:T(8,128)S(1)} %get-tuple-element.64), channel_id=1, source_target_pairs={{0,8},{8,16},{16,24},{24,32},{32,40},{40,48},{48,56},{56,0},{1,9},... | collective-permute-start | bytes 307208 | tf_op jit(solution)/shard_map/ppermute | solution.py:473
  69.6 1.3 %collective-permute-done.19.refs_6_ = f32[5,5,8,128]{3,2,1,0:T(8,128)S(1)} collective-permute-done((f32[5,5,8,128]{3,2,1,0:T(8,128)S(1)}, f32[5,5,8,128]{3,2,1,0:T(8,128)S(1)}, u32[]{:S(2)}, u32[]{:S(2)}) %collective-permute-start.19) | collective-permute-done | bytes 102432 | tf_op jit(solution)/shard_map/ppermute | solution.py:473
  71.0 3.9 %collective-permute-done.20.refs_7_ = f32[5,5,8,128]{3,2,1,0:T(8,128)S(1)} collective-permute-done((f32[5,5,8,128]{3,2,1,0:T(8,128)S(1)}, f32[5,5,8,128]{3,2,1,0:T(8,128)S(1)}, u32[]{:S(2)}, u32[]{:S(2)}) %collective-permute-start.20) | collective-permute-done | bytes 102432 | tf_op jit(solution)/shard_map/ppermute | solution.py:473
  74.9 1.9 %stage_three.1 = f32[5,27,2,2,128]{4,3,2,1,0:T(2,128)} custom-call(f32[5,27,8,128]{3,2,1,0:T(8,128)S(1)} %get-tuple-element.49.refs_0_, f32[5,27,8,128]{3,2,1,0:T(8,128)S(1)} %get-tuple-element.61.refs_1_, f32[3,27,8,128]{3,2,1,0:T(8,128)S(1)} %get-tuple-element.50.refs_1_.refs_2_, f32[5,9,8,128]{3,2,1,0:T(8,128)S(1)} %get-tuple-element.51.refs_2_.refs_3_, ...), custom_call_target="tpu_custom_call" | custom-call | tf_op jit(solution)/shard_map/stage_three/pallas_call | solution.py:460
  (36 shorter events, 9.7 us)
Async XLA Ops:
  0.6 0.8 %copy-start = (f32[3,3,3,2,2,128]{5,4,3,2,1,0:T(2,128)S(1)}, f32[3,3,3,2,2,128]{5,4,3,2,1,0:T(2,128)}, u32[]{:S(2)}) copy-start(f32[3,3,3,2,2,128]{5,4,3,2,1,0:T(2,128)} %param.3) | copy-start | bytes 165892
  1.4 0.8 %copy-start.1 = (f32[3,3,3,2,2,128]{5,4,3,2,1,0:T(2,128)S(1)}, f32[3,3,3,2,2,128]{5,4,3,2,1,0:T(2,128)}, u32[]{:S(2)}) copy-start(f32[3,3,3,2,2,128]{5,4,3,2,1,0:T(2,128)} %param.4) | copy-start | bytes 165892
  3.3 11.3 %collective-permute-start = (f32[3,8,128]{2,1,0:T(8,128)S(1)}, f32[3,8,128]{2,1,0:T(8,128)S(1)}, u32[]{:S(2)}, u32[]{:S(2)}) collective-permute-start(f32[3,8,128]{2,1,0:T(8,128)S(1)} %get-tuple-element.36), channel_id=1, source_target_pairs={{0,1},{1,2},{2,3},{3,4},{4,5},{5,6},{6,7},{7,0},{8,9},{9,10},{10,1... | collective-permute-start | bytes 36872 | tf_op jit(solution)/shard_map/ppermute | solution.py:473
  4.6 10.1 %collective-permute-start.1 = (f32[3,8,128]{2,1,0:T(8,128)S(1)}, f32[3,8,128]{2,1,0:T(8,128)S(1)}, u32[]{:S(2)}, u32[]{:S(2)}) collective-permute-start(f32[3,8,128]{2,1,0:T(8,128)S(1)} %get-tuple-element.37), channel_id=1, source_target_pairs={{0,7},{1,0},{2,1},{3,2},{4,3},{5,4},{6,5},{7,6},{8,15},{9,8},{10,9... | collective-permute-start | bytes 36872 | tf_op jit(solution)/shard_map/ppermute | solution.py:473
  10.8 6.9 %collective-permute-start.8 = (f32[8,128]{1,0:T(8,128)S(1)}, f32[8,128]{1,0:T(8,128)S(1)}, u32[]{:S(2)}, u32[]{:S(2)}) collective-permute-start(f32[8,128]{1,0:T(8,128)S(1)} %get-tuple-element.46), channel_id=1, source_target_pairs={{0,192},{64,0},{128,64},{192,128},{1,193},{65,1},{129,65},{193,129... | collective-permute-start | bytes 12296 | tf_op jit(solution)/shard_map/ppermute | solution.py:473
  13.6 4.2 %collective-permute-start.7 = (f32[8,128]{1,0:T(8,128)S(1)}, f32[8,128]{1,0:T(8,128)S(1)}, u32[]{:S(2)}, u32[]{:S(2)}) collective-permute-start(f32[8,128]{1,0:T(8,128)S(1)} %get-tuple-element.46), channel_id=1, source_target_pairs={{0,128},{64,192},{128,0},{192,64},{1,129},{65,193},{129,1},{193,65... | collective-permute-start | bytes 12296 | tf_op jit(solution)/shard_map/ppermute | solution.py:473
  13.9 3.8 %collective-permute-start.6 = (f32[8,128]{1,0:T(8,128)S(1)}, f32[8,128]{1,0:T(8,128)S(1)}, u32[]{:S(2)}, u32[]{:S(2)}) collective-permute-start(f32[8,128]{1,0:T(8,128)S(1)} %get-tuple-element.46), channel_id=1, source_target_pairs={{0,64},{64,128},{128,192},{192,0},{1,65},{65,129},{129,193},{193,1... | collective-permute-start | bytes 12296 | tf_op jit(solution)/shard_map/ppermute | solution.py:473
  15.0 4.5 %collective-permute-start.2 = (f32[12,8,128]{2,1,0:T(8,128)S(1)}, f32[12,8,128]{2,1,0:T(8,128)S(1)}, u32[]{:S(2)}, u32[]{:S(2)}) collective-permute-start(f32[12,8,128]{2,1,0:T(8,128)S(1)} %get-tuple-element.40), channel_id=1, source_target_pairs={{0,64},{64,128},{128,192},{192,0},{1,65},{65,129},{129,193},{193,1... | collective-permute-start | bytes 147464 | tf_op jit(solution)/shard_map/ppermute | solution.py:473
  16.6 3.5 %collective-permute-start.3 = (f32[18,8,128]{2,1,0:T(8,128)S(1)}, f32[18,8,128]{2,1,0:T(8,128)S(1)}, u32[]{:S(2)}, u32[]{:S(2)}) collective-permute-start(f32[18,8,128]{2,1,0:T(8,128)S(1)} %get-tuple-element.41), channel_id=1, source_target_pairs={{0,192},{64,0},{128,64},{192,128},{1,193},{65,1},{129,65},{193,129... | collective-permute-start | bytes 221192 | tf_op jit(solution)/shard_map/ppermute | solution.py:473
  20.2 19.2 %collective-permute-start.5 = (f32[21,8,128]{2,1,0:T(8,128)S(1)}, f32[21,8,128]{2,1,0:T(8,128)S(1)}, u32[]{:S(2)}, u32[]{:S(2)}) collective-permute-start(f32[21,8,128]{2,1,0:T(8,128)S(1)} %get-tuple-element.45), channel_id=1, source_target_pairs={{0,56},{8,0},{16,8},{24,16},{32,24},{40,32},{48,40},{56,48},{1,57}... | collective-permute-start | bytes 258056 | tf_op jit(solution)/shard_map/ppermute | solution.py:473
  24.1 15.2 %all-to-all-start = ((f32[64,1,128]{2,1,0:T(1,128)}), f32[64,1,128]{2,1,0:T(1,128)S(1)}, u32[]{:S(2)}, u32[]{:S(2)}) async-start(f32[64,1,128]{2,1,0:T(1,128)} %broadcast_in_dim.2), calls=%async_computation | async-start | bytes 65536 | tf_op jit(solution)/shard_map/all_to_all | solution.py:502
  33.1 6.3 %collective-permute-start.4 = (f32[12,8,128]{2,1,0:T(8,128)S(1)}, f32[12,8,128]{2,1,0:T(8,128)S(1)}, u32[]{:S(2)}, u32[]{:S(2)}) collective-permute-start(f32[12,8,128]{2,1,0:T(8,128)S(1)} %get-tuple-element.44), channel_id=1, source_target_pairs={{0,8},{8,16},{16,24},{24,32},{32,40},{40,48},{48,56},{56,0},{1,9},... | collective-permute-start | bytes 147464 | tf_op jit(solution)/shard_map/ppermute | solution.py:473
  40.4 6.5 %collective-permute-start.9 = (f32[5,5,8,128]{3,2,1,0:T(8,128)S(1)}, f32[5,5,8,128]{3,2,1,0:T(8,128)S(1)}, u32[]{:S(2)}, u32[]{:S(2)}) collective-permute-start(f32[5,5,8,128]{3,2,1,0:T(8,128)S(1)} %get-tuple-element.52), channel_id=1, source_target_pairs={{0,64},{64,128},{128,192},{192,0},{1,65},{65,129},{129,193},{193,1... | collective-permute-start | bytes 307208 | tf_op jit(solution)/shard_map/ppermute | solution.py:473
  41.7 5.2 %collective-permute-start.10 = (f32[5,5,8,128]{3,2,1,0:T(8,128)S(1)}, f32[5,5,8,128]{3,2,1,0:T(8,128)S(1)}, u32[]{:S(2)}, u32[]{:S(2)}) collective-permute-start(f32[5,5,8,128]{3,2,1,0:T(8,128)S(1)} %get-tuple-element.53), channel_id=1, source_target_pairs={{0,192},{64,0},{128,64},{192,128},{1,193},{65,1},{129,65},{193,129... | collective-permute-start | bytes 307208 | tf_op jit(solution)/shard_map/ppermute | solution.py:473
  43.1 5.7 %collective-permute-start.11 = (f32[5,5,8,128]{3,2,1,0:T(8,128)S(1)}, f32[5,5,8,128]{3,2,1,0:T(8,128)S(1)}, u32[]{:S(2)}, u32[]{:S(2)}) collective-permute-start(f32[5,5,8,128]{3,2,1,0:T(8,128)S(1)} %get-tuple-element.54), channel_id=1, source_target_pairs={{0,8},{8,16},{16,24},{24,32},{32,40},{40,48},{48,56},{56,0},{1,9},... | collective-permute-start | bytes 307208 | tf_op jit(solution)/shard_map/ppermute | solution.py:473
  46.8 5.9 %collective-permute-start.12 = (f32[5,5,8,128]{3,2,1,0:T(8,128)S(1)}, f32[5,5,8,128]{3,2,1,0:T(8,128)S(1)}, u32[]{:S(2)}, u32[]{:S(2)}) collective-permute-start(f32[5,5,8,128]{3,2,1,0:T(8,128)S(1)} %get-tuple-element.55), channel_id=1, source_target_pairs={{0,56},{8,0},{16,8},{24,16},{32,24},{40,32},{48,40},{56,48},{1,57}... | collective-permute-start | bytes 307208 | tf_op jit(solution)/shard_map/ppermute | solution.py:473
  53.9 5.0 %collective-permute-start.13 = (f32[5,5,8,128]{3,2,1,0:T(8,128)S(1)}, f32[5,5,8,128]{3,2,1,0:T(8,128)S(1)}, u32[]{:S(2)}, u32[]{:S(2)}) collective-permute-start(f32[5,5,8,128]{3,2,1,0:T(8,128)S(1)} %get-tuple-element.57), channel_id=1, source_target_pairs={{0,64},{64,128},{128,192},{192,0},{1,65},{65,129},{129,193},{193,1... | collective-permute-start | bytes 307208 | tf_op jit(solution)/shard_map/ppermute | solution.py:473
  54.2 4.6 %collective-permute-start.14 = (f32[5,5,8,128]{3,2,1,0:T(8,128)S(1)}, f32[5,5,8,128]{3,2,1,0:T(8,128)S(1)}, u32[]{:S(2)}, u32[]{:S(2)}) collective-permute-start(f32[5,5,8,128]{3,2,1,0:T(8,128)S(1)} %get-tuple-element.58), channel_id=1, source_target_pairs={{0,192},{64,0},{128,64},{192,128},{1,193},{65,1},{129,65},{193,129... | collective-permute-start | bytes 307208 | tf_op jit(solution)/shard_map/ppermute | solution.py:473
  56.8 3.4 %collective-permute-start.15 = (f32[5,5,8,128]{3,2,1,0:T(8,128)S(1)}, f32[5,5,8,128]{3,2,1,0:T(8,128)S(1)}, u32[]{:S(2)}, u32[]{:S(2)}) collective-permute-start(f32[5,5,8,128]{3,2,1,0:T(8,128)S(1)} %get-tuple-element.59), channel_id=1, source_target_pairs={{0,8},{8,16},{16,24},{24,32},{32,40},{40,48},{48,56},{56,0},{1,9},... | collective-permute-start | bytes 307208 | tf_op jit(solution)/shard_map/ppermute | solution.py:473
  57.7 5.9 %collective-permute-start.16 = (f32[5,5,8,128]{3,2,1,0:T(8,128)S(1)}, f32[5,5,8,128]{3,2,1,0:T(8,128)S(1)}, u32[]{:S(2)}, u32[]{:S(2)}) collective-permute-start(f32[5,5,8,128]{3,2,1,0:T(8,128)S(1)} %get-tuple-element.60), channel_id=1, source_target_pairs={{0,56},{8,0},{16,8},{24,16},{32,24},{40,32},{48,40},{56,48},{1,57}... | collective-permute-start | bytes 307208 | tf_op jit(solution)/shard_map/ppermute | solution.py:473
  64.8 4.8 %collective-permute-start.17 = (f32[5,5,8,128]{3,2,1,0:T(8,128)S(1)}, f32[5,5,8,128]{3,2,1,0:T(8,128)S(1)}, u32[]{:S(2)}, u32[]{:S(2)}) collective-permute-start(f32[5,5,8,128]{3,2,1,0:T(8,128)S(1)} %get-tuple-element.62), channel_id=1, source_target_pairs={{0,64},{64,128},{128,192},{192,0},{1,65},{65,129},{129,193},{193,1... | collective-permute-start | bytes 307208 | tf_op jit(solution)/shard_map/ppermute | solution.py:473
  64.9 4.7 %collective-permute-start.18 = (f32[5,5,8,128]{3,2,1,0:T(8,128)S(1)}, f32[5,5,8,128]{3,2,1,0:T(8,128)S(1)}, u32[]{:S(2)}, u32[]{:S(2)}) collective-permute-start(f32[5,5,8,128]{3,2,1,0:T(8,128)S(1)} %get-tuple-element.63), channel_id=1, source_target_pairs={{0,192},{64,0},{128,64},{192,128},{1,193},{65,1},{129,65},{193,129... | collective-permute-start | bytes 307208 | tf_op jit(solution)/shard_map/ppermute | solution.py:473
  67.6 3.4 %collective-permute-start.19 = (f32[5,5,8,128]{3,2,1,0:T(8,128)S(1)}, f32[5,5,8,128]{3,2,1,0:T(8,128)S(1)}, u32[]{:S(2)}, u32[]{:S(2)}) collective-permute-start(f32[5,5,8,128]{3,2,1,0:T(8,128)S(1)} %get-tuple-element.64), channel_id=1, source_target_pairs={{0,8},{8,16},{16,24},{24,32},{32,40},{40,48},{48,56},{56,0},{1,9},... | collective-permute-start | bytes 307208 | tf_op jit(solution)/shard_map/ppermute | solution.py:473
  69.0 5.9 %collective-permute-start.20 = (f32[5,5,8,128]{3,2,1,0:T(8,128)S(1)}, f32[5,5,8,128]{3,2,1,0:T(8,128)S(1)}, u32[]{:S(2)}, u32[]{:S(2)}) collective-permute-start(f32[5,5,8,128]{3,2,1,0:T(8,128)S(1)} %get-tuple-element.65), channel_id=1, source_target_pairs={{0,56},{8,0},{16,8},{24,16},{32,24},{40,32},{48,40},{56,48},{1,57}... | collective-permute-start | bytes 307208 | tf_op jit(solution)/shard_map/ppermute | solution.py:473
  (1 other events, 0.8 us)
where the time goes:
time: 77.1 us; the launch traced here: 76.8 us
  starting transfers between devices  41.1 us (53%)
  waiting for transfers between devices  26 us (34%)
  Pallas kernels  5.88 us (8%)
  local copies, waits for them, and re-layouts  3.05 us (4%)
    ppermute x21, starting transfers between devices, send(): lax.ppermute(value, axis, [(i, (i + by) % count) for i in range(count)])  32.1 us
    ppermute x21, waiting for transfers between devices, send(): lax.ppermute(value, axis, [(i, (i + by) % count) for i in range(count)])  20 us
    all_to_all x1, starting transfers between devices, shards(): tops = lax.all_to_all(spread, ('gy', 'gz'), 0, 0, tiled=True)  8.98 us
    all_to_all x1, waiting for transfers between devices, shards(): tops = lax.all_to_all(spread, ('gy', 'gz'), 0, 0, tiled=True)  5.99 us
    pallas_call x7, Pallas kernels, call(): pl.pallas_call(kernel, out_shape=[jax.ShapeDtypeStruct(o, F32) for o in o...  5.88 us
    unnamed x6, local copies, waits for them, and re-layouts  2.42 us
  transfers between devices with their start and end apart: 22, of which 11 were waited for; matrix products, arithmetic and copies ran while one was open for 1% of the time, Pallas kernels for 0%

commit v1 on v0

--- a/solution.py
+++ b/solution.py
@@ -6,12 +6,19 @@
 from jax import lax
 from jax.experimental import pallas as pl
 from jax.experimental.pallas import tpu as pltpu
+from jax.sharding import Mesh
 from jax.sharding import PartitionSpec as P
 
 GAMMA = 1.4
 CFL = 0.1
 F32 = jnp.float32
 TILE = (8, 128)
+GX = ("gx",)
+GY = ("zl", "co")
+GZ = ("zh", "xx")
+FLAT = ("gx", "xx")
+DEEP = ("zl", "co", "zh")
+WEIGHT = pl.CostEstimate(flops=10**11, bytes_accessed=10**8, transcendentals=0)
 GROUP = 14
 
 
@@ -84,6 +91,7 @@
         row = row_index()
         lane = lane_index()
         self.first = {2: (row & 2) == 0, 1: (row & 1) == 0}
+        self.own = row < 4
         self.top = lane == 127
         self.bottom = lane == 0
 
@@ -100,6 +108,14 @@
     def next(self, own, packed, second, step):
         outside = packed if second else roll_rows(packed, step)
         return jnp.where(self.first[step], roll_rows(own, -step), outside)
+
+    def beside(self, over, under, step):
+        return jnp.where(self.first[step], over, under)
+
+    def before(self, first_from, second_from, step):
+        return jnp.where(
+            self.first[step], roll_rows(first_from, -step), roll_rows(second_from, step)
+        )
 
     def z_prev(self, x):
         t = roll_lanes(x, 1)
@@ -134,6 +150,92 @@
     return result
 
 
+def message_size(halves):
+    tiles = -(-halves // 2)
+    return -(-tiles // 2) + -(-tiles // 32)
+
+
+def write_message(sh, ref, values, high, step):
+    values = list(values)
+    if len(values) % 2:
+        values.append(None)
+    pack = sh.pack_high if high else sh.pack_low
+    tiles = [pack(values[n], values[n + 1], step) for n in range(0, len(values), 2)]
+    group = lane_index() // 8
+    base = -(-len(tiles) // 2)
+    halos = []
+    for n, tile in enumerate(tiles):
+        moved = roll_lanes(tile, 8 * (n % 16) + 4)
+        if n % 16 == 0:
+            halos.append(moved)
+        else:
+            halos[-1] = jnp.where(group == n % 16, moved, halos[-1])
+    if len(tiles) % 2:
+        tiles.append(tiles[-1])
+    if len(halos) % 2:
+        halos.append(halos[-1])
+    for n in range(0, len(tiles), 2):
+        ref[n // 2] = jnp.where(sh.own, tiles[n], roll_rows(tiles[n + 1], 4))
+    for n in range(0, len(halos), 2):
+        ref[base + n // 2] = jnp.where(sh.own, roll_rows(halos[n], 4), halos[n + 1])
+
+
+def read_message(sh, ref, keys, high, step):
+    places = {key: n for n, key in enumerate(keys)}
+    base = -(-(-(-len(keys) // 2)) // 2)
+
+    def get(key):
+        n, odd = divmod(places[key], 2)
+        main = ref[n // 2]
+        if n % 2:
+            main = roll_rows(main, 4)
+        halo = ref[base + n // 32]
+        if n // 16 % 2 == 0:
+            halo = roll_rows(halo, 4)
+        tile = jnp.where(sh.own, main, roll_lanes(halo, 124 - 8 * (n % 16)))
+        if odd:
+            tile = roll_rows(tile, step if high else -step)
+        return tile
+
+    return get
+
+
+FIELDS = range(4)
+TRIPLE = range(3)
+PAIR = range(2)
+
+
+def x_keys(high):
+    keys = [("sum", f, a, b, z) for f in FIELDS for a in TRIPLE for b in TRIPLE for z in PAIR]
+    nodes = 2 if high else 3
+    keys += [("old", d, a, p, z) for d in TRIPLE for a in range(nodes) for p in PAIR for z in PAIR]
+    return keys + side_keys()
+
+
+def side_keys():
+    keys = [("rho",) + key for key in POINTS]
+    return keys + [("heat", m, n) for m in TRIPLE for n in TRIPLE]
+
+
+def y_keys(high):
+    keys = [("sum", f, a, b, z) for f in FIELDS for a in TRIPLE for b in TRIPLE for z in PAIR]
+    keys += [("side", f, a, z) for f in FIELDS for a in TRIPLE for z in PAIR]
+    nodes = 2 if high else 3
+    keys += [("old", d, a, b, z) for d in TRIPLE for a in TRIPLE for b in range(nodes) for z in PAIR]
+    if not high:
+        keys += [("old_side", d, a, z) for d in TRIPLE for a in TRIPLE for z in PAIR]
+    return keys + side_keys()
+
+
+def side_values(rho, direction, trace):
+    values = {("rho",) + key: rho[0, point(*key)] for key in POINTS}
+    for m in TRIPLE:
+        for n in TRIPLE:
+            keys = [(a, m, n) if direction == 0 else (m, a, n) for a in TRIPLE]
+            values["heat", m, n] = combine([rho[1, point(*k)] for k in keys], trace)
+    return values
+
+
 POINTS = [(a, b, c) for a in range(3) for b in range(3) for c in range(3)]
 
 
@@ -149,7 +251,7 @@
             both[q, 2 * i : 2 * i + 2, :] = dens[q, i]
             both[q, 4 + 2 * i : 6 + 2 * i, :] = ener[q, i]
             low = jnp.maximum(low, ener[q, i])
-    top[...] = jnp.broadcast_to(jnp.max(low, keepdims=True), TILE)
+    top[...] = jnp.broadcast_to(jnp.max(low, keepdims=True), top.shape)
     half = (2 * lane) % 128
     for d in range(3):
         for px in range(2):
@@ -180,18 +282,25 @@
         to_down[t] = down
 
 
+def top_kernel(tops, spread):
+    spread[...] = jnp.broadcast_to(jnp.max(tops[...], axis=0, keepdims=True), spread.shape)
+
+
+def step_kernel(tops, step):
+    top = jnp.broadcast_to(jnp.max(tops[...], axis=0, keepdims=True), TILE)
+    step[...] = CFL / jnp.sqrt((GAMMA * (GAMMA - 1.0)) * top)
+
+
 def force_kernel(both, nodes, from_below, from_above, rho, vz, parts, to_right, to_left):
     sh = Shifts()
-    row = row_index()
-    own = row < 4
     lane = lane_index()
     merged = [jnp.where((lane & 7) < 4, from_below[t], from_above[t]) for t in range(3)]
 
     def extend(tile, t, g):
         halo = roll_lanes(merged[t], 124 - 8 * g)
         return (
-            jnp.where(own, tile, roll_rows(halo, 4)),
-            jnp.where(own, roll_rows(tile, 4), halo),
+            jnp.where(sh.own, tile, roll_rows(halo, 4)),
+            jnp.where(sh.own, roll_rows(tile, 4), halo),
         )
 
     density = {}
@@ -199,15 +308,15 @@
     for key in POINTS:
         q = point(*key)
         dens, ener = extend(both[q], q // GROUP, q % GROUP)
+        heat = dens * ener
         rho[0, q] = dens
-        heat = dens * ener
         rho[1, q] = heat
         density[key] = dens
         pressure[key] = (GAMMA - 1.0) * heat
     for n in range(12):
         even, odd = extend(nodes[n], 2, n)
-        vz[2 * n] = even
-        vz[2 * n + 1] = odd
+        vz[n, 0] = even
+        vz[n, 1] = odd
     fb = TAB["force_b"]
     fd = TAB["force_d"]
     along_b = contract(pressure, fb, 0)
@@ -219,49 +328,101 @@
         contract(bb, fd, 2),
         contract(contract(contract(density, fb, 0), fb, 1), fb, 2),
     ]
-    for f in range(4):
-        for a in range(3):
-            for b in range(3):
-                even = fields[f][a, b, 0] + sh.z_prev(fields[f][a, b, 2])
-                odd = fields[f][a, b, 1]
-                parts[f, 3 * a + b, 0] = even
-                parts[f, 3 * a + b, 1] = odd
-                if a == 2:
-                    to_right[3 * f + b] = sh.pack_high(even, odd, 2)
-                if a == 0:
-                    to_left[3 * f + b] = sh.pack_low(even, odd, 2)
-    for d in range(3):
-        for py in range(2):
-            n = 4 * d + py
-            to_left[12 + 2 * d + py] = sh.pack_low(vz[2 * n], vz[2 * n + 1], 2)
-
-
-def rim_kernel(parts, vz, from_left, from_right, sums, ev, to_up, to_down):
+    for f in FIELDS:
+        for a in TRIPLE:
+            for b in TRIPLE:
+                parts[f, 3 * a + b, 0] = fields[f][a, b, 0] + sh.z_prev(fields[f][a, b, 2])
+                parts[f, 3 * a + b, 1] = fields[f][a, b, 1]
+    for high, ref, trace in ((True, to_right, "high_trace"), (False, to_left, "low_trace")):
+        values = side_values(rho, 0, TAB[trace])
+        for f in FIELDS:
+            for b in TRIPLE:
+                for z in PAIR:
+                    line = [parts[f, 3 * a + b, z] for a in TRIPLE]
+                    if high:
+                        line[0] = line[0] + roll_rows(line[2], 2)
+                    else:
+                        line[2] = line[2] + roll_rows(line[0], -2)
+                    for a in TRIPLE:
+                        values["sum", f, a, b, z] = line[a]
+        for d in TRIPLE:
+            for p in PAIR:
+                for z in PAIR:
+                    first = vz[4 * d + p, z]
+                    values["old", d, 0, p, z] = first
+                    values["old", d, 1, p, z] = vz[4 * d + 2 + p, z]
+                    values["old", d, 2, p, z] = roll_rows(first, -2)
+        write_message(sh, ref, [values[key] for key in x_keys(high)], high, 2)
+
+
+def assemble(sh, own, side, step):
+    inner = [own[0] + sh.before(side[2], own[2], step), own[1], own[2] + sh.before(own[0], side[0], step)]
+    outer = [
+        jnp.where(sh.first[step], side[0] + roll_rows(own[2], -step), side[0]),
+        side[1],
+        jnp.where(sh.first[step], side[2], side[2] + roll_rows(own[0], step)),
+    ]
+    return inner, outer
+
+
+def rim_kernel(
+    parts, vz, rho, from_left, from_right,
+    sums, sums_x, old, old_x, rho_x, heat_x, to_up, to_down,
+):
     sh = Shifts()
-    for f in range(4):
-        for b in range(3):
-            for z in range(2):
-                first = parts[f, b, z]
-                last = parts[f, 6 + b, z]
-                full = [
-                    first + sh.prev(last, from_left[3 * f + b], z, 2),
-                    parts[f, 3 + b, z],
-                    last + sh.next(first, from_right[3 * f + b], z, 2),
-                ]
-                for a in range(3):
-                    sums[f, 3 * a + b, z] = full[a]
-        for a in range(3):
-            to_up[3 * f + a] = sh.pack_high(sums[f, 3 * a + 2, 0], sums[f, 3 * a + 2, 1], 1)
-            to_down[3 * f + a] = sh.pack_low(sums[f, 3 * a, 0], sums[f, 3 * a, 1], 1)
-    for d in range(3):
-        for py in range(2):
-            for z in range(2):
-                first = vz[2 * (4 * d + py) + z]
-                ev[d, py, z] = first
-                ev[d, 2 + py, z] = vz[2 * (4 * d + 2 + py) + z]
-                ev[d, 4 + py, z] = sh.next(first, from_right[12 + 2 * d + py], z, 2)
-        for a in range(3):
-            to_down[12 + 3 * d + a] = sh.pack_low(ev[d, 2 * a, 0], ev[d, 2 * a, 1], 1)
+    left = read_message(sh, from_left, x_keys(True), True, 2)
+    right = read_message(sh, from_right, x_keys(False), False, 2)
+
+    def beside(*key):
+        return sh.beside(right(key), left(key), 2)
+
+    for f in FIELDS:
+        for b in TRIPLE:
+            for z in PAIR:
+                own = [parts[f, 3 * a + b, z] for a in TRIPLE]
+                side = [beside("sum", f, a, b, z) for a in TRIPLE]
+                inner, outer = assemble(sh, own, side, 2)
+                for a in TRIPLE:
+                    sums[f, 3 * a + b, z] = inner[a]
+                    sums_x[f, 3 * a + b, z] = outer[a]
+    for d in TRIPLE:
+        for p in PAIR:
+            for z in PAIR:
+                first = vz[4 * d + p, z]
+                beyond = beside("old", d, 0, p, z)
+                old[d, p, z] = first
+                old[d, 2 + p, z] = vz[4 * d + 2 + p, z]
+                old[d, 4 + p, z] = sh.before(first, beyond, 2)
+                old_x[d, p, z] = beyond
+                old_x[d, 2 + p, z] = beside("old", d, 1, p, z)
+                old_x[d, 4 + p, z] = sh.beside(right(("old", d, 2, p, z)), roll_rows(first, 2), 2)
+    for key in POINTS:
+        rho_x[point(*key)] = beside("rho", *key)
+    for m in TRIPLE:
+        for n in TRIPLE:
+            heat_x[3 * m + n] = beside("heat", m, n)
+    for high, ref, trace in ((True, to_up, "high_trace"), (False, to_down, "low_trace")):
+        values = side_values(rho, 1, TAB[trace])
+        for f in FIELDS:
+            for a in TRIPLE:
+                for z in PAIR:
+                    line = [sums[f, 3 * a + b, z] for b in TRIPLE]
+                    if high:
+                        line[0] = line[0] + roll_rows(line[2], 1)
+                    else:
+                        line[2] = line[2] + roll_rows(line[0], -1)
+                    for b in TRIPLE:
+                        values["sum", f, a, b, z] = line[b]
+                    values["side", f, a, z] = sums_x[f, 3 * a + (2 if high else 0), z]
+        for d in TRIPLE:
+            for a in TRIPLE:
+                for z in PAIR:
+                    first = old[d, 2 * a, z]
+                    values["old", d, a, 0, z] = first
+                    values["old", d, a, 1, z] = old[d, 2 * a + 1, z]
+                    values["old", d, a, 2, z] = roll_rows(first, -1)
+                    values["old_side", d, a, z] = old_x[d, 2 * a, z]
+        write_message(sh, ref, [values[key] for key in y_keys(high)], high, 1)
 
 
 def face_messages(sh, fields, f, right, left, up, down):
@@ -286,41 +447,56 @@
 
 
 def velocity_kernel(
-    sums, ev, from_down, from_up, tops, rho,
-    new_vel, u0, disp, speeds, right, left, up, down, split, wide,
+    scale, sums, sums_x, old, old_x, rho, rho_x, heat_x, from_down, from_up,
+    new_vel, u0, disp, speeds, sides, split, wide,
 ):
     sh = Shifts()
     lane = lane_index()
-    top = tops[0:8]
-    for n in range(1, tops.shape[0] // 8):
-        top = jnp.maximum(top, tops[8 * n : 8 * n + 8])
-    for by in (4, 2, 1):
-        top = jnp.maximum(top, roll_rows(top, by))
-    step = CFL / jnp.sqrt((GAMMA * (GAMMA - 1.0)) * top)
-    vel = [{} for _ in range(3)]
-    for a in range(3):
-        for z in range(2):
+    step = scale[...]
+    down = read_message(sh, from_down, y_keys(True), True, 1)
+    up = read_message(sh, from_up, y_keys(False), False, 1)
+
+    def beside(*key):
+        return sh.beside(up(key), down(key), 1)
+
+    centre = [{} for _ in TRIPLE]
+    side_x = [{} for _ in TRIPLE]
+    side_y = [{} for _ in TRIPLE]
+    for a in TRIPLE:
+        for z in PAIR:
             total = []
-            for f in range(4):
-                first = sums[f, 3 * a, z]
-                last = sums[f, 3 * a + 2, z]
-                total.append(
+            for f in FIELDS:
+                own = [sums[f, 3 * a + b, z] for b in TRIPLE]
+                inner, outer = assemble(sh, own, [beside("sum", f, a, b, z) for b in TRIPLE], 1)
+                aside = [sums_x[f, 3 * a + b, z] for b in TRIPLE]
+                aside = [
+                    aside[0] + sh.before(down(("side", f, a, z)), aside[2], 1),
+                    aside[1],
+                    aside[2] + sh.before(aside[0], up(("side", f, a, z)), 1),
+                ]
+                total.append((inner, aside, outer))
+            for d in TRIPLE:
+                first = old[d, 2 * a, z]
+                first_x = old_x[d, 2 * a, z]
+                beyond = beside("old", d, a, 0, z)
+                olds = (
+                    [first, old[d, 2 * a + 1, z], sh.before(first, beyond, 1)],
                     [
-                        first + sh.prev(last, from_down[3 * f + a], z, 1),
-                        sums[f, 3 * a + 1, z],
-                        last + sh.next(first, from_up[3 * f + a], z, 1),
-                    ]
+                        first_x,
+                        old_x[d, 2 * a + 1, z],
+                        sh.before(first_x, up(("old_side", d, a, z)), 1),
+                    ],
+                    [
+                        beyond,
+                        beside("old", d, a, 1, z),
+                        sh.beside(up(("old", d, a, 2, z)), roll_rows(first, 1), 1),
+                    ],
                 )
-            scale = [step / total[3][b] for b in range(3)]
-            for d in range(3):
-                first = ev[d, 2 * a, z]
-                old = [
-                    first,
-                    ev[d, 2 * a + 1, z],
-                    sh.next(first, from_up[12 + 3 * d + a], z, 1),
-                ]
-                for b in range(3):
-                    vel[d][a, b, z] = old[b] + total[d][b] * scale[b]
+                for kind, target in enumerate((centre, side_x, side_y)):
+                    for b in TRIPLE:
+                        over_mass = step / total[3][kind][b]
+                        target[d][a, b, z] = olds[kind][b] + total[d][kind][b] * over_mass
+    vel = centre
     for d in range(3):
         for px in range(2):
             slot = 2 * d + px
@@ -347,52 +523,77 @@
         line = [even, odd, sh.z_next(even)]
         return [combine(line, column(eb, q)) for q in range(3)]
 
+    def at_points(nodes, own):
+        gauss = [{} for _ in range(3)]
+        for d in range(3):
+            across = {}
+            for b in range(3):
+                for z in range(2):
+                    line = [nodes[d][a, b, z] for a in range(3)]
+                    for q in range(3):
+                        across[q, b, z] = combine(line, column(eb, q))
+            if d == 1 and own:
+                for b, at in ((0, 2), (2, 3)):
+                    for q in range(3):
+                        for c, value in enumerate(along_z(across[q, b, 0], across[q, b, 1])):
+                            speeds[at, 3 * q + c] = minus * value
+            for qx in range(3):
+                for qy in range(3):
+                    pair = [
+                        combine([across[qx, b, z] for b in range(3)], column(eb, qy))
+                        for z in range(2)
+                    ]
+                    if d == 2 and own:
+                        speeds[4, 3 * qx + qy] = minus * pair[0]
+                    for c, value in enumerate(along_z(*pair)):
+                        gauss[d][qx, qy, c] = value
+                        if own:
+                            disp[d, point(qx, qy, c)] = minus * value
+        return gauss
+
     for a, at in ((0, 0), (2, 1)):
         for q in range(3):
             pair = [combine([vel[0][a, b, z] for b in range(3)], column(eb, q)) for z in range(2)]
             for c, value in enumerate(along_z(*pair)):
                 speeds[at, 3 * q + c] = minus * value
-    gauss = [{} for _ in range(3)]
+    gauss = at_points(centre, True)
+    for q in range(27):
+        u0[0, q] = rho[0, q]
+        u0[1, q] = rho[1, q]
     for d in range(3):
-        across = {}
-        for b in range(3):
-            for z in range(2):
-                line = [vel[d][a, b, z] for a in range(3)]
-                for q in range(3):
-                    across[q, b, z] = combine(line, column(eb, q))
-        if d == 1:
-            for b, at in ((0, 2), (2, 3)):
-                for q in range(3):
-                    for c, value in enumerate(along_z(across[q, b, 0], across[q, b, 1])):
-                        speeds[at, 3 * q + c] = minus * value
-        for qx in range(3):
-            for qy in range(3):
-                pair = [
-                    combine([across[qx, b, z] for b in range(3)], column(eb, qy)) for z in range(2)
-                ]
-                if d == 2:
-                    speeds[4, 3 * qx + qy] = minus * pair[0]
-                for c, value in enumerate(along_z(*pair)):
-                    gauss[d][qx, qy, c] = value
-                    disp[d, point(qx, qy, c)] = minus * value
-    for f in range(5):
-        fields = {}
         for key in POINTS:
-            q = point(*key)
-            if f < 2:
-                fields[key] = rho[f, q]
-            else:
-                fields[key] = rho[0, q] * gauss[f - 2][key]
-            u0[f, q] = fields[key]
-        face_messages(sh, fields, f, right, left, up, down)
+            u0[2 + d, point(*key)] = rho[0, point(*key)] * gauss[d][key]
+    low = TAB["low_trace"]
+    high = TAB["high_trace"]
+    for side, nodes in enumerate((side_x, side_y)):
+        turn = 2 - side
+        gauss = at_points(nodes, False)
+        trace = [jnp.where(sh.first[turn], low[a], high[a]) for a in TRIPLE]
+        weigh = {}
+        for key in POINTS:
+            dens = beside("rho", *key) if side else rho_x[point(*key)]
+            weigh[key] = trace[key[side]] * dens
+        for m in TRIPLE:
+            for n in TRIPLE:
+                keys = [(a, m, n) if side == 0 else (m, a, n) for a in TRIPLE]
+                at = 3 * m + n
+                sides[side, 0, at] = weigh[keys[0]] + weigh[keys[1]] + weigh[keys[2]]
+                sides[side, 1, at] = beside("heat", m, n) if side else heat_x[at]
+                for d in TRIPLE:
+                    sides[side, 2 + d, at] = sum(weigh[k] * gauss[d][k] for k in keys)
 
 
 def stage_kernel(weight, last, *refs):
     refs = list(refs)
     u0 = refs.pop(0)
     u = u0 if weight is None else refs.pop(0)
-    disp, speeds, from_left, from_right, from_down, from_up = refs[:6]
-    outs = refs[6:]
+    disp, speeds = refs[:2]
+    if weight is None:
+        (sides,) = refs[2:3]
+        outs = refs[3:]
+    else:
+        from_left, from_right, from_down, from_up = refs[2:6]
+        outs = refs[6:]
     sh = Shifts()
     low = TAB["low_trace"]
     high = TAB["high_trace"]
@@ -419,9 +620,13 @@
                     tp = combine(line, high)
                     if d < 2:
                         step = 2 - d
-                        under, over = ((from_left, from_right), (from_down, from_up))[d]
-                        before = sh.prev(tp, under[f, at // 2], at % 2, step)
-                        after = sh.next(tm, over[f, at // 2], at % 2, step)
+                        if weight is None:
+                            before = sh.before(sides[d, f, at], tp, step)
+                            after = sh.before(tm, sides[d, f, at], step)
+                        else:
+                            under, over = ((from_left, from_right), (from_down, from_up))[d]
+                            before = sh.prev(tp, under[f, at // 2], at % 2, step)
+                            after = sh.next(tm, over[f, at // 2], at % 2, step)
                         s_low = speeds[2 * d, at]
                         s_high = speeds[2 * d + 1, at]
                         f_low = s_low * jnp.where(s_low > 0.0, before, tm)
@@ -456,7 +661,7 @@
     lax.fori_loop(0, 5, one_field, 0)
 
 
-def call(kernel, outs, *args, scratch=(), name=None):
+def call(kernel, outs, *args, scratch=(), name=None, weigh=None):
     return pl.pallas_call(
         kernel,
         out_shape=[jax.ShapeDtypeStruct(o, F32) for o in outs],
@@ -464,21 +669,26 @@
         out_specs=[pl.BlockSpec(memory_space=pltpu.VMEM)] * len(outs),
         scratch_shapes=[pltpu.VMEM(s, F32) for s in scratch],
         compiler_params=pltpu.CompilerParams(vmem_limit_bytes=32 * 1024 * 1024),
+        cost_estimate=weigh,
         name=name,
     )(*args)
 
 
+def axis_count(axes):
+    return math.prod(lax.axis_size(axis) for axis in axes)
+
+
 def send(value, axis, by):
-    count = lax.axis_size(axis)
+    count = axis_count(axis)
     return lax.ppermute(value, axis, [(i, (i + by) % count) for i in range(count)])
 
 
 def exchange(right, left, up, down):
     return (
-        send(right, "gx", 1),
-        send(left, "gx", -1),
-        send(up, "gy", 1),
-        send(down, "gy", -1),
+        send(right, GX, 1),
+        send(left, GX, -1),
+        send(up, GY, 1),
+        send(down, GY, -1),
     )
 
 
@@ -488,46 +698,55 @@
     ener = energy.reshape((27,) + energy.shape[3:])
     to_up, to_down, both, nodes, top = call(
         pack_kernel,
-        [(3,) + tile, (3,) + tile, (27,) + tile, (12,) + tile, tile],
+        [(3,) + tile, (3,) + tile, (27,) + tile, (12,) + tile, (axis_count(FLAT), 128)],
         dens, ener, velocity,
         scratch=[(6, 8, 256), (6, 16, 128)],
         name="pack",
     )
-    from_below = send(to_up, "gz", 1)
-    from_above = send(to_down, "gz", -1)
-    tops = [top] + [send(top, "gx", k) for k in range(1, lax.axis_size("gx"))]
-    top = functools.reduce(jnp.maximum, tops)
-    peers = lax.axis_size("gy") * lax.axis_size("gz")
-    spread = jnp.broadcast_to(top[0:1], (peers, 128))
-    tops = lax.all_to_all(spread, ("gy", "gz"), 0, 0, tiled=True)
+    from_below = send(to_up, GZ, 1)
+    from_above = send(to_down, GZ, -1)
+    tops = lax.all_to_all(top, FLAT, 0, 0, tiled=True)
+    (top,) = call(top_kernel, [(axis_count(DEEP), 128)], tops, name="top", weigh=WEIGHT)
+    tops = lax.all_to_all(top, DEEP, 0, 0, tiled=True)
+    (step,) = call(step_kernel, [tile], tops, name="step", weigh=WEIGHT)
+    parts_shape = (4, 9, 2) + tile
+    old_shape = (3, 6, 2) + tile
     rho, vz, parts, to_right, to_left = call(
         force_kernel,
-        [(2, 27) + tile, (24,) + tile, (4, 9, 2) + tile, (12,) + tile, (18,) + tile],
+        [
+            (2, 27) + tile, (12, 2) + tile, parts_shape,
+            (message_size(len(x_keys(True))),) + tile,
+            (message_size(len(x_keys(False))),) + tile,
+        ],
         both, nodes, from_below, from_above,
         name="force",
     )
-    from_left = send(to_right, "gx", 1)
-    from_right = send(to_left, "gx", -1)
-    sums, ev, to_up, to_down = call(
+    from_left = send(to_right, GX, 1)
+    from_right = send(to_left, GX, -1)
+    sums, sums_x, old, old_x, rho_x, heat_x, to_up, to_down = call(
         rim_kernel,
-        [(4, 9, 2) + tile, (3, 6, 2) + tile, (12,) + tile, (21,) + tile],
-        parts, vz, from_left, from_right,
+        [
+            parts_shape, parts_shape, old_shape, old_shape, (27,) + tile, (9,) + tile,
+            (message_size(len(y_keys(True))),) + tile,
+            (message_size(len(y_keys(False))),) + tile,
+        ],
+        parts, vz, rho, from_left, from_right,
         name="rim",
     )
-    from_down = send(to_up, "gy", 1)
-    from_up = send(to_down, "gy", -1)
+    from_down = send(to_up, GY, 1)
+    from_up = send(to_down, GY, -1)
     faces = [(5, 5) + tile] * 4
     state = (5, 27) + tile
-    new_velocity, u0, disp, speeds, *messages = call(
+    new_velocity, u0, disp, speeds, sides = call(
         velocity_kernel,
-        [velocity.shape, state, (3, 27) + tile, (5, 9) + tile] + faces,
-        sums, ev, from_down, from_up, tops, rho,
+        [velocity.shape, state, (3, 27) + tile, (5, 9) + tile, (2, 5, 9) + tile],
+        step, sums, sums_x, old, old_x, rho, rho_x, heat_x, from_down, from_up,
         scratch=[(6, 16, 128), (6, 8, 256)],
         name="velocity",
     )
     one, *messages = call(
         functools.partial(stage_kernel, None, False), [state] + faces,
-        u0, disp, speeds, *exchange(*messages),
+        u0, disp, speeds, sides,
         name="stage_one",
     )
     two, *messages = call(
@@ -544,14 +763,16 @@
 
 
 def solution(mesh):
+    across, high, deep = (mesh.shape[axis] for axis in ("gx", "gy", "gz"))
+    devices = mesh.devices.reshape(across, high // 2, 2, 2, deep // 2)
     return jax.shard_map(
         shards,
-        mesh=mesh,
+        mesh=Mesh(devices, GX + GY + GZ),
         in_specs=(
-            P(None, None, None, "gx", "gy", "gz"),
-            P(None, None, None, "gx", "gy", "gz"),
-            P(None, "gx", "gy", "gz"),
+            P(None, None, None, GX, GY, GZ),
+            P(None, None, None, GX, GY, GZ),
+            P(None, GX, GY, GZ),
         ),
-        out_specs=(P(None, "gx", "gy", "gz"), P(None, None, None, None, "gx", "gy", "gz")),
+        out_specs=(P(None, GX, GY, GZ), P(None, None, None, None, GX, GY, GZ)),
         check_vma=False,
     )

time: 77.1 us -> 67.5 us (0.88)
  the two profiles are of different devices: /device:TPU:97 before, /device:TPU:225 now
where the time goes in v1:
time: 67.5 us; the launch traced here: 67.2 us
  starting transfers between devices  33.8 us (50%)
  waiting for transfers between devices  22 us (33%)
  Pallas kernels  8.22 us (12%)
  local copies, waits for them, and re-layouts  2.42 us (4%)
  between operations  0.72 us (1%)
    ppermute x14, starting transfers between devices, send(): lax.ppermute(value, axis, [(i, (i + by) % count) for i in range(count)])  21.4 us
    ppermute x14, waiting for transfers between devices, send(): lax.ppermute(value, axis, [(i, (i + by) % count) for i in range(count)])  18.2 us
    pallas_call x9, Pallas kernels, call(): pl.pallas_call(kernel, out_shape=[jax.ShapeDtypeStruct(o, F32) for o in o...  8.22 us
    all_to_all x1, starting transfers between devices, shards(): tops = lax.all_to_all(top, DEEP, 0, 0, tiled=True)  8.16 us
    all_to_all x1, starting transfers between devices, shards(): tops = lax.all_to_all(top, FLAT, 0, 0, tiled=True)  4.29 us
    all_to_all x1, waiting for transfers between devices, shards(): tops = lax.all_to_all(top, FLAT, 0, 0, tiled=True)  3.03 us
    unnamed x6, local copies, waits for them, and re-layouts  2.42 us
  transfers between devices with their start and end apart: 16, of which 10 were waited for; matrix products, arithmetic and copies ran while one was open for 0% of the time, Pallas kernels for 3%

profile of v1, /device:TPU:225, one launch (start us, length us, event | category | flops | bytes accessed | tf_op | source)
XLA Modules:
  0.0 67.2 jit_solution(3810182311340028575)
XLA Ops:
  0.6 0.8 %copy-done = f32[3,3,3,2,2,128]{5,4,3,2,1,0:T(2,128)S(1)} copy-done((f32[3,3,3,2,2,128]{5,4,3,2,1,0:T(2,128)S(1)}, f32[3,3,3,2,2,128]{5,4,3,2,1,0:T(2,128)}, u32[]{:S(2)}) %copy-start) | copy-done | bytes 55320
  1.4 0.8 %copy-done.1 = f32[3,3,3,2,2,128]{5,4,3,2,1,0:T(2,128)S(1)} copy-done((f32[3,3,3,2,2,128]{5,4,3,2,1,0:T(2,128)S(1)}, f32[3,3,3,2,2,128]{5,4,3,2,1,0:T(2,128)}, u32[]{:S(2)}) %copy-start.1) | copy-done | bytes 55320
  3.9 1.2 %collective-permute-start = (f32[3,8,128]{2,1,0:T(8,128)S(1)}, f32[3,8,128]{2,1,0:T(8,128)S(1)}, u32[]{:S(2)}, u32[]{:S(2)}) collective-permute-start(f32[3,8,128]{2,1,0:T(8,128)S(1)} %get-tuple-element.38), channel_id=1, source_target_pairs={{0,1},{1,2},{2,3},{3,4},{4,5},{5,6},{6,7},{7,0},{8,9},{9,10},{10,1... | collective-permute-start | bytes 36872 | tf_op jit(solution)/shard_map/ppermute | solution.py:683
  5.1 6.3 %collective-permute-start.1 = (f32[3,8,128]{2,1,0:T(8,128)S(1)}, f32[3,8,128]{2,1,0:T(8,128)S(1)}, u32[]{:S(2)}, u32[]{:S(2)}) collective-permute-start(f32[3,8,128]{2,1,0:T(8,128)S(1)} %get-tuple-element.39), channel_id=1, source_target_pairs={{0,7},{1,0},{2,1},{3,2},{4,3},{5,4},{6,5},{7,6},{8,15},{9,8},{10,9... | collective-permute-start | bytes 36872 | tf_op jit(solution)/shard_map/ppermute | solution.py:683
  11.3 4.3 %all-to-all-start = ((f32[16,1,128]{2,1,0:T(1,128)}), f32[16,1,128]{2,1,0:T(1,128)S(1)}, u32[]{:S(2)}, u32[]{:S(2)}) async-start(f32[16,1,128]{2,1,0:T(1,128)} %bitcast.3), calls=%async_computation | async-start | bytes 16384 | tf_op jit(solution)/shard_map/all_to_all | solution.py:708
  16.2 1.4 %collective-permute-start.2 = (f32[36,8,128]{2,1,0:T(8,128)S(1)}, f32[36,8,128]{2,1,0:T(8,128)S(1)}, u32[]{:S(2)}, u32[]{:S(2)}) collective-permute-start(f32[36,8,128]{2,1,0:T(8,128)S(1)} %get-tuple-element.43), channel_id=1, source_target_pairs={{0,64},{64,128},{128,192},{192,0},{1,65},{65,129},{129,193},{193,1... | collective-permute-start | bytes 442376 | tf_op jit(solution)/shard_map/ppermute | solution.py:683
  17.6 1.3 %collective-permute-start.3 = (f32[39,8,128]{2,1,0:T(8,128)S(1)}, f32[39,8,128]{2,1,0:T(8,128)S(1)}, u32[]{:S(2)}, u32[]{:S(2)}) collective-permute-start(f32[39,8,128]{2,1,0:T(8,128)S(1)} %get-tuple-element.44), channel_id=1, source_target_pairs={{0,192},{64,0},{128,64},{192,128},{1,193},{65,1},{129,65},{193,129... | collective-permute-start | bytes 479240 | tf_op jit(solution)/shard_map/ppermute | solution.py:683
  18.9 3.0 %all-to-all-done = f32[16,1,128]{2,1,0:T(1,128)S(1)} async-done(((f32[16,1,128]{2,1,0:T(1,128)}), f32[16,1,128]{2,1,0:T(1,128)S(1)}, u32[]{:S(2)}, u32[]{:S(2)}) %all-to-all-start) | async-done | bytes 8224 | tf_op jit(solution)/shard_map/all_to_all | solution.py:708
  22.6 8.2 %all-to-all-start.1 = ((f32[16,1,128]{2,1,0:T(1,128)}), f32[16,1,128]{2,1,0:T(1,128)S(1)}, u32[]{:S(2)}, u32[]{:S(2)}) async-start(f32[16,1,128]{2,1,0:T(1,128)} %bitcast.6), calls=%async_computation.1 | async-start | bytes 16384 | tf_op jit(solution)/shard_map/all_to_all | solution.py:710
  31.4 3.3 %collective-permute-start.4 = (f32[45,8,128]{2,1,0:T(8,128)S(1)}, f32[45,8,128]{2,1,0:T(8,128)S(1)}, u32[]{:S(2)}, u32[]{:S(2)}) collective-permute-start(f32[45,8,128]{2,1,0:T(8,128)S(1)} %get-tuple-element.51), channel_id=1, source_target_pairs={{0,8},{8,16},{16,24},{24,32},{32,40},{40,48},{48,56},{56,0},{1,9},... | collective-permute-start | bytes 552968 | tf_op jit(solution)/shard_map/ppermute | solution.py:683
  35.5 3.2 %collective-permute-done.4.from_down = f32[45,8,128]{2,1,0:T(8,128)S(1)} collective-permute-done((f32[45,8,128]{2,1,0:T(8,128)S(1)}, f32[45,8,128]{2,1,0:T(8,128)S(1)}, u32[]{:S(2)}, u32[]{:S(2)}) %collective-permute-start.4) | collective-permute-done | bytes 184352 | tf_op jit(solution)/shard_map/ppermute | solution.py:683
  38.6 3.2 %collective-permute-done.5.from_up = f32[55,8,128]{2,1,0:T(8,128)S(1)} collective-permute-done((f32[55,8,128]{2,1,0:T(8,128)S(1)}, f32[55,8,128]{2,1,0:T(8,128)S(1)}, u32[]{:S(2)}, u32[]{:S(2)}) %collective-permute-start.5) | collective-permute-done | bytes 225312 | tf_op jit(solution)/shard_map/ppermute | solution.py:683
  41.9 1.4 %velocity.1 = (f32[3,4,4,256]{3,2,1,0:T(4,128)}, f32[5,27,8,128]{3,2,1,0:T(8,128)S(1)}, f32[3,27,8,128]{3,2,1,0:T(8,128)S(1)}, f32[5,9,8,128]{3,2,1,0:T(8,128)S(1)}, f32[2,5,9,8,128]{4,3,2,1,0:T(8,128)S(1)}) custom-call(f32[8,128]{1,0:T(8,128)S(1)} %step.1.scale, f32[4,9,2,8,128]{4,3,2,1,0:T(8,128)S(1)} %get-tuple-element.45.sums, ...), custom_call_target="tpu_custom_call" | custom-call | tf_op jit(solution)/shard_map/velocity/pallas_call | solution.py:665
  43.3 1.2 %stage_one.1 = (f32[5,27,8,128]{3,2,1,0:T(8,128)S(1)}, f32[5,5,8,128]{3,2,1,0:T(8,128)S(1)}, f32[5,5,8,128]{3,2,1,0:T(8,128)S(1)}, f32[5,5,8,128]{3,2,1,0:T(8,128)S(1)}, f32[5,5,8,128]{3,2,1,0:T(8,128)S(1)}) custom-call(f32[5,27,8,128]{3,2,1,0:T(8,128)S(1)} %get-tuple-element.54.refs_0_, f32[3,27,8,128]{3,2,1,0:T(8,128)S(1)} %get-tuple-element.55.refs_1_.refs_2_, ...), custom_call_target="tpu_custom_call" | custom-call | tf_op jit(solution)/shard_map/stage_one/pallas_call | solution.py:665
  44.9 2.4 %collective-permute-start.7 = (f32[5,5,8,128]{3,2,1,0:T(8,128)S(1)}, f32[5,5,8,128]{3,2,1,0:T(8,128)S(1)}, u32[]{:S(2)}, u32[]{:S(2)}) collective-permute-start(f32[5,5,8,128]{3,2,1,0:T(8,128)S(1)} %get-tuple-element.60), channel_id=1, source_target_pairs={{0,192},{64,0},{128,64},{192,128},{1,193},{65,1},{129,65},{193,129... | collective-permute-start | bytes 307208 | tf_op jit(solution)/shard_map/ppermute | solution.py:683
  47.2 1.6 %collective-permute-start.8 = (f32[5,5,8,128]{3,2,1,0:T(8,128)S(1)}, f32[5,5,8,128]{3,2,1,0:T(8,128)S(1)}, u32[]{:S(2)}, u32[]{:S(2)}) collective-permute-start(f32[5,5,8,128]{3,2,1,0:T(8,128)S(1)} %get-tuple-element.61), channel_id=1, source_target_pairs={{0,8},{8,16},{16,24},{24,32},{32,40},{40,48},{48,56},{56,0},{1,9},... | collective-permute-start | bytes 307208 | tf_op jit(solution)/shard_map/ppermute | solution.py:683
  49.3 1.3 %collective-permute-done.8.refs_6_ = f32[5,5,8,128]{3,2,1,0:T(8,128)S(1)} collective-permute-done((f32[5,5,8,128]{3,2,1,0:T(8,128)S(1)}, f32[5,5,8,128]{3,2,1,0:T(8,128)S(1)}, u32[]{:S(2)}, u32[]{:S(2)}) %collective-permute-start.8) | collective-permute-done | bytes 102432 | tf_op jit(solution)/shard_map/ppermute | solution.py:683
  50.6 4.1 %collective-permute-done.9.refs_7_ = f32[5,5,8,128]{3,2,1,0:T(8,128)S(1)} collective-permute-done((f32[5,5,8,128]{3,2,1,0:T(8,128)S(1)}, f32[5,5,8,128]{3,2,1,0:T(8,128)S(1)}, u32[]{:S(2)}, u32[]{:S(2)}) %collective-permute-start.9) | collective-permute-done | bytes 102432 | tf_op jit(solution)/shard_map/ppermute | solution.py:683
  54.7 1.2 %stage_two.1 = (f32[5,27,8,128]{3,2,1,0:T(8,128)S(1)}, f32[5,5,8,128]{3,2,1,0:T(8,128)S(1)}, f32[5,5,8,128]{3,2,1,0:T(8,128)S(1)}, f32[5,5,8,128]{3,2,1,0:T(8,128)S(1)}, f32[5,5,8,128]{3,2,1,0:T(8,128)S(1)}) custom-call(f32[5,27,8,128]{3,2,1,0:T(8,128)S(1)} %get-tuple-element.54.refs_0_, f32[5,27,8,128]{3,2,1,0:T(8,128)S(1)} %get-tuple-element.58.refs_1_, ...), custom_call_target="tpu_custom_call" | custom-call | tf_op jit(solution)/shard_map/stage_two/pallas_call | solution.py:665
  56.0 2.7 %collective-permute-start.11 = (f32[5,5,8,128]{3,2,1,0:T(8,128)S(1)}, f32[5,5,8,128]{3,2,1,0:T(8,128)S(1)}, u32[]{:S(2)}, u32[]{:S(2)}) collective-permute-start(f32[5,5,8,128]{3,2,1,0:T(8,128)S(1)} %get-tuple-element.65), channel_id=1, source_target_pairs={{0,192},{64,0},{128,64},{192,128},{1,193},{65,1},{129,65},{193,129... | collective-permute-start | bytes 307208 | tf_op jit(solution)/shard_map/ppermute | solution.py:683
  59.5 1.3 %collective-permute-done.10.refs_4_ = f32[5,5,8,128]{3,2,1,0:T(8,128)S(1)} collective-permute-done((f32[5,5,8,128]{3,2,1,0:T(8,128)S(1)}, f32[5,5,8,128]{3,2,1,0:T(8,128)S(1)}, u32[]{:S(2)}, u32[]{:S(2)}) %collective-permute-start.10) | collective-permute-done | bytes 102432 | tf_op jit(solution)/shard_map/ppermute | solution.py:683
  60.8 1.4 %collective-permute-done.12.refs_6_ = f32[5,5,8,128]{3,2,1,0:T(8,128)S(1)} collective-permute-done((f32[5,5,8,128]{3,2,1,0:T(8,128)S(1)}, f32[5,5,8,128]{3,2,1,0:T(8,128)S(1)}, u32[]{:S(2)}, u32[]{:S(2)}) %collective-permute-start.12) | collective-permute-done | bytes 102432 | tf_op jit(solution)/shard_map/ppermute | solution.py:683
  62.2 3.2 %collective-permute-done.13.refs_7_ = f32[5,5,8,128]{3,2,1,0:T(8,128)S(1)} collective-permute-done((f32[5,5,8,128]{3,2,1,0:T(8,128)S(1)}, f32[5,5,8,128]{3,2,1,0:T(8,128)S(1)}, u32[]{:S(2)}, u32[]{:S(2)}) %collective-permute-start.13) | collective-permute-done | bytes 102432 | tf_op jit(solution)/shard_map/ppermute | solution.py:683
  65.3 1.8 %stage_three.1 = f32[5,27,2,2,128]{4,3,2,1,0:T(2,128)} custom-call(f32[5,27,8,128]{3,2,1,0:T(8,128)S(1)} %get-tuple-element.54.refs_0_, f32[5,27,8,128]{3,2,1,0:T(8,128)S(1)} %get-tuple-element.63.refs_1_, f32[3,27,8,128]{3,2,1,0:T(8,128)S(1)} %get-tuple-element.55.refs_1_.refs_2_, f32[5,9,8,128]{3,2,1,0:T(8,128)S(1)} %get-tuple-element.56.refs_2_.refs_3_, ...), custom_call_target="tpu_custom_call" | custom-call | tf_op jit(solution)/shard_map/stage_three/pallas_call | solution.py:665
  (23 shorter events, 5.8 us)
Async XLA Ops:
  0.6 0.8 %copy-start = (f32[3,3,3,2,2,128]{5,4,3,2,1,0:T(2,128)S(1)}, f32[3,3,3,2,2,128]{5,4,3,2,1,0:T(2,128)}, u32[]{:S(2)}) copy-start(f32[3,3,3,2,2,128]{5,4,3,2,1,0:T(2,128)} %param.3) | copy-start | bytes 165892
  1.4 0.8 %copy-start.1 = (f32[3,3,3,2,2,128]{5,4,3,2,1,0:T(2,128)S(1)}, f32[3,3,3,2,2,128]{5,4,3,2,1,0:T(2,128)}, u32[]{:S(2)}) copy-start(f32[3,3,3,2,2,128]{5,4,3,2,1,0:T(2,128)} %param.4) | copy-start | bytes 165892
  2.3 0.8 %copy-start.2 = (f32[3,4,4,256]{3,2,1,0:T(4,128)S(1)}, f32[3,4,4,256]{3,2,1,0:T(4,128)}, u32[]{:S(2)}) copy-start(f32[3,4,4,256]{3,2,1,0:T(4,128)} %vel.1) | copy-start | bytes 147460
  3.9 11.8 %collective-permute-start = (f32[3,8,128]{2,1,0:T(8,128)S(1)}, f32[3,8,128]{2,1,0:T(8,128)S(1)}, u32[]{:S(2)}, u32[]{:S(2)}) collective-permute-start(f32[3,8,128]{2,1,0:T(8,128)S(1)} %get-tuple-element.38), channel_id=1, source_target_pairs={{0,1},{1,2},{2,3},{3,4},{4,5},{5,6},{6,7},{7,0},{8,9},{9,10},{10,1... | collective-permute-start | bytes 36872 | tf_op jit(solution)/shard_map/ppermute | solution.py:683
  5.1 10.6 %collective-permute-start.1 = (f32[3,8,128]{2,1,0:T(8,128)S(1)}, f32[3,8,128]{2,1,0:T(8,128)S(1)}, u32[]{:S(2)}, u32[]{:S(2)}) collective-permute-start(f32[3,8,128]{2,1,0:T(8,128)S(1)} %get-tuple-element.39), channel_id=1, source_target_pairs={{0,7},{1,0},{2,1},{3,2},{4,3},{5,4},{6,5},{7,6},{8,15},{9,8},{10,9... | collective-permute-start | bytes 36872 | tf_op jit(solution)/shard_map/ppermute | solution.py:683
  11.3 10.6 %all-to-all-start = ((f32[16,1,128]{2,1,0:T(1,128)}), f32[16,1,128]{2,1,0:T(1,128)S(1)}, u32[]{:S(2)}, u32[]{:S(2)}) async-start(f32[16,1,128]{2,1,0:T(1,128)} %bitcast.3), calls=%async_computation | async-start | bytes 16384 | tf_op jit(solution)/shard_map/all_to_all | solution.py:708
  16.2 14.5 %collective-permute-start.2 = (f32[36,8,128]{2,1,0:T(8,128)S(1)}, f32[36,8,128]{2,1,0:T(8,128)S(1)}, u32[]{:S(2)}, u32[]{:S(2)}) collective-permute-start(f32[36,8,128]{2,1,0:T(8,128)S(1)} %get-tuple-element.43), channel_id=1, source_target_pairs={{0,64},{64,128},{128,192},{192,0},{1,65},{65,129},{129,193},{193,1... | collective-permute-start | bytes 442376 | tf_op jit(solution)/shard_map/ppermute | solution.py:683
  17.6 13.1 %collective-permute-start.3 = (f32[39,8,128]{2,1,0:T(8,128)S(1)}, f32[39,8,128]{2,1,0:T(8,128)S(1)}, u32[]{:S(2)}, u32[]{:S(2)}) collective-permute-start(f32[39,8,128]{2,1,0:T(8,128)S(1)} %get-tuple-element.44), channel_id=1, source_target_pairs={{0,192},{64,0},{128,64},{192,128},{1,193},{65,1},{129,65},{193,129... | collective-permute-start | bytes 479240 | tf_op jit(solution)/shard_map/ppermute | solution.py:683
  22.6 12.9 %all-to-all-start.1 = ((f32[16,1,128]{2,1,0:T(1,128)}), f32[16,1,128]{2,1,0:T(1,128)S(1)}, u32[]{:S(2)}, u32[]{:S(2)}) async-start(f32[16,1,128]{2,1,0:T(1,128)} %bitcast.6), calls=%async_computation.1 | async-start | bytes 16384 | tf_op jit(solution)/shard_map/all_to_all | solution.py:710
  31.4 7.3 %collective-permute-start.4 = (f32[45,8,128]{2,1,0:T(8,128)S(1)}, f32[45,8,128]{2,1,0:T(8,128)S(1)}, u32[]{:S(2)}, u32[]{:S(2)}) collective-permute-start(f32[45,8,128]{2,1,0:T(8,128)S(1)} %get-tuple-element.51), channel_id=1, source_target_pairs={{0,8},{8,16},{16,24},{24,32},{32,40},{40,48},{48,56},{56,0},{1,9},... | collective-permute-start | bytes 552968 | tf_op jit(solution)/shard_map/ppermute | solution.py:683
  34.7 7.2 %collective-permute-start.5 = (f32[55,8,128]{2,1,0:T(8,128)S(1)}, f32[55,8,128]{2,1,0:T(8,128)S(1)}, u32[]{:S(2)}, u32[]{:S(2)}) collective-permute-start(f32[55,8,128]{2,1,0:T(8,128)S(1)} %get-tuple-element.52), channel_id=1, source_target_pairs={{0,56},{8,0},{16,8},{24,16},{32,24},{40,32},{48,40},{56,48},{1,57}... | collective-permute-start | bytes 675848 | tf_op jit(solution)/shard_map/ppermute | solution.py:683
  44.5 4.8 %collective-permute-start.6 = (f32[5,5,8,128]{3,2,1,0:T(8,128)S(1)}, f32[5,5,8,128]{3,2,1,0:T(8,128)S(1)}, u32[]{:S(2)}, u32[]{:S(2)}) collective-permute-start(f32[5,5,8,128]{3,2,1,0:T(8,128)S(1)} %get-tuple-element.59), channel_id=1, source_target_pairs={{0,64},{64,128},{128,192},{192,0},{1,65},{65,129},{129,193},{193,1... | collective-permute-start | bytes 307208 | tf_op jit(solution)/shard_map/ppermute | solution.py:683
  44.9 4.4 %collective-permute-start.7 = (f32[5,5,8,128]{3,2,1,0:T(8,128)S(1)}, f32[5,5,8,128]{3,2,1,0:T(8,128)S(1)}, u32[]{:S(2)}, u32[]{:S(2)}) collective-permute-start(f32[5,5,8,128]{3,2,1,0:T(8,128)S(1)} %get-tuple-element.60), channel_id=1, source_target_pairs={{0,192},{64,0},{128,64},{192,128},{1,193},{65,1},{129,65},{193,129... | collective-permute-start | bytes 307208 | tf_op jit(solution)/shard_map/ppermute | solution.py:683
  47.2 3.4 %collective-permute-start.8 = (f32[5,5,8,128]{3,2,1,0:T(8,128)S(1)}, f32[5,5,8,128]{3,2,1,0:T(8,128)S(1)}, u32[]{:S(2)}, u32[]{:S(2)}) collective-permute-start(f32[5,5,8,128]{3,2,1,0:T(8,128)S(1)} %get-tuple-element.61), channel_id=1, source_target_pairs={{0,8},{8,16},{16,24},{24,32},{32,40},{40,48},{48,56},{56,0},{1,9},... | collective-permute-start | bytes 307208 | tf_op jit(solution)/shard_map/ppermute | solution.py:683
  48.8 5.9 %collective-permute-start.9 = (f32[5,5,8,128]{3,2,1,0:T(8,128)S(1)}, f32[5,5,8,128]{3,2,1,0:T(8,128)S(1)}, u32[]{:S(2)}, u32[]{:S(2)}) collective-permute-start(f32[5,5,8,128]{3,2,1,0:T(8,128)S(1)} %get-tuple-element.62), channel_id=1, source_target_pairs={{0,56},{8,0},{16,8},{24,16},{32,24},{40,32},{48,40},{56,48},{1,57}... | collective-permute-start | bytes 307208 | tf_op jit(solution)/shard_map/ppermute | solution.py:683
  56.0 4.8 %collective-permute-start.10 = (f32[5,5,8,128]{3,2,1,0:T(8,128)S(1)}, f32[5,5,8,128]{3,2,1,0:T(8,128)S(1)}, u32[]{:S(2)}, u32[]{:S(2)}) collective-permute-start(f32[5,5,8,128]{3,2,1,0:T(8,128)S(1)} %get-tuple-element.64), channel_id=1, source_target_pairs={{0,64},{64,128},{128,192},{192,0},{1,65},{65,129},{129,193},{193,1... | collective-permute-start | bytes 307208 | tf_op jit(solution)/shard_map/ppermute | solution.py:683
  56.0 4.7 %collective-permute-start.11 = (f32[5,5,8,128]{3,2,1,0:T(8,128)S(1)}, f32[5,5,8,128]{3,2,1,0:T(8,128)S(1)}, u32[]{:S(2)}, u32[]{:S(2)}) collective-permute-start(f32[5,5,8,128]{3,2,1,0:T(8,128)S(1)} %get-tuple-element.65), channel_id=1, source_target_pairs={{0,192},{64,0},{128,64},{192,128},{1,193},{65,1},{129,65},{193,129... | collective-permute-start | bytes 307208 | tf_op jit(solution)/shard_map/ppermute | solution.py:683
  58.7 3.5 %collective-permute-start.12 = (f32[5,5,8,128]{3,2,1,0:T(8,128)S(1)}, f32[5,5,8,128]{3,2,1,0:T(8,128)S(1)}, u32[]{:S(2)}, u32[]{:S(2)}) collective-permute-start(f32[5,5,8,128]{3,2,1,0:T(8,128)S(1)} %get-tuple-element.66), channel_id=1, source_target_pairs={{0,8},{8,16},{16,24},{24,32},{32,40},{40,48},{48,56},{56,0},{1,9},... | collective-permute-start | bytes 307208 | tf_op jit(solution)/shard_map/ppermute | solution.py:683
  59.5 5.9 %collective-permute-start.13 = (f32[5,5,8,128]{3,2,1,0:T(8,128)S(1)}, f32[5,5,8,128]{3,2,1,0:T(8,128)S(1)}, u32[]{:S(2)}, u32[]{:S(2)}) collective-permute-start(f32[5,5,8,128]{3,2,1,0:T(8,128)S(1)} %get-tuple-element.67), channel_id=1, source_target_pairs={{0,56},{8,0},{16,8},{24,16},{32,24},{40,32},{48,40},{56,48},{1,57}... | collective-permute-start | bytes 307208 | tf_op jit(solution)/shard_map/ppermute | solution.py:683

commit v2 on v1

--- a/solution.py
+++ b/solution.py
@@ -18,6 +18,7 @@
 GZ = ("zh", "xx")
 FLAT = ("gx", "xx")
 DEEP = ("zl", "co", "zh")
+FIRST, SECOND = FLAT, DEEP
 WEIGHT = pl.CostEstimate(flops=10**11, bytes_accessed=10**8, transcendentals=0)
 GROUP = 14
 
@@ -69,6 +70,10 @@
 TAB = tables()
 
 
+def even_along(axes):
+    return lax.rem(lax.axis_index(axes[-1]), 2) == 0
+
+
 def row_index():
     return lax.broadcasted_iota(jnp.int32, TILE, 0)
 
@@ -150,19 +155,18 @@
     return result
 
 
-def message_size(halves):
-    tiles = -(-halves // 2)
+def message_size(*keys):
+    tiles = -(-max(len(k) for k in keys) // 2)
     return -(-tiles // 2) + -(-tiles // 32)
 
 
-def write_message(sh, ref, values, high, step):
+def packed_tiles(sh, values, high, step):
     values = list(values)
     if len(values) % 2:
         values.append(None)
     pack = sh.pack_high if high else sh.pack_low
     tiles = [pack(values[n], values[n + 1], step) for n in range(0, len(values), 2)]
     group = lane_index() // 8
-    base = -(-len(tiles) // 2)
     halos = []
     for n, tile in enumerate(tiles):
         moved = roll_lanes(tile, 8 * (n % 16) + 4)
@@ -174,30 +178,50 @@
         tiles.append(tiles[-1])
     if len(halos) % 2:
         halos.append(halos[-1])
-    for n in range(0, len(tiles), 2):
-        ref[n // 2] = jnp.where(sh.own, tiles[n], roll_rows(tiles[n + 1], 4))
-    for n in range(0, len(halos), 2):
-        ref[base + n // 2] = jnp.where(sh.own, roll_rows(halos[n], 4), halos[n + 1])
-
-
-def read_message(sh, ref, keys, high, step):
-    places = {key: n for n, key in enumerate(keys)}
-    base = -(-(-(-len(keys) // 2)) // 2)
-
-    def get(key):
-        n, odd = divmod(places[key], 2)
-        main = ref[n // 2]
-        if n % 2:
-            main = roll_rows(main, 4)
-        halo = ref[base + n // 32]
-        if n // 16 % 2 == 0:
-            halo = roll_rows(halo, 4)
-        tile = jnp.where(sh.own, main, roll_lanes(halo, 124 - 8 * (n % 16)))
-        if odd:
-            tile = roll_rows(tile, step if high else -step)
-        return tile
-
-    return get
+    return [
+        jnp.where(sh.own, tiles[n], roll_rows(tiles[n + 1], 4)) for n in range(0, len(tiles), 2)
+    ] + [jnp.where(sh.own, roll_rows(halos[n], 4), halos[n + 1]) for n in range(0, len(halos), 2)]
+
+
+def write_messages(sh, even, near, far, over, under, step):
+    over = packed_tiles(sh, over, True, step)
+    under = packed_tiles(sh, under, False, step)
+    for n in range(max(len(over), len(under))):
+        up = over[min(n, len(over) - 1)]
+        down = under[min(n, len(under) - 1)]
+        near[n] = jnp.where(even, up, down)
+        far[n] = jnp.where(even, down, up)
+
+
+def read_messages(sh, even, near, far, over_keys, under_keys, step):
+    def reader(first, second, keys, high):
+        places = {key: n for n, key in enumerate(keys)}
+        base = -(-(-(-len(keys) // 2)) // 2)
+        packed = {}
+        tiles = {}
+
+        def load(k):
+            if k not in packed:
+                packed[k] = jnp.where(even, first[k], second[k])
+            return packed[k]
+
+        def get(key):
+            n, odd = divmod(places[key], 2)
+            if n not in tiles:
+                main = load(n // 2)
+                if n % 2:
+                    main = roll_rows(main, 4)
+                halo = load(base + n // 32)
+                if n // 16 % 2 == 0:
+                    halo = roll_rows(halo, 4)
+                tiles[n] = jnp.where(sh.own, main, roll_lanes(halo, 124 - 8 * (n % 16)))
+            if odd:
+                return roll_rows(tiles[n], step if high else -step)
+            return tiles[n]
+
+        return get
+
+    return reader(far, near, over_keys, True), reader(near, far, under_keys, False)
 
 
 FIELDS = range(4)
@@ -243,15 +267,20 @@
     return 9 * a + 3 * b + c
 
 
-def pack_kernel(dens, ener, vel, to_up, to_down, both, nodes, top, wide, split):
+def pack_kernel(
+    dens_far, ener_far, vel_far, near, far, both, nodes, top, dens, ener, vel, wide, split, sems
+):
     lane = lane_index()
-    low = ener[0, 0]
-    for q in range(27):
-        for i in range(2):
-            both[q, 2 * i : 2 * i + 2, :] = dens[q, i]
-            both[q, 4 + 2 * i : 6 + 2 * i, :] = ener[q, i]
-            low = jnp.maximum(low, ener[q, i])
-    top[...] = jnp.broadcast_to(jnp.max(low, keepdims=True), top.shape)
+    even = even_along(GZ)
+    copies = [
+        pltpu.make_async_copy(source, target, sems.at[n])
+        for n, (source, target) in enumerate(
+            ((vel_far, vel), (ener_far, ener), (dens_far, dens))
+        )
+    ]
+    for copy in copies:
+        copy.start()
+    copies[0].wait()
     half = (2 * lane) % 128
     for d in range(3):
         for px in range(2):
@@ -269,6 +298,15 @@
                 split[slot, 8 * pz : 8 * pz + 8, :] = picked
             for py in range(2):
                 nodes[2 * slot + py] = split[slot, pl.ds(py, 8, stride=2), :]
+    copies[1].wait()
+    copies[2].wait()
+    low = ener[0, 0]
+    for q in range(27):
+        for i in range(2):
+            both[q, 2 * i : 2 * i + 2, :] = dens[q, i]
+            both[q, 4 + 2 * i : 6 + 2 * i, :] = ener[q, i]
+            low = jnp.maximum(low, ener[q, i])
+    top[...] = jnp.broadcast_to(jnp.max(low, keepdims=True), top.shape)
     sources = [[both[q] for q in range(GROUP)], [both[q] for q in range(GROUP, 27)]]
     sources.append([nodes[n] for n in range(12)])
     for t in range(3):
@@ -278,8 +316,8 @@
             group = lane // 4
             up = jnp.where(group == 2 * g, roll_lanes(tile, 8 * g - 124), up)
             down = jnp.where(group == 2 * g + 1, roll_lanes(tile, 8 * g + 4), down)
-        to_up[t] = up
-        to_down[t] = down
+        near[t] = jnp.where(even, up, down)
+        far[t] = jnp.where(even, down, up)
 
 
 def top_kernel(tops, spread):
@@ -291,10 +329,10 @@
     step[...] = CFL / jnp.sqrt((GAMMA * (GAMMA - 1.0)) * top)
 
 
-def force_kernel(both, nodes, from_below, from_above, rho, vz, parts, to_right, to_left):
+def force_kernel(both, nodes, from_near, from_far, rho, vz, parts, near, far):
     sh = Shifts()
-    lane = lane_index()
-    merged = [jnp.where((lane & 7) < 4, from_below[t], from_above[t]) for t in range(3)]
+    below = ((lane_index() & 7) < 4) ^ (~even_along(GZ))
+    merged = [jnp.where(below, from_far[t], from_near[t]) for t in range(3)]
 
     def extend(tile, t, g):
         halo = roll_lanes(merged[t], 124 - 8 * g)
@@ -333,7 +371,8 @@
             for b in TRIPLE:
                 parts[f, 3 * a + b, 0] = fields[f][a, b, 0] + sh.z_prev(fields[f][a, b, 2])
                 parts[f, 3 * a + b, 1] = fields[f][a, b, 1]
-    for high, ref, trace in ((True, to_right, "high_trace"), (False, to_left, "low_trace")):
+    lists = []
+    for high, trace in ((True, "high_trace"), (False, "low_trace")):
         values = side_values(rho, 0, TAB[trace])
         for f in FIELDS:
             for b in TRIPLE:
@@ -352,7 +391,8 @@
                     values["old", d, 0, p, z] = first
                     values["old", d, 1, p, z] = vz[4 * d + 2 + p, z]
                     values["old", d, 2, p, z] = roll_rows(first, -2)
-        write_message(sh, ref, [values[key] for key in x_keys(high)], high, 2)
+        lists.append([values[key] for key in x_keys(high)])
+    write_messages(sh, even_along(GX), near, far, *lists, 2)
 
 
 def assemble(sh, own, side, step):
@@ -366,12 +406,13 @@
 
 
 def rim_kernel(
-    parts, vz, rho, from_left, from_right,
-    sums, sums_x, old, old_x, rho_x, heat_x, to_up, to_down,
+    parts, vz, rho, from_near, from_far,
+    sums, sums_x, old, old_x, rho_x, heat_x, near, far,
 ):
     sh = Shifts()
-    left = read_message(sh, from_left, x_keys(True), True, 2)
-    right = read_message(sh, from_right, x_keys(False), False, 2)
+    left, right = read_messages(
+        sh, even_along(GX), from_near, from_far, x_keys(True), x_keys(False), 2
+    )
 
     def beside(*key):
         return sh.beside(right(key), left(key), 2)
@@ -401,7 +442,8 @@
     for m in TRIPLE:
         for n in TRIPLE:
             heat_x[3 * m + n] = beside("heat", m, n)
-    for high, ref, trace in ((True, to_up, "high_trace"), (False, to_down, "low_trace")):
+    lists = []
+    for high, trace in ((True, "high_trace"), (False, "low_trace")):
         values = side_values(rho, 1, TAB[trace])
         for f in FIELDS:
             for a in TRIPLE:
@@ -422,39 +464,23 @@
                     values["old", d, a, 1, z] = old[d, 2 * a + 1, z]
                     values["old", d, a, 2, z] = roll_rows(first, -1)
                     values["old_side", d, a, z] = old_x[d, 2 * a, z]
-        write_message(sh, ref, [values[key] for key in y_keys(high)], high, 1)
-
-
-def face_messages(sh, fields, f, right, left, up, down):
-    low = TAB["low_trace"]
-    high = TAB["high_trace"]
-    for step, over, under in ((2, right, left), (1, up, down)):
-        lows = []
-        highs = []
-        for m in range(3):
-            for c in range(3):
-                if step == 2:
-                    line = [fields[a, m, c] for a in range(3)]
-                else:
-                    line = [fields[m, b, c] for b in range(3)]
-                lows.append(combine(line, low))
-                highs.append(combine(line, high))
-        lows.append(None)
-        highs.append(None)
-        for n in range(5):
-            over[f, n] = sh.pack_high(highs[2 * n], highs[2 * n + 1], step)
-            under[f, n] = sh.pack_low(lows[2 * n], lows[2 * n + 1], step)
+        lists.append([values[key] for key in y_keys(high)])
+    write_messages(sh, even_along(GY), near, far, *lists, 1)
+
+
+FACE_KEYS = [(f, m) for f in range(5) for m in range(9)]
 
 
 def velocity_kernel(
-    scale, sums, sums_x, old, old_x, rho, rho_x, heat_x, from_down, from_up,
+    scale, sums, sums_x, old, old_x, rho, rho_x, heat_x, from_near, from_far,
     new_vel, u0, disp, speeds, sides, split, wide,
 ):
     sh = Shifts()
     lane = lane_index()
     step = scale[...]
-    down = read_message(sh, from_down, y_keys(True), True, 1)
-    up = read_message(sh, from_up, y_keys(False), False, 1)
+    down, up = read_messages(
+        sh, even_along(GY), from_near, from_far, y_keys(True), y_keys(False), 1
+    )
 
     def beside(*key):
         return sh.beside(up(key), down(key), 1)
@@ -588,13 +614,21 @@
     u0 = refs.pop(0)
     u = u0 if weight is None else refs.pop(0)
     disp, speeds = refs[:2]
+    sh = Shifts()
+    even = [even_along(GX), even_along(GY)]
     if weight is None:
-        (sides,) = refs[2:3]
+        sides = refs[2]
         outs = refs[3:]
     else:
-        from_left, from_right, from_down, from_up = refs[2:6]
         outs = refs[6:]
-    sh = Shifts()
+        sides = outs.pop()
+        for d in range(2):
+            step = 2 - d
+            near, far = refs[2 + 2 * d : 4 + 2 * d]
+            under, over = read_messages(sh, even[d], near, far, FACE_KEYS, FACE_KEYS, step)
+            for f, m in FACE_KEYS:
+                sides[d, f, m] = sh.beside(over((f, m)), under((f, m)), step)
+    traces = None if last else outs.pop()
     low = TAB["low_trace"]
     high = TAB["high_trace"]
     low_lift = TAB["low_lift"]
@@ -620,13 +654,8 @@
                     tp = combine(line, high)
                     if d < 2:
                         step = 2 - d
-                        if weight is None:
-                            before = sh.before(sides[d, f, at], tp, step)
-                            after = sh.before(tm, sides[d, f, at], step)
-                        else:
-                            under, over = ((from_left, from_right), (from_down, from_up))[d]
-                            before = sh.prev(tp, under[f, at // 2], at % 2, step)
-                            after = sh.next(tm, over[f, at // 2], at % 2, step)
+                        before = sh.before(sides[d, f, at], tp, step)
+                        after = sh.before(tm, sides[d, f, at], step)
                         s_low = speeds[2 * d, at]
                         s_high = speeds[2 * d + 1, at]
                         f_low = s_low * jnp.where(s_low > 0.0, before, tm)
@@ -655,19 +684,30 @@
                 outs[0][f, q] = value
                 after[key] = value
         if not last:
-            face_messages(sh, after, f, *outs[1:])
+            for d in range(2):
+                for m in range(3):
+                    for n in range(3):
+                        keys = [(a, m, n) if d == 0 else (m, a, n) for a in range(3)]
+                        line = [after[k] for k in keys]
+                        traces[2 * d, f, 3 * m + n] = combine(line, high)
+                        traces[2 * d + 1, f, 3 * m + n] = combine(line, low)
         return carry
 
     lax.fori_loop(0, 5, one_field, 0)
-
-
-def call(kernel, outs, *args, scratch=(), name=None, weigh=None):
+    if not last:
+        for d in range(2):
+            lists = [[traces[2 * d + k, f, m] for f, m in FACE_KEYS] for k in range(2)]
+            write_messages(sh, even[d], outs[1 + 2 * d], outs[2 + 2 * d], *lists, 2 - d)
+
+
+def call(kernel, outs, *args, scratch=(), name=None, weigh=None, far=False):
+    space = pltpu.HBM if far else pltpu.VMEM
     return pl.pallas_call(
         kernel,
         out_shape=[jax.ShapeDtypeStruct(o, F32) for o in outs],
-        in_specs=[pl.BlockSpec(memory_space=pltpu.VMEM)] * len(args),
+        in_specs=[pl.BlockSpec(memory_space=space) for _ in args],
         out_specs=[pl.BlockSpec(memory_space=pltpu.VMEM)] * len(outs),
-        scratch_shapes=[pltpu.VMEM(s, F32) for s in scratch],
+        scratch_shapes=[pltpu.VMEM(s, F32) if isinstance(s, tuple) else s for s in scratch],
         compiler_params=pltpu.CompilerParams(vmem_limit_bytes=32 * 1024 * 1024),
         cost_estimate=weigh,
         name=name,
@@ -678,85 +718,93 @@
     return math.prod(lax.axis_size(axis) for axis in axes)
 
 
-def send(value, axis, by):
+def near_swap(value, axis):
+    return lax.ppermute(value, axis, [(i, i ^ 1) for i in range(axis_count(axis))])
+
+
+def far_swap(value, axis):
     count = axis_count(axis)
-    return lax.ppermute(value, axis, [(i, (i + by) % count) for i in range(count)])
-
-
-def exchange(right, left, up, down):
-    return (
-        send(right, GX, 1),
-        send(left, GX, -1),
-        send(up, GY, 1),
-        send(down, GY, -1),
-    )
+    return lax.ppermute(value, axis, [(i, (i + 2 * (i % 2) - 1) % count) for i in range(count)])
+
+
+def exchange(near_x, far_x, near_y, far_y):
+    far_y = far_swap(far_y, GY)
+    far_x = far_swap(far_x, GX)
+    near_x = near_swap(near_x, GX)
+    near_y = near_swap(near_y, GY)
+    return near_x, far_x, near_y, far_y
 
 
 def shards(density, energy, velocity):
     tile = TILE
     dens = density.reshape((27,) + density.shape[3:])
     ener = energy.reshape((27,) + energy.shape[3:])
-    to_up, to_down, both, nodes, top = call(
+    near, far, both, nodes, top = call(
         pack_kernel,
-        [(3,) + tile, (3,) + tile, (27,) + tile, (12,) + tile, (axis_count(FLAT), 128)],
+        [(3,) + tile, (3,) + tile, (27,) + tile, (12,) + tile, (axis_count(FIRST), 128)],
         dens, ener, velocity,
-        scratch=[(6, 8, 256), (6, 16, 128)],
+        scratch=[
+            dens.shape, ener.shape, velocity.shape,
+            (6, 8, 256), (6, 16, 128), pltpu.SemaphoreType.DMA((3,)),
+        ],
+        far=True,
         name="pack",
     )
-    from_below = send(to_up, GZ, 1)
-    from_above = send(to_down, GZ, -1)
-    tops = lax.all_to_all(top, FLAT, 0, 0, tiled=True)
-    (top,) = call(top_kernel, [(axis_count(DEEP), 128)], tops, name="top", weigh=WEIGHT)
-    tops = lax.all_to_all(top, DEEP, 0, 0, tiled=True)
+    far = far_swap(far, GZ)
+    near = near_swap(near, GZ)
+    tops = lax.all_to_all(top, FIRST, 0, 0, tiled=True)
+    (top,) = call(top_kernel, [(axis_count(SECOND), 128)], tops, name="top", weigh=WEIGHT)
+    tops = lax.all_to_all(top, SECOND, 0, 0, tiled=True)
     (step,) = call(step_kernel, [tile], tops, name="step", weigh=WEIGHT)
     parts_shape = (4, 9, 2) + tile
     old_shape = (3, 6, 2) + tile
-    rho, vz, parts, to_right, to_left = call(
+    message = (message_size(x_keys(True), x_keys(False)),) + tile
+    rho, vz, parts, near, far = call(
         force_kernel,
-        [
-            (2, 27) + tile, (12, 2) + tile, parts_shape,
-            (message_size(len(x_keys(True))),) + tile,
-            (message_size(len(x_keys(False))),) + tile,
-        ],
-        both, nodes, from_below, from_above,
+        [(2, 27) + tile, (12, 2) + tile, parts_shape, message, message],
+        both, nodes, near, far,
         name="force",
     )
-    from_left = send(to_right, GX, 1)
-    from_right = send(to_left, GX, -1)
-    sums, sums_x, old, old_x, rho_x, heat_x, to_up, to_down = call(
+    far = far_swap(far, GX)
+    near = near_swap(near, GX)
+    message = (message_size(y_keys(True), y_keys(False)),) + tile
+    sums, sums_x, old, old_x, rho_x, heat_x, near, far = call(
         rim_kernel,
         [
             parts_shape, parts_shape, old_shape, old_shape, (27,) + tile, (9,) + tile,
-            (message_size(len(y_keys(True))),) + tile,
-            (message_size(len(y_keys(False))),) + tile,
+            message, message,
         ],
-        parts, vz, rho, from_left, from_right,
+        parts, vz, rho, near, far,
         name="rim",
     )
-    from_down = send(to_up, GY, 1)
-    from_up = send(to_down, GY, -1)
-    faces = [(5, 5) + tile] * 4
+    far = far_swap(far, GY)
+    near = near_swap(near, GY)
     state = (5, 27) + tile
     new_velocity, u0, disp, speeds, sides = call(
         velocity_kernel,
         [velocity.shape, state, (3, 27) + tile, (5, 9) + tile, (2, 5, 9) + tile],
-        step, sums, sums_x, old, old_x, rho, rho_x, heat_x, from_down, from_up,
+        step, sums, sums_x, old, old_x, rho, rho_x, heat_x, near, far,
         scratch=[(6, 16, 128), (6, 8, 256)],
         name="velocity",
     )
+    faces = [(message_size(FACE_KEYS),) + tile] * 4
+    held = (4, 5, 9) + tile
     one, *messages = call(
         functools.partial(stage_kernel, None, False), [state] + faces,
         u0, disp, speeds, sides,
+        scratch=[held],
         name="stage_one",
     )
     two, *messages = call(
         functools.partial(stage_kernel, 0.25, False), [state] + faces,
         u0, one, disp, speeds, *exchange(*messages),
+        scratch=[held, sides.shape],
         name="stage_two",
     )
     (remapped,) = call(
         functools.partial(stage_kernel, 2.0 / 3.0, True), [(5, 27) + density.shape[3:]],
         u0, two, disp, speeds, *exchange(*messages),
+        scratch=[sides.shape],
         name="stage_three",
     )
     return new_velocity, remapped.reshape((5, 3, 3, 3) + density.shape[3:])

time: 67.5 us -> 63 us (0.933)
  the two profiles are of different devices: /device:TPU:225 before, /device:TPU:1 now
where the time goes in v2:
time: 63 us; the launch traced here: 62.6 us
  starting transfers between devices  34.7 us (55%)
  waiting for transfers between devices  15.8 us (25%)
  Pallas kernels  9.06 us (14%)
  local copies, waits for them, and re-layouts  2.42 us (4%)
  between operations  0.74 us (1%)
    ppermute x7, starting transfers between devices, far_swap(): lax.ppermute(value, axis, [(i, (i + 2 * (i % 2) - 1) % count) for i in ra...  14.5 us
    ppermute x7, starting transfers between devices, near_swap(): lax.ppermute(value, axis, [(i, i ^ 1) for i in range(axis_count(axis))])  9.35 us
    pallas_call x9, Pallas kernels, call(): pl.pallas_call(kernel, out_shape=[jax.ShapeDtypeStruct(o, F32) for o in o...  9.06 us
    ppermute x7, waiting for transfers between devices, far_swap(): lax.ppermute(value, axis, [(i, (i + 2 * (i % 2) - 1) % count) for i in ra...  7.63 us
    all_to_all x1, starting transfers between devices, shards(): tops = lax.all_to_all(top, SECOND, 0, 0, tiled=True)  5.93 us
    all_to_all x1, starting transfers between devices, shards(): tops = lax.all_to_all(top, FIRST, 0, 0, tiled=True)  4.87 us
    all_to_all x1, waiting for transfers between devices, shards(): tops = lax.all_to_all(top, SECOND, 0, 0, tiled=True)  4.74 us
    all_to_all x1, waiting for transfers between devices, shards(): tops = lax.all_to_all(top, FIRST, 0, 0, tiled=True)  2.52 us
  transfers between devices with their start and end apart: 16, of which 7 were waited for; matrix products, arithmetic and copies ran while one was open for 0% of the time, Pallas kernels for 3%

profile of v2, /device:TPU:1, one launch (start us, length us, event | category | flops | bytes accessed | tf_op | source)
XLA Modules:
  0.0 62.6 jit_solution(15293463596488491073)
XLA Ops:
  1.4 0.8 %copy-done.1 = f32[3,3,3,2,2,128]{5,4,3,2,1,0:T(2,128)S(1)} copy-done((f32[3,3,3,2,2,128]{5,4,3,2,1,0:T(2,128)S(1)}, f32[3,3,3,2,2,128]{5,4,3,2,1,0:T(2,128)}, u32[]{:S(2)}) %copy-start.1) | copy-done | bytes 55320
  3.1 1.1 %pack.1 = (f32[3,8,128]{2,1,0:T(8,128)S(1)}, f32[3,8,128]{2,1,0:T(8,128)S(1)}, f32[27,8,128]{2,1,0:T(8,128)S(1)}, f32[12,8,128]{2,1,0:T(8,128)S(1)}, f32[16,128]{1,0:T(8,128)}) custom-call(f32[27,2,2,128]{3,2,1,0:T(2,128)S(1)} %bitcast.11, f32[27,2,2,128]{3,2,1,0:T(2,128)S(1)} %bitcast.12, f32[3,4,4,256]{3,2,1,0:T(4,128)S(1)} %copy-done.2), custom_call_target="tpu_custom_call" | custom-call | tf_op jit(solution)/shard_map/pack/pallas_call | solution.py:705
  4.2 2.1 %collective-permute-start = (f32[3,8,128]{2,1,0:T(8,128)S(1)}, f32[3,8,128]{2,1,0:T(8,128)S(1)}, u32[]{:S(2)}, u32[]{:S(2)}) collective-permute-start(f32[3,8,128]{2,1,0:T(8,128)S(1)} %get-tuple-element.38), channel_id=1, source_target_pairs={{0,1},{1,0},{2,3},{3,2},{4,5},{5,4},{6,7},{7,6},{8,9},{9,8},{10,11... | collective-permute-start | bytes 36872 | tf_op jit(solution)/shard_map/ppermute | solution.py:722
  6.3 8.4 %collective-permute-start.1 = (f32[3,8,128]{2,1,0:T(8,128)S(1)}, f32[3,8,128]{2,1,0:T(8,128)S(1)}, u32[]{:S(2)}, u32[]{:S(2)}) collective-permute-start(f32[3,8,128]{2,1,0:T(8,128)S(1)} %get-tuple-element.39), channel_id=1, source_target_pairs={{0,7},{1,2},{2,1},{3,4},{4,3},{5,6},{6,5},{7,0},{8,15},{9,10},{10,... | collective-permute-start | bytes 36872 | tf_op jit(solution)/shard_map/ppermute | solution.py:727
  14.7 4.9 %all-to-all-start = ((f32[16,1,128]{2,1,0:T(1,128)}), f32[16,1,128]{2,1,0:T(1,128)S(1)}, u32[]{:S(2)}, u32[]{:S(2)}) async-start(f32[16,1,128]{2,1,0:T(1,128)} %bitcast.3), calls=%async_computation | async-start | bytes 16384 | tf_op jit(solution)/shard_map/all_to_all | solution.py:755
  20.2 1.4 %collective-permute-start.2 = (f32[39,8,128]{2,1,0:T(8,128)S(1)}, f32[39,8,128]{2,1,0:T(8,128)S(1)}, u32[]{:S(2)}, u32[]{:S(2)}) collective-permute-start(f32[39,8,128]{2,1,0:T(8,128)S(1)} %get-tuple-element.43), channel_id=1, source_target_pairs={{0,64},{64,0},{128,192},{192,128},{1,65},{65,1},{129,193},{193,129... | collective-permute-start | bytes 479240 | tf_op jit(solution)/shard_map/ppermute | solution.py:722
  21.7 1.8 %collective-permute-start.3 = (f32[39,8,128]{2,1,0:T(8,128)S(1)}, f32[39,8,128]{2,1,0:T(8,128)S(1)}, u32[]{:S(2)}, u32[]{:S(2)}) collective-permute-start(f32[39,8,128]{2,1,0:T(8,128)S(1)} %get-tuple-element.44), channel_id=1, source_target_pairs={{0,192},{64,128},{128,64},{192,0},{1,193},{65,129},{129,65},{193,1... | collective-permute-start | bytes 479240 | tf_op jit(solution)/shard_map/ppermute | solution.py:727
  23.4 2.5 %all-to-all-done = f32[16,1,128]{2,1,0:T(1,128)S(1)} async-done(((f32[16,1,128]{2,1,0:T(1,128)}), f32[16,1,128]{2,1,0:T(1,128)S(1)}, u32[]{:S(2)}, u32[]{:S(2)}) %all-to-all-start) | async-done | bytes 8224 | tf_op jit(solution)/shard_map/all_to_all | solution.py:755
  26.6 5.9 %all-to-all-start.1 = ((f32[16,1,128]{2,1,0:T(1,128)}), f32[16,1,128]{2,1,0:T(1,128)S(1)}, u32[]{:S(2)}, u32[]{:S(2)}) async-start(f32[16,1,128]{2,1,0:T(1,128)} %bitcast.6), calls=%async_computation.1 | async-start | bytes 16384 | tf_op jit(solution)/shard_map/all_to_all | solution.py:757
  33.3 1.6 %collective-permute-start.5 = (f32[55,8,128]{2,1,0:T(8,128)S(1)}, f32[55,8,128]{2,1,0:T(8,128)S(1)}, u32[]{:S(2)}, u32[]{:S(2)}) collective-permute-start(f32[55,8,128]{2,1,0:T(8,128)S(1)} %get-tuple-element.52), channel_id=1, source_target_pairs={{0,56},{8,16},{16,8},{24,32},{32,24},{40,48},{48,40},{56,0},{1,57}... | collective-permute-start | bytes 675848 | tf_op jit(solution)/shard_map/ppermute | solution.py:727
  34.9 4.7 %all-to-all-done.1 = f32[16,1,128]{2,1,0:T(1,128)S(1)} async-done(((f32[16,1,128]{2,1,0:T(1,128)}), f32[16,1,128]{2,1,0:T(1,128)S(1)}, u32[]{:S(2)}, u32[]{:S(2)}) %all-to-all-start.1) | async-done | bytes 8224 | tf_op jit(solution)/shard_map/all_to_all | solution.py:757
  39.6 1.2 %collective-permute-done.5.from_far = f32[55,8,128]{2,1,0:T(8,128)S(1)} collective-permute-done((f32[55,8,128]{2,1,0:T(8,128)S(1)}, f32[55,8,128]{2,1,0:T(8,128)S(1)}, u32[]{:S(2)}, u32[]{:S(2)}) %collective-permute-start.5) | collective-permute-done | bytes 225312 | tf_op jit(solution)/shard_map/ppermute | solution.py:727
  40.8 1.5 %velocity.1 = (f32[3,4,4,256]{3,2,1,0:T(4,128)}, f32[5,27,8,128]{3,2,1,0:T(8,128)S(1)}, f32[3,27,8,128]{3,2,1,0:T(8,128)S(1)}, f32[5,9,8,128]{3,2,1,0:T(8,128)S(1)}, f32[2,5,9,8,128]{4,3,2,1,0:T(8,128)S(1)}) custom-call(f32[8,128]{1,0:T(8,128)S(1)} %step.1.scale, f32[4,9,2,8,128]{4,3,2,1,0:T(8,128)S(1)} %get-tuple-element.45.sums, ...), custom_call_target="tpu_custom_call" | custom-call | tf_op jit(solution)/shard_map/velocity/pallas_call | solution.py:705
  42.3 1.3 %stage_one.1 = (f32[5,27,8,128]{3,2,1,0:T(8,128)S(1)}, f32[13,8,128]{2,1,0:T(8,128)S(1)}, f32[13,8,128]{2,1,0:T(8,128)S(1)}, f32[13,8,128]{2,1,0:T(8,128)S(1)}, f32[13,8,128]{2,1,0:T(8,128)S(1)}) custom-call(f32[5,27,8,128]{3,2,1,0:T(8,128)S(1)} %get-tuple-element.54.refs_0_, f32[3,27,8,128]{3,2,1,0:T(8,128)S(1)} %get-tuple-element.55.refs_1_.refs_2_, ...), custom_call_target="tpu_custom_call" | custom-call | tf_op jit(solution)/shard_map/stage_one/pallas_call | solution.py:705
  43.9 0.9 %collective-permute-start.7 = (f32[13,8,128]{2,1,0:T(8,128)S(1)}, f32[13,8,128]{2,1,0:T(8,128)S(1)}, u32[]{:S(2)}, u32[]{:S(2)}) collective-permute-start(f32[13,8,128]{2,1,0:T(8,128)S(1)} %get-tuple-element.60), channel_id=1, source_target_pairs={{0,192},{64,128},{128,64},{192,0},{1,193},{65,129},{129,65},{193,1... | collective-permute-start | bytes 159752 | tf_op jit(solution)/shard_map/ppermute | solution.py:727
  44.8 2.3 %collective-permute-start.8 = (f32[13,8,128]{2,1,0:T(8,128)S(1)}, f32[13,8,128]{2,1,0:T(8,128)S(1)}, u32[]{:S(2)}, u32[]{:S(2)}) collective-permute-start(f32[13,8,128]{2,1,0:T(8,128)S(1)} %get-tuple-element.61), channel_id=1, source_target_pairs={{0,8},{8,0},{16,24},{24,16},{32,40},{40,32},{48,56},{56,48},{1,9},... | collective-permute-start | bytes 159752 | tf_op jit(solution)/shard_map/ppermute | solution.py:722
  47.1 1.0 %collective-permute-done.7.refs_5_ = f32[13,8,128]{2,1,0:T(8,128)S(1)} collective-permute-done((f32[13,8,128]{2,1,0:T(8,128)S(1)}, f32[13,8,128]{2,1,0:T(8,128)S(1)}, u32[]{:S(2)}, u32[]{:S(2)}) %collective-permute-start.7) | collective-permute-done | bytes 53280 | tf_op jit(solution)/shard_map/ppermute | solution.py:727
  48.1 2.8 %collective-permute-done.9.refs_7_ = f32[13,8,128]{2,1,0:T(8,128)S(1)} collective-permute-done((f32[13,8,128]{2,1,0:T(8,128)S(1)}, f32[13,8,128]{2,1,0:T(8,128)S(1)}, u32[]{:S(2)}, u32[]{:S(2)}) %collective-permute-start.9) | collective-permute-done | bytes 53280 | tf_op jit(solution)/shard_map/ppermute | solution.py:727
  50.9 1.5 %stage_two.1 = (f32[5,27,8,128]{3,2,1,0:T(8,128)S(1)}, f32[13,8,128]{2,1,0:T(8,128)S(1)}, f32[13,8,128]{2,1,0:T(8,128)S(1)}, f32[13,8,128]{2,1,0:T(8,128)S(1)}, f32[13,8,128]{2,1,0:T(8,128)S(1)}) custom-call(f32[5,27,8,128]{3,2,1,0:T(8,128)S(1)} %get-tuple-element.54.refs_0_, f32[5,27,8,128]{3,2,1,0:T(8,128)S(1)} %get-tuple-element.58.refs_1_, ...), custom_call_target="tpu_custom_call" | custom-call | tf_op jit(solution)/shard_map/stage_two/pallas_call | solution.py:705
  52.9 1.8 %collective-permute-start.11 = (f32[13,8,128]{2,1,0:T(8,128)S(1)}, f32[13,8,128]{2,1,0:T(8,128)S(1)}, u32[]{:S(2)}, u32[]{:S(2)}) collective-permute-start(f32[13,8,128]{2,1,0:T(8,128)S(1)} %get-tuple-element.65), channel_id=1, source_target_pairs={{0,192},{64,128},{128,64},{192,0},{1,193},{65,129},{129,65},{193,1... | collective-permute-start | bytes 159752 | tf_op jit(solution)/shard_map/ppermute | solution.py:727
  54.7 2.4 %collective-permute-start.12 = (f32[13,8,128]{2,1,0:T(8,128)S(1)}, f32[13,8,128]{2,1,0:T(8,128)S(1)}, u32[]{:S(2)}, u32[]{:S(2)}) collective-permute-start(f32[13,8,128]{2,1,0:T(8,128)S(1)} %get-tuple-element.66), channel_id=1, source_target_pairs={{0,8},{8,0},{16,24},{24,16},{32,40},{40,32},{48,56},{56,48},{1,9},... | collective-permute-start | bytes 159752 | tf_op jit(solution)/shard_map/ppermute | solution.py:722
  57.1 0.9 %collective-permute-done.12.refs_6_ = f32[13,8,128]{2,1,0:T(8,128)S(1)} collective-permute-done((f32[13,8,128]{2,1,0:T(8,128)S(1)}, f32[13,8,128]{2,1,0:T(8,128)S(1)}, u32[]{:S(2)}, u32[]{:S(2)}) %collective-permute-start.12) | collective-permute-done | bytes 53280 | tf_op jit(solution)/shard_map/ppermute | solution.py:722
  57.9 2.7 %collective-permute-done.13.refs_7_ = f32[13,8,128]{2,1,0:T(8,128)S(1)} collective-permute-done((f32[13,8,128]{2,1,0:T(8,128)S(1)}, f32[13,8,128]{2,1,0:T(8,128)S(1)}, u32[]{:S(2)}, u32[]{:S(2)}) %collective-permute-start.13) | collective-permute-done | bytes 53280 | tf_op jit(solution)/shard_map/ppermute | solution.py:727
  60.6 2.0 %stage_three.1 = f32[5,27,2,2,128]{4,3,2,1,0:T(2,128)} custom-call(f32[5,27,8,128]{3,2,1,0:T(8,128)S(1)} %get-tuple-element.54.refs_0_, f32[5,27,8,128]{3,2,1,0:T(8,128)S(1)} %get-tuple-element.63.refs_1_, f32[3,27,8,128]{3,2,1,0:T(8,128)S(1)} %get-tuple-element.55.refs_1_.refs_2_, f32[5,9,8,128]{3,2,1,0:T(8,128)S(1)} %get-tuple-element.56.refs_2_.refs_3_, ...), custom_call_target="tpu_custom_call" | custom-call | tf_op jit(solution)/shard_map/stage_three/pallas_call | solution.py:705
  (23 shorter events, 4.4 us)
Async XLA Ops:
  0.6 0.8 %copy-start = (f32[3,3,3,2,2,128]{5,4,3,2,1,0:T(2,128)S(1)}, f32[3,3,3,2,2,128]{5,4,3,2,1,0:T(2,128)}, u32[]{:S(2)}) copy-start(f32[3,3,3,2,2,128]{5,4,3,2,1,0:T(2,128)} %param.3) | copy-start | bytes 165892
  1.4 0.8 %copy-start.1 = (f32[3,3,3,2,2,128]{5,4,3,2,1,0:T(2,128)S(1)}, f32[3,3,3,2,2,128]{5,4,3,2,1,0:T(2,128)}, u32[]{:S(2)}) copy-start(f32[3,3,3,2,2,128]{5,4,3,2,1,0:T(2,128)} %param.4) | copy-start | bytes 165892
  2.3 0.8 %copy-start.2 = (f32[3,4,4,256]{3,2,1,0:T(4,128)S(1)}, f32[3,4,4,256]{3,2,1,0:T(4,128)}, u32[]{:S(2)}) copy-start(f32[3,4,4,256]{3,2,1,0:T(4,128)} %vel_far.1) | copy-start | bytes 147460
  4.2 15.5 %collective-permute-start = (f32[3,8,128]{2,1,0:T(8,128)S(1)}, f32[3,8,128]{2,1,0:T(8,128)S(1)}, u32[]{:S(2)}, u32[]{:S(2)}) collective-permute-start(f32[3,8,128]{2,1,0:T(8,128)S(1)} %get-tuple-element.38), channel_id=1, source_target_pairs={{0,1},{1,0},{2,3},{3,2},{4,5},{5,4},{6,7},{7,6},{8,9},{9,8},{10,11... | collective-permute-start | bytes 36872 | tf_op jit(solution)/shard_map/ppermute | solution.py:722
  6.3 13.3 %collective-permute-start.1 = (f32[3,8,128]{2,1,0:T(8,128)S(1)}, f32[3,8,128]{2,1,0:T(8,128)S(1)}, u32[]{:S(2)}, u32[]{:S(2)}) collective-permute-start(f32[3,8,128]{2,1,0:T(8,128)S(1)} %get-tuple-element.39), channel_id=1, source_target_pairs={{0,7},{1,2},{2,1},{3,4},{4,3},{5,6},{6,5},{7,0},{8,15},{9,10},{10,... | collective-permute-start | bytes 36872 | tf_op jit(solution)/shard_map/ppermute | solution.py:727
  14.7 11.2 %all-to-all-start = ((f32[16,1,128]{2,1,0:T(1,128)}), f32[16,1,128]{2,1,0:T(1,128)S(1)}, u32[]{:S(2)}, u32[]{:S(2)}) async-start(f32[16,1,128]{2,1,0:T(1,128)} %bitcast.3), calls=%async_computation | async-start | bytes 16384 | tf_op jit(solution)/shard_map/all_to_all | solution.py:755
  20.2 12.3 %collective-permute-start.2 = (f32[39,8,128]{2,1,0:T(8,128)S(1)}, f32[39,8,128]{2,1,0:T(8,128)S(1)}, u32[]{:S(2)}, u32[]{:S(2)}) collective-permute-start(f32[39,8,128]{2,1,0:T(8,128)S(1)} %get-tuple-element.43), channel_id=1, source_target_pairs={{0,64},{64,0},{128,192},{192,128},{1,65},{65,1},{129,193},{193,129... | collective-permute-start | bytes 479240 | tf_op jit(solution)/shard_map/ppermute | solution.py:722
  21.7 10.9 %collective-permute-start.3 = (f32[39,8,128]{2,1,0:T(8,128)S(1)}, f32[39,8,128]{2,1,0:T(8,128)S(1)}, u32[]{:S(2)}, u32[]{:S(2)}) collective-permute-start(f32[39,8,128]{2,1,0:T(8,128)S(1)} %get-tuple-element.44), channel_id=1, source_target_pairs={{0,192},{64,128},{128,64},{192,0},{1,193},{65,129},{129,65},{193,1... | collective-permute-start | bytes 479240 | tf_op jit(solution)/shard_map/ppermute | solution.py:727
  26.6 13.0 %all-to-all-start.1 = ((f32[16,1,128]{2,1,0:T(1,128)}), f32[16,1,128]{2,1,0:T(1,128)S(1)}, u32[]{:S(2)}, u32[]{:S(2)}) async-start(f32[16,1,128]{2,1,0:T(1,128)} %bitcast.6), calls=%async_computation.1 | async-start | bytes 16384 | tf_op jit(solution)/shard_map/all_to_all | solution.py:757
  33.0 6.6 %collective-permute-start.4 = (f32[55,8,128]{2,1,0:T(8,128)S(1)}, f32[55,8,128]{2,1,0:T(8,128)S(1)}, u32[]{:S(2)}, u32[]{:S(2)}) collective-permute-start(f32[55,8,128]{2,1,0:T(8,128)S(1)} %get-tuple-element.51), channel_id=1, source_target_pairs={{0,8},{8,0},{16,24},{24,16},{32,40},{40,32},{48,56},{56,48},{1,9},... | collective-permute-start | bytes 675848 | tf_op jit(solution)/shard_map/ppermute | solution.py:722
  33.3 7.5 %collective-permute-start.5 = (f32[55,8,128]{2,1,0:T(8,128)S(1)}, f32[55,8,128]{2,1,0:T(8,128)S(1)}, u32[]{:S(2)}, u32[]{:S(2)}) collective-permute-start(f32[55,8,128]{2,1,0:T(8,128)S(1)} %get-tuple-element.52), channel_id=1, source_target_pairs={{0,56},{8,16},{16,8},{24,32},{32,24},{40,48},{48,40},{56,0},{1,57}... | collective-permute-start | bytes 675848 | tf_op jit(solution)/shard_map/ppermute | solution.py:727
  43.6 3.6 %collective-permute-start.6 = (f32[13,8,128]{2,1,0:T(8,128)S(1)}, f32[13,8,128]{2,1,0:T(8,128)S(1)}, u32[]{:S(2)}, u32[]{:S(2)}) collective-permute-start(f32[13,8,128]{2,1,0:T(8,128)S(1)} %get-tuple-element.59), channel_id=1, source_target_pairs={{0,64},{64,0},{128,192},{192,128},{1,65},{65,1},{129,193},{193,129... | collective-permute-start | bytes 159752 | tf_op jit(solution)/shard_map/ppermute | solution.py:722
  43.9 4.2 %collective-permute-start.7 = (f32[13,8,128]{2,1,0:T(8,128)S(1)}, f32[13,8,128]{2,1,0:T(8,128)S(1)}, u32[]{:S(2)}, u32[]{:S(2)}) collective-permute-start(f32[13,8,128]{2,1,0:T(8,128)S(1)} %get-tuple-element.60), channel_id=1, source_target_pairs={{0,192},{64,128},{128,64},{192,0},{1,193},{65,129},{129,65},{193,1... | collective-permute-start | bytes 159752 | tf_op jit(solution)/shard_map/ppermute | solution.py:727
  44.8 3.3 %collective-permute-start.8 = (f32[13,8,128]{2,1,0:T(8,128)S(1)}, f32[13,8,128]{2,1,0:T(8,128)S(1)}, u32[]{:S(2)}, u32[]{:S(2)}) collective-permute-start(f32[13,8,128]{2,1,0:T(8,128)S(1)} %get-tuple-element.61), channel_id=1, source_target_pairs={{0,8},{8,0},{16,24},{24,16},{32,40},{40,32},{48,56},{56,48},{1,9},... | collective-permute-start | bytes 159752 | tf_op jit(solution)/shard_map/ppermute | solution.py:722
  47.1 3.8 %collective-permute-start.9 = (f32[13,8,128]{2,1,0:T(8,128)S(1)}, f32[13,8,128]{2,1,0:T(8,128)S(1)}, u32[]{:S(2)}, u32[]{:S(2)}) collective-permute-start(f32[13,8,128]{2,1,0:T(8,128)S(1)} %get-tuple-element.62), channel_id=1, source_target_pairs={{0,56},{8,16},{16,8},{24,32},{32,24},{40,48},{48,40},{56,0},{1,57}... | collective-permute-start | bytes 159752 | tf_op jit(solution)/shard_map/ppermute | solution.py:727
  52.5 4.6 %collective-permute-start.10 = (f32[13,8,128]{2,1,0:T(8,128)S(1)}, f32[13,8,128]{2,1,0:T(8,128)S(1)}, u32[]{:S(2)}, u32[]{:S(2)}) collective-permute-start(f32[13,8,128]{2,1,0:T(8,128)S(1)} %get-tuple-element.64), channel_id=1, source_target_pairs={{0,64},{64,0},{128,192},{192,128},{1,65},{65,1},{129,193},{193,129... | collective-permute-start | bytes 159752 | tf_op jit(solution)/shard_map/ppermute | solution.py:722
  52.9 4.2 %collective-permute-start.11 = (f32[13,8,128]{2,1,0:T(8,128)S(1)}, f32[13,8,128]{2,1,0:T(8,128)S(1)}, u32[]{:S(2)}, u32[]{:S(2)}) collective-permute-start(f32[13,8,128]{2,1,0:T(8,128)S(1)} %get-tuple-element.65), channel_id=1, source_target_pairs={{0,192},{64,128},{128,64},{192,0},{1,193},{65,129},{129,65},{193,1... | collective-permute-start | bytes 159752 | tf_op jit(solution)/shard_map/ppermute | solution.py:727
  54.7 3.2 %collective-permute-start.12 = (f32[13,8,128]{2,1,0:T(8,128)S(1)}, f32[13,8,128]{2,1,0:T(8,128)S(1)}, u32[]{:S(2)}, u32[]{:S(2)}) collective-permute-start(f32[13,8,128]{2,1,0:T(8,128)S(1)} %get-tuple-element.66), channel_id=1, source_target_pairs={{0,8},{8,0},{16,24},{24,16},{32,40},{40,32},{48,56},{56,48},{1,9},... | collective-permute-start | bytes 159752 | tf_op jit(solution)/shard_map/ppermute | solution.py:722
  57.0 3.6 %collective-permute-start.13 = (f32[13,8,128]{2,1,0:T(8,128)S(1)}, f32[13,8,128]{2,1,0:T(8,128)S(1)}, u32[]{:S(2)}, u32[]{:S(2)}) collective-permute-start(f32[13,8,128]{2,1,0:T(8,128)S(1)} %get-tuple-element.67), channel_id=1, source_target_pairs={{0,56},{8,16},{16,8},{24,32},{32,24},{40,48},{48,40},{56,0},{1,57}... | collective-permute-start | bytes 159752 | tf_op jit(solution)/shard_map/ppermute | solution.py:727

commit v3 on v2

--- a/solution.py
+++ b/solution.py
@@ -18,7 +18,7 @@
 GZ = ("zh", "xx")
 FLAT = ("gx", "xx")
 DEEP = ("zl", "co", "zh")
-FIRST, SECOND = FLAT, DEEP
+FIRST, SECOND = ("xx","co"), ("gx","zl","zh")
 WEIGHT = pl.CostEstimate(flops=10**11, bytes_accessed=10**8, transcendentals=0)
 GROUP = 14
 
@@ -143,6 +143,13 @@
 
 def column(matrix, j):
     return [matrix[i][j] for i in range(3)]
+
+
+def both_traces(line):
+    low = TAB["low_trace"]
+    middle = low[1] * line[1] + (0.5 * (low[0] + low[2])) * (line[0] + line[2])
+    slope = (0.5 * (low[0] - low[2])) * (line[0] - line[2])
+    return middle + slope, middle - slope
 
 
 def contract(source, matrix, position):
@@ -267,20 +274,8 @@
     return 9 * a + 3 * b + c
 
 
-def pack_kernel(
-    dens_far, ener_far, vel_far, near, far, both, nodes, top, dens, ener, vel, wide, split, sems
-):
+def arrange_nodes(vel, nodes, wide, split):
     lane = lane_index()
-    even = even_along(GZ)
-    copies = [
-        pltpu.make_async_copy(source, target, sems.at[n])
-        for n, (source, target) in enumerate(
-            ((vel_far, vel), (ener_far, ener), (dens_far, dens))
-        )
-    ]
-    for copy in copies:
-        copy.start()
-    copies[0].wait()
     half = (2 * lane) % 128
     for d in range(3):
         for px in range(2):
@@ -298,22 +293,41 @@
                 split[slot, 8 * pz : 8 * pz + 8, :] = picked
             for py in range(2):
                 nodes[2 * slot + py] = split[slot, pl.ds(py, 8, stride=2), :]
-    copies[1].wait()
-    copies[2].wait()
-    low = ener[0, 0]
+
+
+def arrange_points(dens, ener, both):
     for q in range(27):
         for i in range(2):
             both[q, 2 * i : 2 * i + 2, :] = dens[q, i]
             both[q, 4 + 2 * i : 6 + 2 * i, :] = ener[q, i]
-            low = jnp.maximum(low, ener[q, i])
-    top[...] = jnp.broadcast_to(jnp.max(low, keepdims=True), top.shape)
+
+
+def pack_kernel(
+    dens_far, ener_far, vel_far, near, far, top, dens, ener, vel, both, nodes, wide, split, sems
+):
+    even = even_along(GZ)
+    copies = [
+        pltpu.make_async_copy(source, target, sems.at[n])
+        for n, (source, target) in enumerate(
+            ((vel_far, vel), (ener_far, ener), (dens_far, dens))
+        )
+    ]
+    for copy in copies:
+        copy.start()
+    copies[0].wait()
+    arrange_nodes(vel, nodes, wide, split)
+    copies[1].wait()
+    high = jnp.max(ener[...], axis=(0, 1))
+    top[...] = jnp.broadcast_to(jnp.max(high, keepdims=True), top.shape)
+    copies[2].wait()
+    arrange_points(dens, ener, both)
+    group = lane_index() // 4
     sources = [[both[q] for q in range(GROUP)], [both[q] for q in range(GROUP, 27)]]
     sources.append([nodes[n] for n in range(12)])
     for t in range(3):
         up = jnp.ones(TILE, F32)
         down = jnp.ones(TILE, F32)
         for g, tile in enumerate(sources[t]):
-            group = lane // 4
             up = jnp.where(group == 2 * g, roll_lanes(tile, 8 * g - 124), up)
             down = jnp.where(group == 2 * g + 1, roll_lanes(tile, 8 * g + 4), down)
         near[t] = jnp.where(even, up, down)
@@ -329,8 +343,12 @@
     step[...] = CFL / jnp.sqrt((GAMMA * (GAMMA - 1.0)) * top)
 
 
-def force_kernel(both, nodes, from_near, from_far, rho, vz, parts, near, far):
+def force_kernel(
+    dens, ener, vel, from_near, from_far, rho, vz, parts, near, far, both, nodes, wide, split
+):
     sh = Shifts()
+    arrange_points(dens, ener, both)
+    arrange_nodes(vel, nodes, wide, split)
     below = ((lane_index() & 7) < 4) ^ (~even_along(GZ))
     merged = [jnp.where(below, from_far[t], from_near[t]) for t in range(3)]
 
@@ -345,11 +363,11 @@
     pressure = {}
     for key in POINTS:
         q = point(*key)
-        dens, ener = extend(both[q], q // GROUP, q % GROUP)
-        heat = dens * ener
-        rho[0, q] = dens
+        inside, warmth = extend(both[q], q // GROUP, q % GROUP)
+        heat = inside * warmth
+        rho[0, q] = inside
         rho[1, q] = heat
-        density[key] = dens
+        density[key] = inside
         pressure[key] = (GAMMA - 1.0) * heat
     for n in range(12):
         even, odd = extend(nodes[n], 2, n)
@@ -473,7 +491,7 @@
 
 def velocity_kernel(
     scale, sums, sums_x, old, old_x, rho, rho_x, heat_x, from_near, from_far,
-    new_vel, u0, disp, speeds, sides, split, wide,
+    stored, u0, disp, speeds, sides, split, wide, new_vel, sem,
 ):
     sh = Shifts()
     lane = lane_index()
@@ -542,6 +560,8 @@
                 )
             new_vel[d, px] = wide[slot, 0:4, :]
             new_vel[d, 2 + px] = wide[slot, 4:8, :]
+    store = pltpu.make_async_copy(new_vel, stored, sem)
+    store.start()
     eb = TAB["eval_b"]
     minus = -step
 
@@ -607,6 +627,7 @@
                 sides[side, 1, at] = beside("heat", m, n) if side else heat_x[at]
                 for d in TRIPLE:
                     sides[side, 2 + d, at] = sum(weigh[k] * gauss[d][k] for k in keys)
+    store.wait()
 
 
 def stage_kernel(weight, last, *refs):
@@ -621,6 +642,9 @@
         outs = refs[3:]
     else:
         outs = refs[6:]
+        if last:
+            sems = outs.pop()
+            ready = outs.pop()
         sides = outs.pop()
         for d in range(2):
             step = 2 - d
@@ -629,11 +653,12 @@
             for f, m in FACE_KEYS:
                 sides[d, f, m] = sh.beside(over((f, m)), under((f, m)), step)
     traces = None if last else outs.pop()
-    low = TAB["low_trace"]
-    high = TAB["high_trace"]
-    low_lift = TAB["low_lift"]
-    high_lift = TAB["high_lift"]
+    lift = TAB["low_lift"]
     volume = TAB["volume"]
+    odd_w = 0.5 * (volume[0][0] - volume[2][0])
+    even_w = 0.5 * (volume[0][0] + volume[2][0])
+    odd_f = 0.5 * (lift[0] + lift[2])
+    even_f = 0.5 * (lift[0] - lift[2])
 
     def one_field(f, carry):
         fields = {key: u[f, point(*key)] for key in POINTS}
@@ -650,8 +675,7 @@
                     at = 3 * m + n
                     line = [fields[k] for k in keys]
                     moved = [disp[d, point(*k)] * fields[k] for k in keys]
-                    tm = combine(line, low)
-                    tp = combine(line, high)
+                    tm, tp = both_traces(line)
                     if d < 2:
                         step = 2 - d
                         before = sh.before(sides[d, f, at], tp, step)
@@ -664,12 +688,18 @@
                         s_low = speeds[4, at]
                         f_low = s_low * jnp.where(s_low > 0.0, sh.z_prev(tp), tm)
                         f_high = sh.z_next(f_low)
-                    for a in range(3):
-                        piece = combine(
-                            moved + [f_low, f_high],
-                            column(volume, a) + [low_lift[a], -high_lift[a]],
-                        )
-                        rate[keys[a]] = rate[keys[a]] + piece if d else piece
+                    across = moved[0] - moved[2]
+                    jump = f_low - f_high
+                    odd = odd_w * across + odd_f * jump
+                    even_part = even_w * (moved[0] + moved[2]) + volume[1][0] * moved[1]
+                    even_part = even_part + even_f * (f_low + f_high)
+                    pieces = [
+                        odd + even_part,
+                        volume[0][1] * across + lift[1] * jump,
+                        odd - even_part,
+                    ]
+                    for k, piece in zip(keys, pieces):
+                        rate[k] = rate[k] + piece if d else piece
         after = {}
         for key in POINTS:
             q = point(*key)
@@ -678,37 +708,45 @@
             else:
                 value = (1.0 - weight) * u0[f, q] + weight * (fields[key] + rate[key])
             if last:
-                outs[0][f, q, 0] = value[0:2]
-                outs[0][f, q, 1] = value[2:4]
+                ready[f, q, 0] = value[0:2]
+                ready[f, q, 1] = value[2:4]
             else:
                 outs[0][f, q] = value
                 after[key] = value
-        if not last:
+        if last:
+            pltpu.make_async_copy(ready.at[f], outs[0].at[f], sems.at[f]).start()
+        else:
             for d in range(2):
                 for m in range(3):
                     for n in range(3):
                         keys = [(a, m, n) if d == 0 else (m, a, n) for a in range(3)]
-                        line = [after[k] for k in keys]
-                        traces[2 * d, f, 3 * m + n] = combine(line, high)
-                        traces[2 * d + 1, f, 3 * m + n] = combine(line, low)
+                        tm, tp = both_traces([after[k] for k in keys])
+                        traces[2 * d, f, 3 * m + n] = tp
+                        traces[2 * d + 1, f, 3 * m + n] = tm
         return carry
 
-    lax.fori_loop(0, 5, one_field, 0)
-    if not last:
+    lax.fori_loop(0, 5, one_field, 0, unroll=True)
+    if last:
+        for f in range(5):
+            pltpu.make_async_copy(ready.at[f], outs[0].at[f], sems.at[f]).wait()
+    else:
         for d in range(2):
             lists = [[traces[2 * d + k, f, m] for f, m in FACE_KEYS] for k in range(2)]
             write_messages(sh, even[d], outs[1 + 2 * d], outs[2 + 2 * d], *lists, 2 - d)
 
 
-def call(kernel, outs, *args, scratch=(), name=None, weigh=None, far=False):
+def call(kernel, outs, *args, scratch=(), name=None, weigh=None, far=False, stored=()):
     space = pltpu.HBM if far else pltpu.VMEM
     return pl.pallas_call(
         kernel,
         out_shape=[jax.ShapeDtypeStruct(o, F32) for o in outs],
         in_specs=[pl.BlockSpec(memory_space=space) for _ in args],
-        out_specs=[pl.BlockSpec(memory_space=pltpu.VMEM)] * len(outs),
+        out_specs=[
+            pl.BlockSpec(memory_space=pltpu.HBM if n in stored else pltpu.VMEM)
+            for n in range(len(outs))
+        ],
         scratch_shapes=[pltpu.VMEM(s, F32) if isinstance(s, tuple) else s for s in scratch],
-        compiler_params=pltpu.CompilerParams(vmem_limit_bytes=32 * 1024 * 1024),
+        compiler_params=pltpu.CompilerParams(vmem_limit_bytes=(60 if far else 32) * 1024 * 1024),
         cost_estimate=weigh,
         name=name,
     )(*args)
@@ -739,14 +777,12 @@
     tile = TILE
     dens = density.reshape((27,) + density.shape[3:])
     ener = energy.reshape((27,) + energy.shape[3:])
-    near, far, both, nodes, top = call(
+    arranged = [(27,) + tile, (12,) + tile, (6, 8, 256), (6, 16, 128)]
+    near, far, top = call(
         pack_kernel,
-        [(3,) + tile, (3,) + tile, (27,) + tile, (12,) + tile, (axis_count(FIRST), 128)],
+        [(3,) + tile, (3,) + tile, (axis_count(FIRST), 128)],
         dens, ener, velocity,
-        scratch=[
-            dens.shape, ener.shape, velocity.shape,
-            (6, 8, 256), (6, 16, 128), pltpu.SemaphoreType.DMA((3,)),
-        ],
+        scratch=[dens.shape, ener.shape, velocity.shape] + arranged + [pltpu.SemaphoreType.DMA((3,))],
         far=True,
         name="pack",
     )
@@ -762,7 +798,8 @@
     rho, vz, parts, near, far = call(
         force_kernel,
         [(2, 27) + tile, (12, 2) + tile, parts_shape, message, message],
-        both, nodes, near, far,
+        dens, ener, velocity, near, far,
+        scratch=arranged,
         name="force",
     )
     far = far_swap(far, GX)
@@ -784,7 +821,8 @@
         velocity_kernel,
         [velocity.shape, state, (3, 27) + tile, (5, 9) + tile, (2, 5, 9) + tile],
         step, sums, sums_x, old, old_x, rho, rho_x, heat_x, near, far,
-        scratch=[(6, 16, 128), (6, 8, 256)],
+        scratch=[(6, 16, 128), (6, 8, 256), velocity.shape, pltpu.SemaphoreType.DMA],
+        stored=(0,),
         name="velocity",
     )
     faces = [(message_size(FACE_KEYS),) + tile] * 4
@@ -804,7 +842,8 @@
     (remapped,) = call(
         functools.partial(stage_kernel, 2.0 / 3.0, True), [(5, 27) + density.shape[3:]],
         u0, two, disp, speeds, *exchange(*messages),
-        scratch=[sides.shape],
+        scratch=[sides.shape, (5, 27) + density.shape[3:], pltpu.SemaphoreType.DMA((5,))],
+        stored=(0,),
         name="stage_three",
     )
     return new_velocity, remapped.reshape((5, 3, 3, 3) + density.shape[3:])

time: 63 us -> 59.7 us (0.948)
  the two profiles are of different devices: /device:TPU:1 before, /device:TPU:24 now
where the time goes in v3:
time: 59.7 us; the launch traced here: 59 us
  starting transfers between devices  31.6 us (53%)
  waiting for transfers between devices  17.9 us (30%)
  Pallas kernels  8.68 us (15%)
  between operations  0.79 us (1%)
    ppermute x7, starting transfers between devices, far_swap(): lax.ppermute(value, axis, [(i, (i + 2 * (i % 2) - 1) % count) for i in ra...  18.2 us
    ppermute x7, waiting for transfers between devices, far_swap(): lax.ppermute(value, axis, [(i, (i + 2 * (i % 2) - 1) % count) for i in ra...  8.98 us
    pallas_call x9, Pallas kernels, call(): pl.pallas_call(kernel, out_shape=[jax.ShapeDtypeStruct(o, F32) for o in o...  8.68 us
    all_to_all x1, starting transfers between devices, shards(): tops = lax.all_to_all(top, SECOND, 0, 0, tiled=True)  6.62 us
    all_to_all x1, waiting for transfers between devices, shards(): tops = lax.all_to_all(top, SECOND, 0, 0, tiled=True)  3.93 us
    ppermute x7, starting transfers between devices, near_swap(): lax.ppermute(value, axis, [(i, i ^ 1) for i in range(axis_count(axis))])  3.56 us
    all_to_all x1, starting transfers between devices, shards(): tops = lax.all_to_all(top, FIRST, 0, 0, tiled=True)  3.26 us
    all_to_all x1, waiting for transfers between devices, shards(): tops = lax.all_to_all(top, FIRST, 0, 0, tiled=True)  2.59 us
  transfers between devices with their start and end apart: 16, of which 9 were waited for; matrix products, arithmetic and copies ran while one was open for 0% of the time, Pallas kernels for 3%

profile of v3, /device:TPU:24, one launch (start us, length us, event | category | flops | bytes accessed | tf_op | source)
XLA Modules:
  0.0 59.0 jit_solution(6835483924265411320)
XLA Ops:
  0.7 1.9 %pack.1 = (f32[3,8,128]{2,1,0:T(8,128)}, f32[3,8,128]{2,1,0:T(8,128)}, f32[8,128]{1,0:T(8,128)}) custom-call(f32[27,2,2,128]{3,2,1,0:T(2,128)} %bitcast.11, f32[27,2,2,128]{3,2,1,0:T(2,128)} %bitcast.13, f32[3,4,4,256]{3,2,1,0:T(4,128)} %vel.1), custom_call_target="tpu_custom_call" | custom-call | tf_op jit(solution)/shard_map/pack/pallas_call | solution.py:740
  2.5 1.6 %collective-permute-start = (f32[3,8,128]{2,1,0:T(8,128)}, f32[3,8,128]{2,1,0:T(8,128)S(1)}, u32[]{:S(2)}, u32[]{:S(2)}) collective-permute-start(f32[3,8,128]{2,1,0:T(8,128)} %get-tuple-element.34), channel_id=1, source_target_pairs={{0,1},{1,0},{2,3},{3,2},{4,5},{5,4},{6,7},{7,6},{8,9},{9,8},{10,11... | collective-permute-start | bytes 36872 | tf_op jit(solution)/shard_map/ppermute | solution.py:760
  4.1 8.7 %collective-permute-start.1 = (f32[3,8,128]{2,1,0:T(8,128)}, f32[3,8,128]{2,1,0:T(8,128)S(1)}, u32[]{:S(2)}, u32[]{:S(2)}) collective-permute-start(f32[3,8,128]{2,1,0:T(8,128)} %get-tuple-element.35), channel_id=1, source_target_pairs={{0,7},{1,2},{2,1},{3,4},{4,3},{5,6},{6,5},{7,0},{8,15},{9,10},{10,... | collective-permute-start | bytes 36872 | tf_op jit(solution)/shard_map/ppermute | solution.py:765
  12.8 3.3 %all-to-all-start = ((f32[8,1,128]{2,1,0:T(1,128)}), f32[8,1,128]{2,1,0:T(1,128)S(1)}, u32[]{:S(2)}, u32[]{:S(2)}) async-start(f32[8,1,128]{2,1,0:T(1,128)} %bitcast.3), calls=%async_computation | async-start | bytes 8192 | tf_op jit(solution)/shard_map/all_to_all | solution.py:791
  16.8 0.9 %collective-permute-start.2 = (f32[39,8,128]{2,1,0:T(8,128)S(1)}, f32[39,8,128]{2,1,0:T(8,128)S(1)}, u32[]{:S(2)}, u32[]{:S(2)}) collective-permute-start(f32[39,8,128]{2,1,0:T(8,128)S(1)} %get-tuple-element.39), channel_id=1, source_target_pairs={{0,64},{64,0},{128,192},{192,128},{1,65},{65,1},{129,193},{193,129... | collective-permute-start | bytes 479240 | tf_op jit(solution)/shard_map/ppermute | solution.py:760
  17.6 1.1 %collective-permute-start.3 = (f32[39,8,128]{2,1,0:T(8,128)S(1)}, f32[39,8,128]{2,1,0:T(8,128)S(1)}, u32[]{:S(2)}, u32[]{:S(2)}) collective-permute-start(f32[39,8,128]{2,1,0:T(8,128)S(1)} %get-tuple-element.40), channel_id=1, source_target_pairs={{0,192},{64,128},{128,64},{192,0},{1,193},{65,129},{129,65},{193,1... | collective-permute-start | bytes 479240 | tf_op jit(solution)/shard_map/ppermute | solution.py:765
  18.7 2.6 %all-to-all-done = f32[8,1,128]{2,1,0:T(1,128)S(1)} async-done(((f32[8,1,128]{2,1,0:T(1,128)}), f32[8,1,128]{2,1,0:T(1,128)S(1)}, u32[]{:S(2)}, u32[]{:S(2)}) %all-to-all-start) | async-done | bytes 4128 | tf_op jit(solution)/shard_map/all_to_all | solution.py:791
  21.9 6.6 %all-to-all-start.1 = ((f32[32,1,128]{2,1,0:T(1,128)}), f32[32,1,128]{2,1,0:T(1,128)S(1)}, u32[]{:S(2)}, u32[]{:S(2)}) async-start(f32[32,1,128]{2,1,0:T(1,128)} %bitcast.6), calls=%async_computation.1 | async-start | bytes 32768 | tf_op jit(solution)/shard_map/all_to_all | solution.py:793
  29.1 3.4 %collective-permute-start.5 = (f32[55,8,128]{2,1,0:T(8,128)S(1)}, f32[55,8,128]{2,1,0:T(8,128)S(1)}, u32[]{:S(2)}, u32[]{:S(2)}) collective-permute-start(f32[55,8,128]{2,1,0:T(8,128)S(1)} %get-tuple-element.48), channel_id=1, source_target_pairs={{0,56},{8,16},{16,8},{24,32},{32,24},{40,48},{48,40},{56,0},{1,57}... | collective-permute-start | bytes 675848 | tf_op jit(solution)/shard_map/ppermute | solution.py:765
  32.5 3.9 %all-to-all-done.1 = f32[32,1,128]{2,1,0:T(1,128)S(1)} async-done(((f32[32,1,128]{2,1,0:T(1,128)}), f32[32,1,128]{2,1,0:T(1,128)S(1)}, u32[]{:S(2)}, u32[]{:S(2)}) %all-to-all-start.1) | async-done | bytes 16416 | tf_op jit(solution)/shard_map/all_to_all | solution.py:793
  36.5 1.9 %collective-permute-done.5.from_far = f32[55,8,128]{2,1,0:T(8,128)S(1)} collective-permute-done((f32[55,8,128]{2,1,0:T(8,128)S(1)}, f32[55,8,128]{2,1,0:T(8,128)S(1)}, u32[]{:S(2)}, u32[]{:S(2)}) %collective-permute-start.5) | collective-permute-done | bytes 225312 | tf_op jit(solution)/shard_map/ppermute | solution.py:765
  38.4 1.3 %velocity.1 = (f32[3,4,4,256]{3,2,1,0:T(4,128)}, f32[5,27,8,128]{3,2,1,0:T(8,128)S(1)}, f32[3,27,8,128]{3,2,1,0:T(8,128)S(1)}, f32[5,9,8,128]{3,2,1,0:T(8,128)S(1)}, f32[2,5,9,8,128]{4,3,2,1,0:T(8,128)S(1)}) custom-call(f32[8,128]{1,0:T(8,128)S(1)} %step.1.scale, f32[4,9,2,8,128]{4,3,2,1,0:T(8,128)S(1)} %get-tuple-element.41.sums, ...), custom_call_target="tpu_custom_call" | custom-call | tf_op jit(solution)/shard_map/velocity/pallas_call | solution.py:740
  39.7 1.0 %stage_one.1 = (f32[5,27,8,128]{3,2,1,0:T(8,128)S(1)}, f32[13,8,128]{2,1,0:T(8,128)S(1)}, f32[13,8,128]{2,1,0:T(8,128)S(1)}, f32[13,8,128]{2,1,0:T(8,128)S(1)}, f32[13,8,128]{2,1,0:T(8,128)S(1)}) custom-call(f32[5,27,8,128]{3,2,1,0:T(8,128)S(1)} %get-tuple-element.50.refs_0_, f32[3,27,8,128]{3,2,1,0:T(8,128)S(1)} %get-tuple-element.51.refs_1_.refs_2_, ...), custom_call_target="tpu_custom_call" | custom-call | tf_op jit(solution)/shard_map/stage_one/pallas_call | solution.py:740
  40.7 0.9 %collective-permute-start.6 = (f32[13,8,128]{2,1,0:T(8,128)S(1)}, f32[13,8,128]{2,1,0:T(8,128)S(1)}, u32[]{:S(2)}, u32[]{:S(2)}) collective-permute-start(f32[13,8,128]{2,1,0:T(8,128)S(1)} %get-tuple-element.55), channel_id=1, source_target_pairs={{0,64},{64,0},{128,192},{192,128},{1,65},{65,1},{129,193},{193,129... | collective-permute-start | bytes 159752 | tf_op jit(solution)/shard_map/ppermute | solution.py:760
  41.6 1.2 %collective-permute-start.7 = (f32[13,8,128]{2,1,0:T(8,128)S(1)}, f32[13,8,128]{2,1,0:T(8,128)S(1)}, u32[]{:S(2)}, u32[]{:S(2)}) collective-permute-start(f32[13,8,128]{2,1,0:T(8,128)S(1)} %get-tuple-element.56), channel_id=1, source_target_pairs={{0,192},{64,128},{128,64},{192,0},{1,193},{65,129},{129,65},{193,1... | collective-permute-start | bytes 159752 | tf_op jit(solution)/shard_map/ppermute | solution.py:765
  43.7 1.3 %collective-permute-done.6.refs_4_ = f32[13,8,128]{2,1,0:T(8,128)S(1)} collective-permute-done((f32[13,8,128]{2,1,0:T(8,128)S(1)}, f32[13,8,128]{2,1,0:T(8,128)S(1)}, u32[]{:S(2)}, u32[]{:S(2)}) %collective-permute-start.6) | collective-permute-done | bytes 53280 | tf_op jit(solution)/shard_map/ppermute | solution.py:760
  44.9 2.0 %collective-permute-done.7.refs_5_ = f32[13,8,128]{2,1,0:T(8,128)S(1)} collective-permute-done((f32[13,8,128]{2,1,0:T(8,128)S(1)}, f32[13,8,128]{2,1,0:T(8,128)S(1)}, u32[]{:S(2)}, u32[]{:S(2)}) %collective-permute-start.7) | collective-permute-done | bytes 53280 | tf_op jit(solution)/shard_map/ppermute | solution.py:765
  47.0 1.2 %collective-permute-done.9.refs_7_ = f32[13,8,128]{2,1,0:T(8,128)S(1)} collective-permute-done((f32[13,8,128]{2,1,0:T(8,128)S(1)}, f32[13,8,128]{2,1,0:T(8,128)S(1)}, u32[]{:S(2)}, u32[]{:S(2)}) %collective-permute-start.9) | collective-permute-done | bytes 53280 | tf_op jit(solution)/shard_map/ppermute | solution.py:765
  48.2 1.1 %stage_two.1 = (f32[5,27,8,128]{3,2,1,0:T(8,128)S(1)}, f32[13,8,128]{2,1,0:T(8,128)S(1)}, f32[13,8,128]{2,1,0:T(8,128)S(1)}, f32[13,8,128]{2,1,0:T(8,128)S(1)}, f32[13,8,128]{2,1,0:T(8,128)S(1)}) custom-call(f32[5,27,8,128]{3,2,1,0:T(8,128)S(1)} %get-tuple-element.50.refs_0_, f32[5,27,8,128]{3,2,1,0:T(8,128)S(1)} %get-tuple-element.54.refs_1_, ...), custom_call_target="tpu_custom_call" | custom-call | tf_op jit(solution)/shard_map/stage_two/pallas_call | solution.py:740
  49.4 2.6 %collective-permute-start.11 = (f32[13,8,128]{2,1,0:T(8,128)S(1)}, f32[13,8,128]{2,1,0:T(8,128)S(1)}, u32[]{:S(2)}, u32[]{:S(2)}) collective-permute-start(f32[13,8,128]{2,1,0:T(8,128)S(1)} %get-tuple-element.61), channel_id=1, source_target_pairs={{0,192},{64,128},{128,64},{192,0},{1,193},{65,129},{129,65},{193,1... | collective-permute-start | bytes 159752 | tf_op jit(solution)/shard_map/ppermute | solution.py:765
  52.4 1.1 %collective-permute-done.10.refs_4_ = f32[13,8,128]{2,1,0:T(8,128)S(1)} collective-permute-done((f32[13,8,128]{2,1,0:T(8,128)S(1)}, f32[13,8,128]{2,1,0:T(8,128)S(1)}, u32[]{:S(2)}, u32[]{:S(2)}) %collective-permute-start.10) | collective-permute-done | bytes 53280 | tf_op jit(solution)/shard_map/ppermute | solution.py:760
  53.5 1.3 %collective-permute-done.11.refs_5_ = f32[13,8,128]{2,1,0:T(8,128)S(1)} collective-permute-done((f32[13,8,128]{2,1,0:T(8,128)S(1)}, f32[13,8,128]{2,1,0:T(8,128)S(1)}, u32[]{:S(2)}, u32[]{:S(2)}) %collective-permute-start.11) | collective-permute-done | bytes 53280 | tf_op jit(solution)/shard_map/ppermute | solution.py:765
  54.8 2.6 %collective-permute-done.13.refs_7_ = f32[13,8,128]{2,1,0:T(8,128)S(1)} collective-permute-done((f32[13,8,128]{2,1,0:T(8,128)S(1)}, f32[13,8,128]{2,1,0:T(8,128)S(1)}, u32[]{:S(2)}, u32[]{:S(2)}) %collective-permute-start.13) | collective-permute-done | bytes 53280 | tf_op jit(solution)/shard_map/ppermute | solution.py:765
  57.4 1.6 %stage_three.1 = f32[5,27,2,2,128]{4,3,2,1,0:T(2,128)} custom-call(f32[5,27,8,128]{3,2,1,0:T(8,128)S(1)} %get-tuple-element.50.refs_0_, f32[5,27,8,128]{3,2,1,0:T(8,128)S(1)} %get-tuple-element.59.refs_1_, f32[3,27,8,128]{3,2,1,0:T(8,128)S(1)} %get-tuple-element.51.refs_1_.refs_2_, f32[5,9,8,128]{3,2,1,0:T(8,128)S(1)} %get-tuple-element.52.refs_2_.refs_3_, ...), custom_call_target="tpu_custom_call" | custom-call | tf_op jit(solution)/shard_map/stage_three/pallas_call | solution.py:740
  (23 shorter events, 3.1 us)
Async XLA Ops:
  0.6 15.5 %copy-start = (f32[3,3,3,2,2,128]{5,4,3,2,1,0:T(2,128)S(1)}, f32[3,3,3,2,2,128]{5,4,3,2,1,0:T(2,128)}, u32[]{:S(2)}) copy-start(f32[3,3,3,2,2,128]{5,4,3,2,1,0:T(2,128)} %param.3) | copy-start | bytes 165892
  0.6 15.5 %copy-start.1 = (f32[3,3,3,2,2,128]{5,4,3,2,1,0:T(2,128)S(1)}, f32[3,3,3,2,2,128]{5,4,3,2,1,0:T(2,128)}, u32[]{:S(2)}) copy-start(f32[3,3,3,2,2,128]{5,4,3,2,1,0:T(2,128)} %param.4) | copy-start | bytes 165892
  0.6 15.5 %copy-start.2 = (f32[3,4,4,256]{3,2,1,0:T(4,128)S(1)}, f32[3,4,4,256]{3,2,1,0:T(4,128)}, u32[]{:S(2)}) copy-start(f32[3,4,4,256]{3,2,1,0:T(4,128)} %vel.1) | copy-start | bytes 147460
  2.5 13.6 %collective-permute-start = (f32[3,8,128]{2,1,0:T(8,128)}, f32[3,8,128]{2,1,0:T(8,128)S(1)}, u32[]{:S(2)}, u32[]{:S(2)}) collective-permute-start(f32[3,8,128]{2,1,0:T(8,128)} %get-tuple-element.34), channel_id=1, source_target_pairs={{0,1},{1,0},{2,3},{3,2},{4,5},{5,4},{6,7},{7,6},{8,9},{9,8},{10,11... | collective-permute-start | bytes 36872 | tf_op jit(solution)/shard_map/ppermute | solution.py:760
  4.1 12.0 %collective-permute-start.1 = (f32[3,8,128]{2,1,0:T(8,128)}, f32[3,8,128]{2,1,0:T(8,128)S(1)}, u32[]{:S(2)}, u32[]{:S(2)}) collective-permute-start(f32[3,8,128]{2,1,0:T(8,128)} %get-tuple-element.35), channel_id=1, source_target_pairs={{0,7},{1,2},{2,1},{3,4},{4,3},{5,6},{6,5},{7,0},{8,15},{9,10},{10,... | collective-permute-start | bytes 36872 | tf_op jit(solution)/shard_map/ppermute | solution.py:765
  12.8 8.4 %all-to-all-start = ((f32[8,1,128]{2,1,0:T(1,128)}), f32[8,1,128]{2,1,0:T(1,128)S(1)}, u32[]{:S(2)}, u32[]{:S(2)}) async-start(f32[8,1,128]{2,1,0:T(1,128)} %bitcast.3), calls=%async_computation | async-start | bytes 8192 | tf_op jit(solution)/shard_map/all_to_all | solution.py:791
  16.8 11.7 %collective-permute-start.2 = (f32[39,8,128]{2,1,0:T(8,128)S(1)}, f32[39,8,128]{2,1,0:T(8,128)S(1)}, u32[]{:S(2)}, u32[]{:S(2)}) collective-permute-start(f32[39,8,128]{2,1,0:T(8,128)S(1)} %get-tuple-element.39), channel_id=1, source_target_pairs={{0,64},{64,0},{128,192},{192,128},{1,65},{65,1},{129,193},{193,129... | collective-permute-start | bytes 479240 | tf_op jit(solution)/shard_map/ppermute | solution.py:760
  17.6 10.9 %collective-permute-start.3 = (f32[39,8,128]{2,1,0:T(8,128)S(1)}, f32[39,8,128]{2,1,0:T(8,128)S(1)}, u32[]{:S(2)}, u32[]{:S(2)}) collective-permute-start(f32[39,8,128]{2,1,0:T(8,128)S(1)} %get-tuple-element.40), channel_id=1, source_target_pairs={{0,192},{64,128},{128,64},{192,0},{1,193},{65,129},{129,65},{193,1... | collective-permute-start | bytes 479240 | tf_op jit(solution)/shard_map/ppermute | solution.py:765
  21.9 14.6 %all-to-all-start.1 = ((f32[32,1,128]{2,1,0:T(1,128)}), f32[32,1,128]{2,1,0:T(1,128)S(1)}, u32[]{:S(2)}, u32[]{:S(2)}) async-start(f32[32,1,128]{2,1,0:T(1,128)} %bitcast.6), calls=%async_computation.1 | async-start | bytes 32768 | tf_op jit(solution)/shard_map/all_to_all | solution.py:793
  29.0 7.5 %collective-permute-start.4 = (f32[55,8,128]{2,1,0:T(8,128)S(1)}, f32[55,8,128]{2,1,0:T(8,128)S(1)}, u32[]{:S(2)}, u32[]{:S(2)}) collective-permute-start(f32[55,8,128]{2,1,0:T(8,128)S(1)} %get-tuple-element.47), channel_id=1, source_target_pairs={{0,8},{8,0},{16,24},{24,16},{32,40},{40,32},{48,56},{56,48},{1,9},... | collective-permute-start | bytes 675848 | tf_op jit(solution)/shard_map/ppermute | solution.py:760
  29.1 9.2 %collective-permute-start.5 = (f32[55,8,128]{2,1,0:T(8,128)S(1)}, f32[55,8,128]{2,1,0:T(8,128)S(1)}, u32[]{:S(2)}, u32[]{:S(2)}) collective-permute-start(f32[55,8,128]{2,1,0:T(8,128)S(1)} %get-tuple-element.48), channel_id=1, source_target_pairs={{0,56},{8,16},{16,8},{24,32},{32,24},{40,48},{48,40},{56,0},{1,57}... | collective-permute-start | bytes 675848 | tf_op jit(solution)/shard_map/ppermute | solution.py:765
  40.7 4.2 %collective-permute-start.6 = (f32[13,8,128]{2,1,0:T(8,128)S(1)}, f32[13,8,128]{2,1,0:T(8,128)S(1)}, u32[]{:S(2)}, u32[]{:S(2)}) collective-permute-start(f32[13,8,128]{2,1,0:T(8,128)S(1)} %get-tuple-element.55), channel_id=1, source_target_pairs={{0,64},{64,0},{128,192},{192,128},{1,65},{65,1},{129,193},{193,129... | collective-permute-start | bytes 159752 | tf_op jit(solution)/shard_map/ppermute | solution.py:760
  41.6 5.3 %collective-permute-start.7 = (f32[13,8,128]{2,1,0:T(8,128)S(1)}, f32[13,8,128]{2,1,0:T(8,128)S(1)}, u32[]{:S(2)}, u32[]{:S(2)}) collective-permute-start(f32[13,8,128]{2,1,0:T(8,128)S(1)} %get-tuple-element.56), channel_id=1, source_target_pairs={{0,192},{64,128},{128,64},{192,0},{1,193},{65,129},{129,65},{193,1... | collective-permute-start | bytes 159752 | tf_op jit(solution)/shard_map/ppermute | solution.py:765
  42.8 4.2 %collective-permute-start.8 = (f32[13,8,128]{2,1,0:T(8,128)S(1)}, f32[13,8,128]{2,1,0:T(8,128)S(1)}, u32[]{:S(2)}, u32[]{:S(2)}) collective-permute-start(f32[13,8,128]{2,1,0:T(8,128)S(1)} %get-tuple-element.57), channel_id=1, source_target_pairs={{0,8},{8,0},{16,24},{24,16},{32,40},{40,32},{48,56},{56,48},{1,9},... | collective-permute-start | bytes 159752 | tf_op jit(solution)/shard_map/ppermute | solution.py:760
  42.8 5.4 %collective-permute-start.9 = (f32[13,8,128]{2,1,0:T(8,128)S(1)}, f32[13,8,128]{2,1,0:T(8,128)S(1)}, u32[]{:S(2)}, u32[]{:S(2)}) collective-permute-start(f32[13,8,128]{2,1,0:T(8,128)S(1)} %get-tuple-element.58), channel_id=1, source_target_pairs={{0,56},{8,16},{16,8},{24,32},{32,24},{40,48},{48,40},{56,0},{1,57}... | collective-permute-start | bytes 159752 | tf_op jit(solution)/shard_map/ppermute | solution.py:765
  49.3 4.2 %collective-permute-start.10 = (f32[13,8,128]{2,1,0:T(8,128)S(1)}, f32[13,8,128]{2,1,0:T(8,128)S(1)}, u32[]{:S(2)}, u32[]{:S(2)}) collective-permute-start(f32[13,8,128]{2,1,0:T(8,128)S(1)} %get-tuple-element.60), channel_id=1, source_target_pairs={{0,64},{64,0},{128,192},{192,128},{1,65},{65,1},{129,193},{193,129... | collective-permute-start | bytes 159752 | tf_op jit(solution)/shard_map/ppermute | solution.py:760
  49.4 5.4 %collective-permute-start.11 = (f32[13,8,128]{2,1,0:T(8,128)S(1)}, f32[13,8,128]{2,1,0:T(8,128)S(1)}, u32[]{:S(2)}, u32[]{:S(2)}) collective-permute-start(f32[13,8,128]{2,1,0:T(8,128)S(1)} %get-tuple-element.61), channel_id=1, source_target_pairs={{0,192},{64,128},{128,64},{192,0},{1,193},{65,129},{129,65},{193,1... | collective-permute-start | bytes 159752 | tf_op jit(solution)/shard_map/ppermute | solution.py:765
  52.0 2.8 %collective-permute-start.12 = (f32[13,8,128]{2,1,0:T(8,128)S(1)}, f32[13,8,128]{2,1,0:T(8,128)S(1)}, u32[]{:S(2)}, u32[]{:S(2)}) collective-permute-start(f32[13,8,128]{2,1,0:T(8,128)S(1)} %get-tuple-element.62), channel_id=1, source_target_pairs={{0,8},{8,0},{16,24},{24,16},{32,40},{40,32},{48,56},{56,48},{1,9},... | collective-permute-start | bytes 159752 | tf_op jit(solution)/shard_map/ppermute | solution.py:760
  52.0 5.4 %collective-permute-start.13 = (f32[13,8,128]{2,1,0:T(8,128)S(1)}, f32[13,8,128]{2,1,0:T(8,128)S(1)}, u32[]{:S(2)}, u32[]{:S(2)}) collective-permute-start(f32[13,8,128]{2,1,0:T(8,128)S(1)} %get-tuple-element.63), channel_id=1, source_target_pairs={{0,56},{8,16},{16,8},{24,32},{32,24},{40,48},{48,40},{56,0},{1,57}... | collective-permute-start | bytes 159752 | tf_op jit(solution)/shard_map/ppermute | solution.py:765

commit v4 on v3

--- a/solution.py
+++ b/solution.py
@@ -19,6 +19,7 @@
 FLAT = ("gx", "xx")
 DEEP = ("zl", "co", "zh")
 FIRST, SECOND = ("xx","co"), ("gx","zl","zh")
+ORDER = [("far", 0), ("far", 1), ("near", 0), ("near", 1)]
 WEIGHT = pl.CostEstimate(flops=10**11, bytes_accessed=10**8, transcendentals=0)
 GROUP = 14
 
@@ -344,7 +345,7 @@
 
 
 def force_kernel(
-    dens, ener, vel, from_near, from_far, rho, vz, parts, near, far, both, nodes, wide, split
+    dens, ener, vel, from_far, from_near, rho, vz, parts, near, far, both, nodes, wide, split
 ):
     sh = Shifts()
     arrange_points(dens, ener, both)
@@ -424,7 +425,7 @@
 
 
 def rim_kernel(
-    parts, vz, rho, from_near, from_far,
+    parts, vz, rho, from_far, from_near,
     sums, sums_x, old, old_x, rho_x, heat_x, near, far,
 ):
     sh = Shifts()
@@ -490,7 +491,7 @@
 
 
 def velocity_kernel(
-    scale, sums, sums_x, old, old_x, rho, rho_x, heat_x, from_near, from_far,
+    scale, sums, sums_x, old, old_x, rho, rho_x, heat_x, from_far, from_near,
     stored, u0, disp, speeds, sides, split, wide, new_vel, sem,
 ):
     sh = Shifts()
@@ -648,7 +649,7 @@
         sides = outs.pop()
         for d in range(2):
             step = 2 - d
-            near, far = refs[2 + 2 * d : 4 + 2 * d]
+            near, far = (refs[2 + ORDER.index((k, d))] for k in ("near", "far"))
             under, over = read_messages(sh, even[d], near, far, FACE_KEYS, FACE_KEYS, step)
             for f, m in FACE_KEYS:
                 sides[d, f, m] = sh.beside(over((f, m)), under((f, m)), step)
@@ -766,11 +767,13 @@
 
 
 def exchange(near_x, far_x, near_y, far_y):
-    far_y = far_swap(far_y, GY)
-    far_x = far_swap(far_x, GX)
-    near_x = near_swap(near_x, GX)
-    near_y = near_swap(near_y, GY)
-    return near_x, far_x, near_y, far_y
+    received = {
+        ("near", 0): near_swap(near_x, GX),
+        ("far", 0): far_swap(far_x, GX),
+        ("near", 1): near_swap(near_y, GY),
+        ("far", 1): far_swap(far_y, GY),
+    }
+    return [received[key] for key in ORDER]
 
 
 def shards(density, energy, velocity):
@@ -798,7 +801,7 @@
     rho, vz, parts, near, far = call(
         force_kernel,
         [(2, 27) + tile, (12, 2) + tile, parts_shape, message, message],
-        dens, ener, velocity, near, far,
+        dens, ener, velocity, far, near,
         scratch=arranged,
         name="force",
     )
@@ -811,7 +814,7 @@
             parts_shape, parts_shape, old_shape, old_shape, (27,) + tile, (9,) + tile,
             message, message,
         ],
-        parts, vz, rho, near, far,
+        parts, vz, rho, far, near,
         name="rim",
     )
     far = far_swap(far, GY)
@@ -820,7 +823,7 @@
     new_velocity, u0, disp, speeds, sides = call(
         velocity_kernel,
         [velocity.shape, state, (3, 27) + tile, (5, 9) + tile, (2, 5, 9) + tile],
-        step, sums, sums_x, old, old_x, rho, rho_x, heat_x, near, far,
+        step, sums, sums_x, old, old_x, rho, rho_x, heat_x, far, near,
         scratch=[(6, 16, 128), (6, 8, 256), velocity.shape, pltpu.SemaphoreType.DMA],
         stored=(0,),
         name="velocity",

time: 59.7 us -> 57.3 us (0.960)
  starting transfers between devices: 31.6 us -> 28.8 us
  waiting for transfers between devices: 17.9 us -> 18.8 us
    ppermute x7, waiting for transfers between devices: 2.42 us -> 0.61 us  [near_swap(): lax.ppermute(value, axis, [(i, i ^ 1) for i in range(axis_count(axis))])]
    ppermute x7, starting transfers between devices: 3.56 us -> 1.84 us  [near_swap(): lax.ppermute(value, axis, [(i, i ^ 1) for i in range(axis_count(axis))])]
    ppermute x7, waiting for transfers between devices: 8.98 us -> 10.3 us  [far_swap(): lax.ppermute(value, axis, [(i, (i + 2 * (i % 2) - 1) % count) for i in ra...]
    all_to_all x1, waiting for transfers between devices: 3.93 us -> 5.18 us  [shards(): tops = lax.all_to_all(top, SECOND, 0, 0, tiled=True)]
    ppermute x7, starting transfers between devices: 18.2 us -> 17.4 us  [far_swap(): lax.ppermute(value, axis, [(i, (i + 2 * (i % 2) - 1) % count) for i in ra...]
  transfers between devices with their start and end apart: 16 -> 16, of which waited for: 9 -> 8; matrix products, arithmetic and copies ran while one was open for 0% -> 0% of each run, Pallas kernels for 3% -> 3%
where the time goes in v4:
time: 57.3 us; the launch traced here: 57 us
  starting transfers between devices  28.8 us (50%)
  waiting for transfers between devices  18.8 us (33%)
  Pallas kernels  8.69 us (15%)
  between operations  0.75 us (1%)
    ppermute x7, starting transfers between devices, far_swap(): lax.ppermute(value, axis, [(i, (i + 2 * (i % 2) - 1) % count) for i in ra...  17.4 us
    ppermute x7, waiting for transfers between devices, far_swap(): lax.ppermute(value, axis, [(i, (i + 2 * (i % 2) - 1) % count) for i in ra...  10.3 us
    pallas_call x9, Pallas kernels, call(): pl.pallas_call(kernel, out_shape=[jax.ShapeDtypeStruct(o, F32) for o in o...  8.69 us
    all_to_all x1, starting transfers between devices, shards(): tops = lax.all_to_all(top, SECOND, 0, 0, tiled=True)  6.26 us
    all_to_all x1, waiting for transfers between devices, shards(): tops = lax.all_to_all(top, SECOND, 0, 0, tiled=True)  5.18 us
    all_to_all x1, starting transfers between devices, shards(): tops = lax.all_to_all(top, FIRST, 0, 0, tiled=True)  3.3 us
    all_to_all x1, waiting for transfers between devices, shards(): tops = lax.all_to_all(top, FIRST, 0, 0, tiled=True)  2.74 us
    ppermute x7, starting transfers between devices, near_swap(): lax.ppermute(value, axis, [(i, i ^ 1) for i in range(axis_count(axis))])  1.84 us
  transfers between devices with their start and end apart: 16, of which 8 were waited for; matrix products, arithmetic and copies ran while one was open for 0% of the time, Pallas kernels for 3%

profile of v4, /device:TPU:24, one launch (start us, length us, event | category | flops | bytes accessed | tf_op | source)
XLA Modules:
  0.0 57.0 jit_solution(7946079640364564692)
XLA Ops:
  0.7 1.9 %pack.1 = (f32[3,8,128]{2,1,0:T(8,128)}, f32[3,8,128]{2,1,0:T(8,128)}, f32[8,128]{1,0:T(8,128)}) custom-call(f32[27,2,2,128]{3,2,1,0:T(2,128)} %bitcast.11, f32[27,2,2,128]{3,2,1,0:T(2,128)} %bitcast.13, f32[3,4,4,256]{3,2,1,0:T(4,128)} %vel.1), custom_call_target="tpu_custom_call" | custom-call | tf_op jit(solution)/shard_map/pack/pallas_call | solution.py:741
  2.5 9.5 %collective-permute-start = (f32[3,8,128]{2,1,0:T(8,128)}, f32[3,8,128]{2,1,0:T(8,128)S(1)}, u32[]{:S(2)}, u32[]{:S(2)}) collective-permute-start(f32[3,8,128]{2,1,0:T(8,128)} %get-tuple-element.34), channel_id=1, source_target_pairs={{0,7},{1,2},{2,1},{3,4},{4,3},{5,6},{6,5},{7,0},{8,15},{9,10},{10,... | collective-permute-start | bytes 36872 | tf_op jit(solution)/shard_map/ppermute | solution.py:766
  12.0 3.3 %all-to-all-start = ((f32[8,1,128]{2,1,0:T(1,128)}), f32[8,1,128]{2,1,0:T(1,128)S(1)}, u32[]{:S(2)}, u32[]{:S(2)}) async-start(f32[8,1,128]{2,1,0:T(1,128)} %bitcast.3), calls=%async_computation | async-start | bytes 8192 | tf_op jit(solution)/shard_map/all_to_all | solution.py:794
  15.3 0.6 %collective-permute-done.1.from_near = f32[3,8,128]{2,1,0:T(8,128)S(1)} collective-permute-done((f32[3,8,128]{2,1,0:T(8,128)}, f32[3,8,128]{2,1,0:T(8,128)S(1)}, u32[]{:S(2)}, u32[]{:S(2)}) %collective-permute-start.1) | collective-permute-done | bytes 12320 | tf_op jit(solution)/shard_map/ppermute | solution.py:761
  15.9 0.6 %force.1 = (f32[2,27,8,128]{3,2,1,0:T(8,128)S(1)}, f32[12,2,8,128]{3,2,1,0:T(8,128)S(1)}, f32[4,9,2,8,128]{4,3,2,1,0:T(8,128)S(1)}, f32[39,8,128]{2,1,0:T(8,128)S(1)}, f32[39,8,128]{2,1,0:T(8,128)S(1)}) custom-call(f32[27,2,2,128]{3,2,1,0:T(2,128)S(1)} %bitcast.12, f32[27,2,2,128]{3,2,1,0:T(2,128)S(1)} %bitcast.14, f32[3,4,4,256]{3,2,1,0:T(4,128)S(1)} %copy-done.2, ...), custom_call_target="tpu_custom_call" | custom-call | tf_op jit(solution)/shard_map/force/pallas_call | solution.py:741
  16.9 1.0 %collective-permute-start.3 = (f32[39,8,128]{2,1,0:T(8,128)S(1)}, f32[39,8,128]{2,1,0:T(8,128)S(1)}, u32[]{:S(2)}, u32[]{:S(2)}) collective-permute-start(f32[39,8,128]{2,1,0:T(8,128)S(1)} %get-tuple-element.40), channel_id=1, source_target_pairs={{0,64},{64,0},{128,192},{192,128},{1,65},{65,1},{129,193},{193,129... | collective-permute-start | bytes 479240 | tf_op jit(solution)/shard_map/ppermute | solution.py:761
  17.8 2.7 %all-to-all-done = f32[8,1,128]{2,1,0:T(1,128)S(1)} async-done(((f32[8,1,128]{2,1,0:T(1,128)}), f32[8,1,128]{2,1,0:T(1,128)S(1)}, u32[]{:S(2)}, u32[]{:S(2)}) %all-to-all-start) | async-done | bytes 4128 | tf_op jit(solution)/shard_map/all_to_all | solution.py:794
  20.6 0.6 %top.1 = f32[32,128]{1,0:T(8,128)} custom-call(f32[8,128]{1,0:T(8,128)S(1)} %bitcast.16), custom_call_target="tpu_custom_call" | custom-call | flops 99999997952 | bytes 100000000 | tf_op jit(solution)/shard_map/top/pallas_call | solution.py:741
  21.2 6.3 %all-to-all-start.1 = ((f32[32,1,128]{2,1,0:T(1,128)}), f32[32,1,128]{2,1,0:T(1,128)S(1)}, u32[]{:S(2)}, u32[]{:S(2)}) async-start(f32[32,1,128]{2,1,0:T(1,128)} %bitcast.6), calls=%async_computation.1 | async-start | bytes 32768 | tf_op jit(solution)/shard_map/all_to_all | solution.py:796
  27.5 0.5 rim.1
  28.0 2.2 %collective-permute-start.4 = (f32[55,8,128]{2,1,0:T(8,128)S(1)}, f32[55,8,128]{2,1,0:T(8,128)S(1)}, u32[]{:S(2)}, u32[]{:S(2)}) collective-permute-start(f32[55,8,128]{2,1,0:T(8,128)S(1)} %get-tuple-element.47), channel_id=1, source_target_pairs={{0,56},{8,16},{16,8},{24,32},{32,24},{40,48},{48,40},{56,0},{1,57}... | collective-permute-start | bytes 675848 | tf_op jit(solution)/shard_map/ppermute | solution.py:766
  30.2 5.2 %all-to-all-done.1 = f32[32,1,128]{2,1,0:T(1,128)S(1)} async-done(((f32[32,1,128]{2,1,0:T(1,128)}), f32[32,1,128]{2,1,0:T(1,128)S(1)}, u32[]{:S(2)}, u32[]{:S(2)}) %all-to-all-start.1) | async-done | bytes 16416 | tf_op jit(solution)/shard_map/all_to_all | solution.py:796
  35.4 2.4 %collective-permute-done.4.from_far = f32[55,8,128]{2,1,0:T(8,128)S(1)} collective-permute-done((f32[55,8,128]{2,1,0:T(8,128)S(1)}, f32[55,8,128]{2,1,0:T(8,128)S(1)}, u32[]{:S(2)}, u32[]{:S(2)}) %collective-permute-start.4) | collective-permute-done | bytes 225312 | tf_op jit(solution)/shard_map/ppermute | solution.py:766
  37.8 1.3 %velocity.1 = (f32[3,4,4,256]{3,2,1,0:T(4,128)}, f32[5,27,8,128]{3,2,1,0:T(8,128)S(1)}, f32[3,27,8,128]{3,2,1,0:T(8,128)S(1)}, f32[5,9,8,128]{3,2,1,0:T(8,128)S(1)}, f32[2,5,9,8,128]{4,3,2,1,0:T(8,128)S(1)}) custom-call(f32[8,128]{1,0:T(8,128)S(1)} %step.1.scale, f32[4,9,2,8,128]{4,3,2,1,0:T(8,128)S(1)} %get-tuple-element.41.sums, ...), custom_call_target="tpu_custom_call" | custom-call | tf_op jit(solution)/shard_map/velocity/pallas_call | solution.py:741
  39.1 1.0 %stage_one.1 = (f32[5,27,8,128]{3,2,1,0:T(8,128)S(1)}, f32[13,8,128]{2,1,0:T(8,128)S(1)}, f32[13,8,128]{2,1,0:T(8,128)S(1)}, f32[13,8,128]{2,1,0:T(8,128)S(1)}, f32[13,8,128]{2,1,0:T(8,128)S(1)}) custom-call(f32[5,27,8,128]{3,2,1,0:T(8,128)S(1)} %get-tuple-element.50.refs_0_, f32[3,27,8,128]{3,2,1,0:T(8,128)S(1)} %get-tuple-element.51.refs_1_.refs_2_, ...), custom_call_target="tpu_custom_call" | custom-call | tf_op jit(solution)/shard_map/stage_one/pallas_call | solution.py:741
  40.2 1.1 %collective-permute-start.7 = (f32[13,8,128]{2,1,0:T(8,128)S(1)}, f32[13,8,128]{2,1,0:T(8,128)S(1)}, u32[]{:S(2)}, u32[]{:S(2)}) collective-permute-start(f32[13,8,128]{2,1,0:T(8,128)S(1)} %get-tuple-element.56), channel_id=1, source_target_pairs={{0,56},{8,16},{16,8},{24,32},{32,24},{40,48},{48,40},{56,0},{1,57}... | collective-permute-start | bytes 159752 | tf_op jit(solution)/shard_map/ppermute | solution.py:766
  41.3 0.9 %collective-permute-start.8 = (f32[13,8,128]{2,1,0:T(8,128)S(1)}, f32[13,8,128]{2,1,0:T(8,128)S(1)}, u32[]{:S(2)}, u32[]{:S(2)}) collective-permute-start(f32[13,8,128]{2,1,0:T(8,128)S(1)} %get-tuple-element.57), channel_id=1, source_target_pairs={{0,64},{64,0},{128,192},{192,128},{1,65},{65,1},{129,193},{193,129... | collective-permute-start | bytes 159752 | tf_op jit(solution)/shard_map/ppermute | solution.py:761
  42.2 3.3 %collective-permute-done.6.refs_4_ = f32[13,8,128]{2,1,0:T(8,128)S(1)} collective-permute-done((f32[13,8,128]{2,1,0:T(8,128)S(1)}, f32[13,8,128]{2,1,0:T(8,128)S(1)}, u32[]{:S(2)}, u32[]{:S(2)}) %collective-permute-start.6) | collective-permute-done | bytes 53280 | tf_op jit(solution)/shard_map/ppermute | solution.py:766
  45.7 1.1 %stage_two.1 = (f32[5,27,8,128]{3,2,1,0:T(8,128)S(1)}, f32[13,8,128]{2,1,0:T(8,128)S(1)}, f32[13,8,128]{2,1,0:T(8,128)S(1)}, f32[13,8,128]{2,1,0:T(8,128)S(1)}, f32[13,8,128]{2,1,0:T(8,128)S(1)}) custom-call(f32[5,27,8,128]{3,2,1,0:T(8,128)S(1)} %get-tuple-element.50.refs_0_, f32[5,27,8,128]{3,2,1,0:T(8,128)S(1)} %get-tuple-element.54.refs_1_, ...), custom_call_target="tpu_custom_call" | custom-call | tf_op jit(solution)/shard_map/stage_two/pallas_call | solution.py:741
  46.8 3.2 %collective-permute-start.10 = (f32[13,8,128]{2,1,0:T(8,128)S(1)}, f32[13,8,128]{2,1,0:T(8,128)S(1)}, u32[]{:S(2)}, u32[]{:S(2)}) collective-permute-start(f32[13,8,128]{2,1,0:T(8,128)S(1)} %get-tuple-element.60), channel_id=1, source_target_pairs={{0,192},{64,128},{128,64},{192,0},{1,193},{65,129},{129,65},{193,1... | collective-permute-start | bytes 159752 | tf_op jit(solution)/shard_map/ppermute | solution.py:766
  50.0 0.9 %collective-permute-start.11 = (f32[13,8,128]{2,1,0:T(8,128)S(1)}, f32[13,8,128]{2,1,0:T(8,128)S(1)}, u32[]{:S(2)}, u32[]{:S(2)}) collective-permute-start(f32[13,8,128]{2,1,0:T(8,128)S(1)} %get-tuple-element.61), channel_id=1, source_target_pairs={{0,56},{8,16},{16,8},{24,32},{32,24},{40,48},{48,40},{56,0},{1,57}... | collective-permute-start | bytes 159752 | tf_op jit(solution)/shard_map/ppermute | solution.py:766
  50.9 1.3 %collective-permute-done.10.refs_4_ = f32[13,8,128]{2,1,0:T(8,128)S(1)} collective-permute-done((f32[13,8,128]{2,1,0:T(8,128)S(1)}, f32[13,8,128]{2,1,0:T(8,128)S(1)}, u32[]{:S(2)}, u32[]{:S(2)}) %collective-permute-start.10) | collective-permute-done | bytes 53280 | tf_op jit(solution)/shard_map/ppermute | solution.py:766
  52.2 3.1 %collective-permute-done.11.refs_5_ = f32[13,8,128]{2,1,0:T(8,128)S(1)} collective-permute-done((f32[13,8,128]{2,1,0:T(8,128)S(1)}, f32[13,8,128]{2,1,0:T(8,128)S(1)}, u32[]{:S(2)}, u32[]{:S(2)}) %collective-permute-start.11) | collective-permute-done | bytes 53280 | tf_op jit(solution)/shard_map/ppermute | solution.py:766
  55.4 1.6 %stage_three.1 = f32[5,27,2,2,128]{4,3,2,1,0:T(2,128)} custom-call(f32[5,27,8,128]{3,2,1,0:T(8,128)S(1)} %get-tuple-element.50.refs_0_, f32[5,27,8,128]{3,2,1,0:T(8,128)S(1)} %get-tuple-element.59.refs_1_, f32[3,27,8,128]{3,2,1,0:T(8,128)S(1)} %get-tuple-element.51.refs_1_.refs_2_, f32[5,9,8,128]{3,2,1,0:T(8,128)S(1)} %get-tuple-element.52.refs_2_.refs_3_, ...), custom_call_target="tpu_custom_call" | custom-call | tf_op jit(solution)/shard_map/stage_three/pallas_call | solution.py:741
  (23 shorter events, 0.6 us)
Async XLA Ops:
  0.6 15.3 %copy-start = (f32[3,3,3,2,2,128]{5,4,3,2,1,0:T(2,128)S(1)}, f32[3,3,3,2,2,128]{5,4,3,2,1,0:T(2,128)}, u32[]{:S(2)}) copy-start(f32[3,3,3,2,2,128]{5,4,3,2,1,0:T(2,128)} %param.3) | copy-start | bytes 165892
  0.6 15.3 %copy-start.1 = (f32[3,3,3,2,2,128]{5,4,3,2,1,0:T(2,128)S(1)}, f32[3,3,3,2,2,128]{5,4,3,2,1,0:T(2,128)}, u32[]{:S(2)}) copy-start(f32[3,3,3,2,2,128]{5,4,3,2,1,0:T(2,128)} %param.4) | copy-start | bytes 165892
  0.6 15.3 %copy-start.2 = (f32[3,4,4,256]{3,2,1,0:T(4,128)S(1)}, f32[3,4,4,256]{3,2,1,0:T(4,128)}, u32[]{:S(2)}) copy-start(f32[3,4,4,256]{3,2,1,0:T(4,128)} %vel.1) | copy-start | bytes 147460
  2.5 12.8 %collective-permute-start = (f32[3,8,128]{2,1,0:T(8,128)}, f32[3,8,128]{2,1,0:T(8,128)S(1)}, u32[]{:S(2)}, u32[]{:S(2)}) collective-permute-start(f32[3,8,128]{2,1,0:T(8,128)} %get-tuple-element.34), channel_id=1, source_target_pairs={{0,7},{1,2},{2,1},{3,4},{4,3},{5,6},{6,5},{7,0},{8,15},{9,10},{10,... | collective-permute-start | bytes 36872 | tf_op jit(solution)/shard_map/ppermute | solution.py:766
  12.0 3.9 %collective-permute-start.1 = (f32[3,8,128]{2,1,0:T(8,128)}, f32[3,8,128]{2,1,0:T(8,128)S(1)}, u32[]{:S(2)}, u32[]{:S(2)}) collective-permute-start(f32[3,8,128]{2,1,0:T(8,128)} %get-tuple-element.35), channel_id=1, source_target_pairs={{0,1},{1,0},{2,3},{3,2},{4,5},{5,4},{6,7},{7,6},{8,9},{9,8},{10,11... | collective-permute-start | bytes 36872 | tf_op jit(solution)/shard_map/ppermute | solution.py:761
  12.0 8.6 %all-to-all-start = ((f32[8,1,128]{2,1,0:T(1,128)}), f32[8,1,128]{2,1,0:T(1,128)S(1)}, u32[]{:S(2)}, u32[]{:S(2)}) async-start(f32[8,1,128]{2,1,0:T(1,128)} %bitcast.3), calls=%async_computation | async-start | bytes 8192 | tf_op jit(solution)/shard_map/all_to_all | solution.py:794
  16.6 10.9 %collective-permute-start.2 = (f32[39,8,128]{2,1,0:T(8,128)S(1)}, f32[39,8,128]{2,1,0:T(8,128)S(1)}, u32[]{:S(2)}, u32[]{:S(2)}) collective-permute-start(f32[39,8,128]{2,1,0:T(8,128)S(1)} %get-tuple-element.39), channel_id=1, source_target_pairs={{0,192},{64,128},{128,64},{192,0},{1,193},{65,129},{129,65},{193,1... | collective-permute-start | bytes 479240 | tf_op jit(solution)/shard_map/ppermute | solution.py:766
  16.9 10.6 %collective-permute-start.3 = (f32[39,8,128]{2,1,0:T(8,128)S(1)}, f32[39,8,128]{2,1,0:T(8,128)S(1)}, u32[]{:S(2)}, u32[]{:S(2)}) collective-permute-start(f32[39,8,128]{2,1,0:T(8,128)S(1)} %get-tuple-element.40), channel_id=1, source_target_pairs={{0,64},{64,0},{128,192},{192,128},{1,65},{65,1},{129,193},{193,129... | collective-permute-start | bytes 479240 | tf_op jit(solution)/shard_map/ppermute | solution.py:761
  21.2 14.2 %all-to-all-start.1 = ((f32[32,1,128]{2,1,0:T(1,128)}), f32[32,1,128]{2,1,0:T(1,128)S(1)}, u32[]{:S(2)}, u32[]{:S(2)}) async-start(f32[32,1,128]{2,1,0:T(1,128)} %bitcast.6), calls=%async_computation.1 | async-start | bytes 32768 | tf_op jit(solution)/shard_map/all_to_all | solution.py:796
  28.0 9.8 %collective-permute-start.4 = (f32[55,8,128]{2,1,0:T(8,128)S(1)}, f32[55,8,128]{2,1,0:T(8,128)S(1)}, u32[]{:S(2)}, u32[]{:S(2)}) collective-permute-start(f32[55,8,128]{2,1,0:T(8,128)S(1)} %get-tuple-element.47), channel_id=1, source_target_pairs={{0,56},{8,16},{16,8},{24,32},{32,24},{40,48},{48,40},{56,0},{1,57}... | collective-permute-start | bytes 675848 | tf_op jit(solution)/shard_map/ppermute | solution.py:766
  30.2 7.6 %collective-permute-start.5 = (f32[55,8,128]{2,1,0:T(8,128)S(1)}, f32[55,8,128]{2,1,0:T(8,128)S(1)}, u32[]{:S(2)}, u32[]{:S(2)}) collective-permute-start(f32[55,8,128]{2,1,0:T(8,128)S(1)} %get-tuple-element.48), channel_id=1, source_target_pairs={{0,8},{8,0},{16,24},{24,16},{32,40},{40,32},{48,56},{56,48},{1,9},... | collective-permute-start | bytes 675848 | tf_op jit(solution)/shard_map/ppermute | solution.py:761
  40.1 5.4 %collective-permute-start.6 = (f32[13,8,128]{2,1,0:T(8,128)S(1)}, f32[13,8,128]{2,1,0:T(8,128)S(1)}, u32[]{:S(2)}, u32[]{:S(2)}) collective-permute-start(f32[13,8,128]{2,1,0:T(8,128)S(1)} %get-tuple-element.55), channel_id=1, source_target_pairs={{0,192},{64,128},{128,64},{192,0},{1,193},{65,129},{129,65},{193,1... | collective-permute-start | bytes 159752 | tf_op jit(solution)/shard_map/ppermute | solution.py:766
  40.2 5.4 %collective-permute-start.7 = (f32[13,8,128]{2,1,0:T(8,128)S(1)}, f32[13,8,128]{2,1,0:T(8,128)S(1)}, u32[]{:S(2)}, u32[]{:S(2)}) collective-permute-start(f32[13,8,128]{2,1,0:T(8,128)S(1)} %get-tuple-element.56), channel_id=1, source_target_pairs={{0,56},{8,16},{16,8},{24,32},{32,24},{40,48},{48,40},{56,0},{1,57}... | collective-permute-start | bytes 159752 | tf_op jit(solution)/shard_map/ppermute | solution.py:766
  41.3 4.3 %collective-permute-start.8 = (f32[13,8,128]{2,1,0:T(8,128)S(1)}, f32[13,8,128]{2,1,0:T(8,128)S(1)}, u32[]{:S(2)}, u32[]{:S(2)}) collective-permute-start(f32[13,8,128]{2,1,0:T(8,128)S(1)} %get-tuple-element.57), channel_id=1, source_target_pairs={{0,64},{64,0},{128,192},{192,128},{1,65},{65,1},{129,193},{193,129... | collective-permute-start | bytes 159752 | tf_op jit(solution)/shard_map/ppermute | solution.py:761
  42.2 3.5 %collective-permute-start.9 = (f32[13,8,128]{2,1,0:T(8,128)S(1)}, f32[13,8,128]{2,1,0:T(8,128)S(1)}, u32[]{:S(2)}, u32[]{:S(2)}) collective-permute-start(f32[13,8,128]{2,1,0:T(8,128)S(1)} %get-tuple-element.58), channel_id=1, source_target_pairs={{0,8},{8,0},{16,24},{24,16},{32,40},{40,32},{48,56},{56,48},{1,9},... | collective-permute-start | bytes 159752 | tf_op jit(solution)/shard_map/ppermute | solution.py:761
  46.8 5.4 %collective-permute-start.10 = (f32[13,8,128]{2,1,0:T(8,128)S(1)}, f32[13,8,128]{2,1,0:T(8,128)S(1)}, u32[]{:S(2)}, u32[]{:S(2)}) collective-permute-start(f32[13,8,128]{2,1,0:T(8,128)S(1)} %get-tuple-element.60), channel_id=1, source_target_pairs={{0,192},{64,128},{128,64},{192,0},{1,193},{65,129},{129,65},{193,1... | collective-permute-start | bytes 159752 | tf_op jit(solution)/shard_map/ppermute | solution.py:766
  50.0 5.4 %collective-permute-start.11 = (f32[13,8,128]{2,1,0:T(8,128)S(1)}, f32[13,8,128]{2,1,0:T(8,128)S(1)}, u32[]{:S(2)}, u32[]{:S(2)}) collective-permute-start(f32[13,8,128]{2,1,0:T(8,128)S(1)} %get-tuple-element.61), channel_id=1, source_target_pairs={{0,56},{8,16},{16,8},{24,32},{32,24},{40,48},{48,40},{56,0},{1,57}... | collective-permute-start | bytes 159752 | tf_op jit(solution)/shard_map/ppermute | solution.py:766
  50.9 4.5 %collective-permute-start.12 = (f32[13,8,128]{2,1,0:T(8,128)S(1)}, f32[13,8,128]{2,1,0:T(8,128)S(1)}, u32[]{:S(2)}, u32[]{:S(2)}) collective-permute-start(f32[13,8,128]{2,1,0:T(8,128)S(1)} %get-tuple-element.62), channel_id=1, source_target_pairs={{0,64},{64,0},{128,192},{192,128},{1,65},{65,1},{129,193},{193,129... | collective-permute-start | bytes 159752 | tf_op jit(solution)/shard_map/ppermute | solution.py:761
  50.9 4.5 %collective-permute-start.13 = (f32[13,8,128]{2,1,0:T(8,128)S(1)}, f32[13,8,128]{2,1,0:T(8,128)S(1)}, u32[]{:S(2)}, u32[]{:S(2)}) collective-permute-start(f32[13,8,128]{2,1,0:T(8,128)S(1)} %get-tuple-element.63), channel_id=1, source_target_pairs={{0,8},{8,0},{16,24},{24,16},{32,40},{40,32},{48,56},{56,48},{1,9},... | collective-permute-start | bytes 159752 | tf_op jit(solution)/shard_map/ppermute | solution.py:761

commit v5 on v4

--- a/solution.py
+++ b/solution.py
@@ -251,11 +251,11 @@
 
 def y_keys(high):
     keys = [("sum", f, a, b, z) for f in FIELDS for a in TRIPLE for b in TRIPLE for z in PAIR]
-    keys += [("side", f, a, z) for f in FIELDS for a in TRIPLE for z in PAIR]
+    keys += [("side", f, a, z) for f in FIELDS for a in ("mid", "far") for z in PAIR]
     nodes = 2 if high else 3
     keys += [("old", d, a, b, z) for d in TRIPLE for a in TRIPLE for b in range(nodes) for z in PAIR]
     if not high:
-        keys += [("old_side", d, a, z) for d in TRIPLE for a in TRIPLE for z in PAIR]
+        keys += [("old_side", d, a, z) for d in TRIPLE for a in ("mid", "far") for z in PAIR]
     return keys + side_keys()
 
 
@@ -474,7 +474,11 @@
                         line[2] = line[2] + roll_rows(line[0], -1)
                     for b in TRIPLE:
                         values["sum", f, a, b, z] = line[b]
-                    values["side", f, a, z] = sums_x[f, 3 * a + (2 if high else 0), z]
+        for f in FIELDS:
+            b = 2 if high else 0
+            for z in PAIR:
+                values["side", f, "mid", z] = sums_x[f, 3 + b, z]
+                values["side", f, "far", z] = sh.beside(sums_x[f, 6 + b, z], sums_x[f, b, z], 2)
         for d in TRIPLE:
             for a in TRIPLE:
                 for z in PAIR:
@@ -482,7 +486,9 @@
                     values["old", d, a, 0, z] = first
                     values["old", d, a, 1, z] = old[d, 2 * a + 1, z]
                     values["old", d, a, 2, z] = roll_rows(first, -1)
-                    values["old_side", d, a, z] = old_x[d, 2 * a, z]
+            for z in PAIR:
+                values["old_side", d, "mid", z] = old_x[d, 2, z]
+                values["old_side", d, "far", z] = sh.beside(old_x[d, 4, z], old_x[d, 0, z], 2)
         lists.append([values[key] for key in y_keys(high)])
     write_messages(sh, even_along(GY), near, far, *lists, 1)
 
@@ -503,6 +509,14 @@
 
     def beside(*key):
         return sh.beside(up(key), down(key), 1)
+
+    def aside_of(get, kind, a, own, f, z):
+        if a == 1:
+            return get((kind, f, "mid", z))
+        far = get((kind, f, "far", z))
+        if a == 0:
+            return sh.beside(roll_rows(own(2), -2), far, 2)
+        return sh.beside(far, roll_rows(own(0), 2), 2)
 
     centre = [{} for _ in TRIPLE]
     side_x = [{} for _ in TRIPLE]
@@ -515,9 +529,17 @@
                 inner, outer = assemble(sh, own, [beside("sum", f, a, b, z) for b in TRIPLE], 1)
                 aside = [sums_x[f, 3 * a + b, z] for b in TRIPLE]
                 aside = [
-                    aside[0] + sh.before(down(("side", f, a, z)), aside[2], 1),
+                    aside[0] + sh.before(
+                        aside_of(down, "side", a, lambda n: down(("sum", f, n, 2, z)), f, z),
+                        aside[2],
+                        1,
+                    ),
                     aside[1],
-                    aside[2] + sh.before(aside[0], up(("side", f, a, z)), 1),
+                    aside[2] + sh.before(
+                        aside[0],
+                        aside_of(up, "side", a, lambda n: up(("sum", f, n, 0, z)), f, z),
+                        1,
+                    ),
                 ]
                 total.append((inner, aside, outer))
             for d in TRIPLE:
@@ -529,7 +551,11 @@
                     [
                         first_x,
                         old_x[d, 2 * a + 1, z],
-                        sh.before(first_x, up(("old_side", d, a, z)), 1),
+                        sh.before(
+                            first_x,
+                            aside_of(up, "old_side", a, lambda n: up(("old", d, n, 0, z)), d, z),
+                            1,
+                        ),
                     ],
                     [
                         beyond,
@@ -736,6 +762,13 @@
             write_messages(sh, even[d], outs[1 + 2 * d], outs[2 + 2 * d], *lists, 2 - d)
 
 
+def velocity_stage_kernel(*refs):
+    operands, results, stage, scratch = refs[:10], refs[10:14], refs[14:19], refs[19:]
+    sides, *work, traces = scratch
+    velocity_kernel(*operands, *results, sides, *work)
+    stage_kernel(None, False, *results[1:], sides, *stage, traces)
+
+
 def call(kernel, outs, *args, scratch=(), name=None, weigh=None, far=False, stored=()):
     space = pltpu.HBM if far else pltpu.VMEM
     return pl.pallas_call(
@@ -820,32 +853,29 @@
     far = far_swap(far, GY)
     near = near_swap(near, GY)
     state = (5, 27) + tile
-    new_velocity, u0, disp, speeds, sides = call(
-        velocity_kernel,
-        [velocity.shape, state, (3, 27) + tile, (5, 9) + tile, (2, 5, 9) + tile],
-        step, sums, sums_x, old, old_x, rho, rho_x, heat_x, far, near,
-        scratch=[(6, 16, 128), (6, 8, 256), velocity.shape, pltpu.SemaphoreType.DMA],
-        stored=(0,),
-        name="velocity",
-    )
     faces = [(message_size(FACE_KEYS),) + tile] * 4
     held = (4, 5, 9) + tile
-    one, *messages = call(
-        functools.partial(stage_kernel, None, False), [state] + faces,
-        u0, disp, speeds, sides,
-        scratch=[held],
-        name="stage_one",
+    sides = (2, 5, 9) + tile
+    new_velocity, u0, disp, speeds, one, *messages = call(
+        velocity_stage_kernel,
+        [velocity.shape, state, (3, 27) + tile, (5, 9) + tile, state] + faces,
+        step, sums, sums_x, old, old_x, rho, rho_x, heat_x, far, near,
+        scratch=[
+            sides, (6, 16, 128), (6, 8, 256), velocity.shape, pltpu.SemaphoreType.DMA, held,
+        ],
+        stored=(0,),
+        name="velocity_stage_one",
     )
     two, *messages = call(
         functools.partial(stage_kernel, 0.25, False), [state] + faces,
         u0, one, disp, speeds, *exchange(*messages),
-        scratch=[held, sides.shape],
+        scratch=[held, sides],
         name="stage_two",
     )
     (remapped,) = call(
         functools.partial(stage_kernel, 2.0 / 3.0, True), [(5, 27) + density.shape[3:]],
         u0, two, disp, speeds, *exchange(*messages),
-        scratch=[sides.shape, (5, 27) + density.shape[3:], pltpu.SemaphoreType.DMA((5,))],
+        scratch=[sides, (5, 27) + density.shape[3:], pltpu.SemaphoreType.DMA((5,))],
         stored=(0,),
         name="stage_three",
     )

time: 57.3 us -> 56.8 us (level)
    pallas_call x9 -> x8, Pallas kernels: 8.69 us -> 8.55 us  [call(): pl.pallas_call(kernel, out_shape=[jax.ShapeDtypeStruct(o, F32) for o in o...]
where the time goes in v5:
time: 56.8 us; the launch traced here: 56.5 us
  starting transfers between devices  28.8 us (51%)
  waiting for transfers between devices  18.4 us (32%)
  Pallas kernels  8.55 us (15%)
  between operations  0.75 us (1%)
    ppermute x7, starting transfers between devices, far_swap(): lax.ppermute(value, axis, [(i, (i + 2 * (i % 2) - 1) % count) for i in ra...  17.4 us
    ppermute x7, waiting for transfers between devices, far_swap(): lax.ppermute(value, axis, [(i, (i + 2 * (i % 2) - 1) % count) for i in ra...  9.93 us
    pallas_call x8, Pallas kernels, call(): pl.pallas_call(kernel, out_shape=[jax.ShapeDtypeStruct(o, F32) for o in o...  8.55 us
    all_to_all x1, starting transfers between devices, shards(): tops = lax.all_to_all(top, SECOND, 0, 0, tiled=True)  6.26 us
    all_to_all x1, waiting for transfers between devices, shards(): tops = lax.all_to_all(top, SECOND, 0, 0, tiled=True)  5.19 us
    all_to_all x1, starting transfers between devices, shards(): tops = lax.all_to_all(top, FIRST, 0, 0, tiled=True)  3.33 us
    all_to_all x1, waiting for transfers between devices, shards(): tops = lax.all_to_all(top, FIRST, 0, 0, tiled=True)  2.75 us
    ppermute x7, starting transfers between devices, near_swap(): lax.ppermute(value, axis, [(i, i ^ 1) for i in range(axis_count(axis))])  1.84 us
  transfers between devices with their start and end apart: 16, of which 8 were waited for; matrix products, arithmetic and copies ran while one was open for 0% of the time, Pallas kernels for 3%

profile of v5, /device:TPU:24, one launch (start us, length us, event | category | flops | bytes accessed | tf_op | source)
XLA Modules:
  0.0 56.5 jit_solution(924502211863919858)
XLA Ops:
  0.7 1.9 %pack.1 = (f32[3,8,128]{2,1,0:T(8,128)}, f32[3,8,128]{2,1,0:T(8,128)}, f32[8,128]{1,0:T(8,128)}) custom-call(f32[27,2,2,128]{3,2,1,0:T(2,128)} %bitcast.11, f32[27,2,2,128]{3,2,1,0:T(2,128)} %bitcast.13, f32[3,4,4,256]{3,2,1,0:T(4,128)} %vel.1), custom_call_target="tpu_custom_call" | custom-call | tf_op jit(solution)/shard_map/pack/pallas_call | solution.py:774
  2.5 9.5 %collective-permute-start = (f32[3,8,128]{2,1,0:T(8,128)}, f32[3,8,128]{2,1,0:T(8,128)S(1)}, u32[]{:S(2)}, u32[]{:S(2)}) collective-permute-start(f32[3,8,128]{2,1,0:T(8,128)} %get-tuple-element.33), channel_id=1, source_target_pairs={{0,7},{1,2},{2,1},{3,4},{4,3},{5,6},{6,5},{7,0},{8,15},{9,10},{10,... | collective-permute-start | bytes 36872 | tf_op jit(solution)/shard_map/ppermute | solution.py:799
  12.0 3.3 %all-to-all-start = ((f32[8,1,128]{2,1,0:T(1,128)}), f32[8,1,128]{2,1,0:T(1,128)S(1)}, u32[]{:S(2)}, u32[]{:S(2)}) async-start(f32[8,1,128]{2,1,0:T(1,128)} %bitcast.3), calls=%async_computation | async-start | bytes 8192 | tf_op jit(solution)/shard_map/all_to_all | solution.py:827
  15.4 0.5 collective-permute-done.1.from_near
  15.9 0.6 %force.1 = (f32[2,27,8,128]{3,2,1,0:T(8,128)S(1)}, f32[12,2,8,128]{3,2,1,0:T(8,128)S(1)}, f32[4,9,2,8,128]{4,3,2,1,0:T(8,128)S(1)}, f32[39,8,128]{2,1,0:T(8,128)S(1)}, f32[39,8,128]{2,1,0:T(8,128)S(1)}) custom-call(f32[27,2,2,128]{3,2,1,0:T(2,128)S(1)} %bitcast.12, f32[27,2,2,128]{3,2,1,0:T(2,128)S(1)} %bitcast.14, f32[3,4,4,256]{3,2,1,0:T(4,128)S(1)} %copy-done.2, ...), custom_call_target="tpu_custom_call" | custom-call | tf_op jit(solution)/shard_map/force/pallas_call | solution.py:774
  16.6 0.3 collective-permute-start.2
  16.9 1.0 %collective-permute-start.3 = (f32[39,8,128]{2,1,0:T(8,128)S(1)}, f32[39,8,128]{2,1,0:T(8,128)S(1)}, u32[]{:S(2)}, u32[]{:S(2)}) collective-permute-start(f32[39,8,128]{2,1,0:T(8,128)S(1)} %get-tuple-element.39), channel_id=1, source_target_pairs={{0,64},{64,0},{128,192},{192,128},{1,65},{65,1},{129,193},{193,129... | collective-permute-start | bytes 479240 | tf_op jit(solution)/shard_map/ppermute | solution.py:794
  17.8 2.7 %all-to-all-done = f32[8,1,128]{2,1,0:T(1,128)S(1)} async-done(((f32[8,1,128]{2,1,0:T(1,128)}), f32[8,1,128]{2,1,0:T(1,128)S(1)}, u32[]{:S(2)}, u32[]{:S(2)}) %all-to-all-start) | async-done | bytes 4128 | tf_op jit(solution)/shard_map/all_to_all | solution.py:827
  20.6 0.6 %top.1 = f32[32,128]{1,0:T(8,128)} custom-call(f32[8,128]{1,0:T(8,128)S(1)} %bitcast.16), custom_call_target="tpu_custom_call" | custom-call | flops 99999997952 | bytes 100000000 | tf_op jit(solution)/shard_map/top/pallas_call | solution.py:774
  21.2 6.3 %all-to-all-start.1 = ((f32[32,1,128]{2,1,0:T(1,128)}), f32[32,1,128]{2,1,0:T(1,128)S(1)}, u32[]{:S(2)}, u32[]{:S(2)}) async-start(f32[32,1,128]{2,1,0:T(1,128)} %bitcast.6), calls=%async_computation.1 | async-start | bytes 32768 | tf_op jit(solution)/shard_map/all_to_all | solution.py:829
  27.5 0.5 rim.1
  28.0 2.2 %collective-permute-start.4 = (f32[51,8,128]{2,1,0:T(8,128)S(1)}, f32[51,8,128]{2,1,0:T(8,128)S(1)}, u32[]{:S(2)}, u32[]{:S(2)}) collective-permute-start(f32[51,8,128]{2,1,0:T(8,128)S(1)} %get-tuple-element.46), channel_id=1, source_target_pairs={{0,56},{8,16},{16,8},{24,32},{32,24},{40,48},{48,40},{56,0},{1,57}... | collective-permute-start | bytes 626696 | tf_op jit(solution)/shard_map/ppermute | solution.py:799
  30.2 5.2 %all-to-all-done.1 = f32[32,1,128]{2,1,0:T(1,128)S(1)} async-done(((f32[32,1,128]{2,1,0:T(1,128)}), f32[32,1,128]{2,1,0:T(1,128)S(1)}, u32[]{:S(2)}, u32[]{:S(2)}) %all-to-all-start.1) | async-done | bytes 16416 | tf_op jit(solution)/shard_map/all_to_all | solution.py:829
  35.4 2.0 %collective-permute-done.4.refs_8_ = f32[51,8,128]{2,1,0:T(8,128)S(1)} collective-permute-done((f32[51,8,128]{2,1,0:T(8,128)S(1)}, f32[51,8,128]{2,1,0:T(8,128)S(1)}, u32[]{:S(2)}, u32[]{:S(2)}) %collective-permute-start.4) | collective-permute-done | bytes 208928 | tf_op jit(solution)/shard_map/ppermute | solution.py:799
  37.4 2.2 %velocity_stage_one.1 = (f32[3,4,4,256]{3,2,1,0:T(4,128)}, f32[5,27,8,128]{3,2,1,0:T(8,128)S(1)}, f32[3,27,8,128]{3,2,1,0:T(8,128)S(1)}, f32[5,9,8,128]{3,2,1,0:...) custom-call(f32[8,128]{1,0:T(8,128)S(1)} %step.1.refs_0_, ...), custom_call_target="tpu_custom_call" | custom-call | tf_op jit(solution)/shard_map/velocity_stage_one/pallas_call | solution.py:774
  39.8 1.1 %collective-permute-start.7 = (f32[13,8,128]{2,1,0:T(8,128)S(1)}, f32[13,8,128]{2,1,0:T(8,128)S(1)}, u32[]{:S(2)}, u32[]{:S(2)}) collective-permute-start(f32[13,8,128]{2,1,0:T(8,128)S(1)} %get-tuple-element.54), channel_id=1, source_target_pairs={{0,56},{8,16},{16,8},{24,32},{32,24},{40,48},{48,40},{56,0},{1,57}... | collective-permute-start | bytes 159752 | tf_op jit(solution)/shard_map/ppermute | solution.py:799
  40.9 0.9 %collective-permute-start.8 = (f32[13,8,128]{2,1,0:T(8,128)S(1)}, f32[13,8,128]{2,1,0:T(8,128)S(1)}, u32[]{:S(2)}, u32[]{:S(2)}) collective-permute-start(f32[13,8,128]{2,1,0:T(8,128)S(1)} %get-tuple-element.55), channel_id=1, source_target_pairs={{0,64},{64,0},{128,192},{192,128},{1,65},{65,1},{129,193},{193,129... | collective-permute-start | bytes 159752 | tf_op jit(solution)/shard_map/ppermute | solution.py:794
  41.7 3.3 %collective-permute-done.6.refs_4_ = f32[13,8,128]{2,1,0:T(8,128)S(1)} collective-permute-done((f32[13,8,128]{2,1,0:T(8,128)S(1)}, f32[13,8,128]{2,1,0:T(8,128)S(1)}, u32[]{:S(2)}, u32[]{:S(2)}) %collective-permute-start.6) | collective-permute-done | bytes 53280 | tf_op jit(solution)/shard_map/ppermute | solution.py:799
  45.2 1.1 %stage_two.1 = (f32[5,27,8,128]{3,2,1,0:T(8,128)S(1)}, f32[13,8,128]{2,1,0:T(8,128)S(1)}, f32[13,8,128]{2,1,0:T(8,128)S(1)}, f32[13,8,128]{2,1,0:T(8,128)S(1)}, f32[13,8,128]{2,1,0:T(8,128)S(1)}) custom-call(f32[5,27,8,128]{3,2,1,0:T(8,128)S(1)} %get-tuple-element.49.refs_0_, f32[5,27,8,128]{3,2,1,0:T(8,128)S(1)} %get-tuple-element.50.refs_1_, ...), custom_call_target="tpu_custom_call" | custom-call | tf_op jit(solution)/shard_map/stage_two/pallas_call | solution.py:774
  46.3 3.2 %collective-permute-start.10 = (f32[13,8,128]{2,1,0:T(8,128)S(1)}, f32[13,8,128]{2,1,0:T(8,128)S(1)}, u32[]{:S(2)}, u32[]{:S(2)}) collective-permute-start(f32[13,8,128]{2,1,0:T(8,128)S(1)} %get-tuple-element.58), channel_id=1, source_target_pairs={{0,192},{64,128},{128,64},{192,0},{1,193},{65,129},{129,65},{193,1... | collective-permute-start | bytes 159752 | tf_op jit(solution)/shard_map/ppermute | solution.py:799
  49.6 0.9 %collective-permute-start.11 = (f32[13,8,128]{2,1,0:T(8,128)S(1)}, f32[13,8,128]{2,1,0:T(8,128)S(1)}, u32[]{:S(2)}, u32[]{:S(2)}) collective-permute-start(f32[13,8,128]{2,1,0:T(8,128)S(1)} %get-tuple-element.59), channel_id=1, source_target_pairs={{0,56},{8,16},{16,8},{24,32},{32,24},{40,48},{48,40},{56,0},{1,57}... | collective-permute-start | bytes 159752 | tf_op jit(solution)/shard_map/ppermute | solution.py:799
  50.5 1.3 %collective-permute-done.10.refs_4_ = f32[13,8,128]{2,1,0:T(8,128)S(1)} collective-permute-done((f32[13,8,128]{2,1,0:T(8,128)S(1)}, f32[13,8,128]{2,1,0:T(8,128)S(1)}, u32[]{:S(2)}, u32[]{:S(2)}) %collective-permute-start.10) | collective-permute-done | bytes 53280 | tf_op jit(solution)/shard_map/ppermute | solution.py:799
  51.8 3.1 %collective-permute-done.11.refs_5_ = f32[13,8,128]{2,1,0:T(8,128)S(1)} collective-permute-done((f32[13,8,128]{2,1,0:T(8,128)S(1)}, f32[13,8,128]{2,1,0:T(8,128)S(1)}, u32[]{:S(2)}, u32[]{:S(2)}) %collective-permute-start.11) | collective-permute-done | bytes 53280 | tf_op jit(solution)/shard_map/ppermute | solution.py:799
  54.9 1.6 %stage_three.1 = f32[5,27,2,2,128]{4,3,2,1,0:T(2,128)} custom-call(f32[5,27,8,128]{3,2,1,0:T(8,128)S(1)} %get-tuple-element.49.refs_0_, f32[5,27,8,128]{3,2,1,0:T(8,128)S(1)} %get-tuple-element.57.refs_1_, f32[3,27,8,128]{3,2,1,0:T(8,128)S(1)} %get-tuple-element.51.refs_2_, f32[5,9,8,128]{3,2,1,0:T(8,128)S(1)} %get-tuple-element.52.refs_3_, ...), custom_call_target="tpu_custom_call" | custom-call | tf_op jit(solution)/shard_map/stage_three/pallas_call | solution.py:774
  (22 shorter events, 0.3 us)
Async XLA Ops:
  0.6 15.3 %copy-start = (f32[3,3,3,2,2,128]{5,4,3,2,1,0:T(2,128)S(1)}, f32[3,3,3,2,2,128]{5,4,3,2,1,0:T(2,128)}, u32[]{:S(2)}) copy-start(f32[3,3,3,2,2,128]{5,4,3,2,1,0:T(2,128)} %param.3) | copy-start | bytes 165892
  0.6 15.3 %copy-start.1 = (f32[3,3,3,2,2,128]{5,4,3,2,1,0:T(2,128)S(1)}, f32[3,3,3,2,2,128]{5,4,3,2,1,0:T(2,128)}, u32[]{:S(2)}) copy-start(f32[3,3,3,2,2,128]{5,4,3,2,1,0:T(2,128)} %param.4) | copy-start | bytes 165892
  0.6 15.3 %copy-start.2 = (f32[3,4,4,256]{3,2,1,0:T(4,128)S(1)}, f32[3,4,4,256]{3,2,1,0:T(4,128)}, u32[]{:S(2)}) copy-start(f32[3,4,4,256]{3,2,1,0:T(4,128)} %vel.1) | copy-start | bytes 147460
  2.5 12.8 %collective-permute-start = (f32[3,8,128]{2,1,0:T(8,128)}, f32[3,8,128]{2,1,0:T(8,128)S(1)}, u32[]{:S(2)}, u32[]{:S(2)}) collective-permute-start(f32[3,8,128]{2,1,0:T(8,128)} %get-tuple-element.33), channel_id=1, source_target_pairs={{0,7},{1,2},{2,1},{3,4},{4,3},{5,6},{6,5},{7,0},{8,15},{9,10},{10,... | collective-permute-start | bytes 36872 | tf_op jit(solution)/shard_map/ppermute | solution.py:799
  12.0 3.9 %collective-permute-start.1 = (f32[3,8,128]{2,1,0:T(8,128)}, f32[3,8,128]{2,1,0:T(8,128)S(1)}, u32[]{:S(2)}, u32[]{:S(2)}) collective-permute-start(f32[3,8,128]{2,1,0:T(8,128)} %get-tuple-element.34), channel_id=1, source_target_pairs={{0,1},{1,0},{2,3},{3,2},{4,5},{5,4},{6,7},{7,6},{8,9},{9,8},{10,11... | collective-permute-start | bytes 36872 | tf_op jit(solution)/shard_map/ppermute | solution.py:794
  12.0 8.6 %all-to-all-start = ((f32[8,1,128]{2,1,0:T(1,128)}), f32[8,1,128]{2,1,0:T(1,128)S(1)}, u32[]{:S(2)}, u32[]{:S(2)}) async-start(f32[8,1,128]{2,1,0:T(1,128)} %bitcast.3), calls=%async_computation | async-start | bytes 8192 | tf_op jit(solution)/shard_map/all_to_all | solution.py:827
  16.6 10.9 %collective-permute-start.2 = (f32[39,8,128]{2,1,0:T(8,128)S(1)}, f32[39,8,128]{2,1,0:T(8,128)S(1)}, u32[]{:S(2)}, u32[]{:S(2)}) collective-permute-start(f32[39,8,128]{2,1,0:T(8,128)S(1)} %get-tuple-element.38), channel_id=1, source_target_pairs={{0,192},{64,128},{128,64},{192,0},{1,193},{65,129},{129,65},{193,1... | collective-permute-start | bytes 479240 | tf_op jit(solution)/shard_map/ppermute | solution.py:799
  16.9 10.6 %collective-permute-start.3 = (f32[39,8,128]{2,1,0:T(8,128)S(1)}, f32[39,8,128]{2,1,0:T(8,128)S(1)}, u32[]{:S(2)}, u32[]{:S(2)}) collective-permute-start(f32[39,8,128]{2,1,0:T(8,128)S(1)} %get-tuple-element.39), channel_id=1, source_target_pairs={{0,64},{64,0},{128,192},{192,128},{1,65},{65,1},{129,193},{193,129... | collective-permute-start | bytes 479240 | tf_op jit(solution)/shard_map/ppermute | solution.py:794
  21.2 14.2 %all-to-all-start.1 = ((f32[32,1,128]{2,1,0:T(1,128)}), f32[32,1,128]{2,1,0:T(1,128)S(1)}, u32[]{:S(2)}, u32[]{:S(2)}) async-start(f32[32,1,128]{2,1,0:T(1,128)} %bitcast.6), calls=%async_computation.1 | async-start | bytes 32768 | tf_op jit(solution)/shard_map/all_to_all | solution.py:829
  28.0 9.5 %collective-permute-start.4 = (f32[51,8,128]{2,1,0:T(8,128)S(1)}, f32[51,8,128]{2,1,0:T(8,128)S(1)}, u32[]{:S(2)}, u32[]{:S(2)}) collective-permute-start(f32[51,8,128]{2,1,0:T(8,128)S(1)} %get-tuple-element.46), channel_id=1, source_target_pairs={{0,56},{8,16},{16,8},{24,32},{32,24},{40,48},{48,40},{56,0},{1,57}... | collective-permute-start | bytes 626696 | tf_op jit(solution)/shard_map/ppermute | solution.py:799
  30.2 7.2 %collective-permute-start.5 = (f32[51,8,128]{2,1,0:T(8,128)S(1)}, f32[51,8,128]{2,1,0:T(8,128)S(1)}, u32[]{:S(2)}, u32[]{:S(2)}) collective-permute-start(f32[51,8,128]{2,1,0:T(8,128)S(1)} %get-tuple-element.47), channel_id=1, source_target_pairs={{0,8},{8,0},{16,24},{24,16},{32,40},{40,32},{48,56},{56,48},{1,9},... | collective-permute-start | bytes 626696 | tf_op jit(solution)/shard_map/ppermute | solution.py:794
  39.6 5.4 %collective-permute-start.6 = (f32[13,8,128]{2,1,0:T(8,128)S(1)}, f32[13,8,128]{2,1,0:T(8,128)S(1)}, u32[]{:S(2)}, u32[]{:S(2)}) collective-permute-start(f32[13,8,128]{2,1,0:T(8,128)S(1)} %get-tuple-element.53), channel_id=1, source_target_pairs={{0,192},{64,128},{128,64},{192,0},{1,193},{65,129},{129,65},{193,1... | collective-permute-start | bytes 159752 | tf_op jit(solution)/shard_map/ppermute | solution.py:799
  39.8 5.4 %collective-permute-start.7 = (f32[13,8,128]{2,1,0:T(8,128)S(1)}, f32[13,8,128]{2,1,0:T(8,128)S(1)}, u32[]{:S(2)}, u32[]{:S(2)}) collective-permute-start(f32[13,8,128]{2,1,0:T(8,128)S(1)} %get-tuple-element.54), channel_id=1, source_target_pairs={{0,56},{8,16},{16,8},{24,32},{32,24},{40,48},{48,40},{56,0},{1,57}... | collective-permute-start | bytes 159752 | tf_op jit(solution)/shard_map/ppermute | solution.py:799
  40.9 4.3 %collective-permute-start.8 = (f32[13,8,128]{2,1,0:T(8,128)S(1)}, f32[13,8,128]{2,1,0:T(8,128)S(1)}, u32[]{:S(2)}, u32[]{:S(2)}) collective-permute-start(f32[13,8,128]{2,1,0:T(8,128)S(1)} %get-tuple-element.55), channel_id=1, source_target_pairs={{0,64},{64,0},{128,192},{192,128},{1,65},{65,1},{129,193},{193,129... | collective-permute-start | bytes 159752 | tf_op jit(solution)/shard_map/ppermute | solution.py:794
  41.7 3.5 %collective-permute-start.9 = (f32[13,8,128]{2,1,0:T(8,128)S(1)}, f32[13,8,128]{2,1,0:T(8,128)S(1)}, u32[]{:S(2)}, u32[]{:S(2)}) collective-permute-start(f32[13,8,128]{2,1,0:T(8,128)S(1)} %get-tuple-element.56), channel_id=1, source_target_pairs={{0,8},{8,0},{16,24},{24,16},{32,40},{40,32},{48,56},{56,48},{1,9},... | collective-permute-start | bytes 159752 | tf_op jit(solution)/shard_map/ppermute | solution.py:794
  46.3 5.4 %collective-permute-start.10 = (f32[13,8,128]{2,1,0:T(8,128)S(1)}, f32[13,8,128]{2,1,0:T(8,128)S(1)}, u32[]{:S(2)}, u32[]{:S(2)}) collective-permute-start(f32[13,8,128]{2,1,0:T(8,128)S(1)} %get-tuple-element.58), channel_id=1, source_target_pairs={{0,192},{64,128},{128,64},{192,0},{1,193},{65,129},{129,65},{193,1... | collective-permute-start | bytes 159752 | tf_op jit(solution)/shard_map/ppermute | solution.py:799
  49.6 5.4 %collective-permute-start.11 = (f32[13,8,128]{2,1,0:T(8,128)S(1)}, f32[13,8,128]{2,1,0:T(8,128)S(1)}, u32[]{:S(2)}, u32[]{:S(2)}) collective-permute-start(f32[13,8,128]{2,1,0:T(8,128)S(1)} %get-tuple-element.59), channel_id=1, source_target_pairs={{0,56},{8,16},{16,8},{24,32},{32,24},{40,48},{48,40},{56,0},{1,57}... | collective-permute-start | bytes 159752 | tf_op jit(solution)/shard_map/ppermute | solution.py:799
  50.5 4.5 %collective-permute-start.12 = (f32[13,8,128]{2,1,0:T(8,128)S(1)}, f32[13,8,128]{2,1,0:T(8,128)S(1)}, u32[]{:S(2)}, u32[]{:S(2)}) collective-permute-start(f32[13,8,128]{2,1,0:T(8,128)S(1)} %get-tuple-element.60), channel_id=1, source_target_pairs={{0,64},{64,0},{128,192},{192,128},{1,65},{65,1},{129,193},{193,129... | collective-permute-start | bytes 159752 | tf_op jit(solution)/shard_map/ppermute | solution.py:794
  50.5 4.5 %collective-permute-start.13 = (f32[13,8,128]{2,1,0:T(8,128)S(1)}, f32[13,8,128]{2,1,0:T(8,128)S(1)}, u32[]{:S(2)}, u32[]{:S(2)}) collective-permute-start(f32[13,8,128]{2,1,0:T(8,128)S(1)} %get-tuple-element.61), channel_id=1, source_target_pairs={{0,8},{8,0},{16,24},{24,16},{32,40},{40,32},{48,56},{56,48},{1,9},... | collective-permute-start | bytes 159752 | tf_op jit(solution)/shard_map/ppermute | solution.py:794
